TPU v7x, 32 devices: a whole 2x2x4 slice. The times are simulated.
32 devices in a mesh: members: 2 (over y), lat: 4 (over z), lev: 2 (over x), sub: 2 (over core).
Axes of the slice: x: 2, y: 2, z: 4, core: 2. Of those that a mesh axis runs over, the one named last changes fastest.
Arguments:
- thermal_state_grid: bfloat16 [272, 512, 1024], P(('members', 'lev', 'sub'), 'lat'), parts along dimension 0, may hold values from -6 to 6
- thermal_forcing: bfloat16 [272, 512, 1024], P(('members', 'lev', 'sub'), 'lat'), parts along dimension 0, may hold values from -6 to 6
- spherical_basis_table: bfloat16 [512, 512, 512], P(('lat', 'lev', 'sub')), may hold values from -0.25 to 0.25
- implicit_solver_matrix: bfloat16 [512, 136, 136], P(('lat', 'lev', 'sub')), may hold values from -0.5 to 0.5
- fourier_order_holder: int32 [512], replicated, may hold values from 0 to 511, as said below
Outputs:
- new_temperature: bfloat16 [272, 512, 1024], P(('members', 'lev', 'sub'), 'lat'), parts along dimension 0
There are 2 independent parts, one for each index of `members`. A program takes and returns all parts, laid end to end along the dimension named above; an argument that names none is the same for every part. Nothing has to cross between parts.
Inputs may be any that keep to these rules, and one draw needn't show every extreme that they name: fourier_order_holder is a permutation of the waves; slots 2k and 2k+1 hold waves m and 511-m for some m.
All inputs are finite; a program needn't handle non-finite values.
Results may differ from a plain program's by a relative error of at most 0.0079.
Values may be sent and summed in bfloat16 or wider, within the bound.
No kernel may reach another device: no remote copies, remote signals or barrier semaphores. Data moves between devices by JAX's collectives and lax.ppermute only.
A program may use at most 192 MiB of HBM per device.

v0:
```python
import math

import jax
import jax.numpy as jnp
from jax import lax
from jax.sharding import PartitionSpec as P


def raw_table(fourier_order_holder, lon_count):
    meridian_position = jnp.arange(lon_count, dtype=jnp.int32)
    phases = meridian_position[:, None] * fourier_order_holder[None, :] % lon_count
    angles = phases.astype(jnp.float32) * (2.0 * math.pi / lon_count)
    factor = 1.0 / math.sqrt(lon_count)
    stacked = jnp.stack([jnp.cos(angles), -jnp.sin(angles)], axis=2)
    return stacked.reshape(lon_count, 2 * fourier_order_holder.shape[0]) * factor


def shards(
    thermal_state_grid,
    thermal_forcing,
    spherical_basis_table,
    implicit_solver_matrix,
    fourier_order_holder,
):
    layer_group_span, parallel_group_span, meridian_position = thermal_state_grid.shape
    slot_count, lat_total, wave_total = spherical_basis_table.shape
    present_state = thermal_state_grid.astype(jnp.float32)
    explicit = (
        present_state
        + 0.5 * thermal_forcing.astype(jnp.float32)
        - 0.3
        * present_state
        * present_state
        * present_state
        / (1.0 + present_state * present_state)
    ).astype(jnp.bfloat16)
    raw = raw_table(fourier_order_holder, meridian_position)
    analysis = raw.astype(jnp.bfloat16)
    weights = jnp.where(fourier_order_holder == 0, 1.0, 2.0).astype(jnp.float32)
    synthesis = (raw.T * jnp.repeat(weights, 2)[:, None]).astype(jnp.bfloat16)
    spectral = jnp.dot(
        explicit.reshape(layer_group_span * parallel_group_span, meridian_position),
        analysis,
        preferred_element_type=jnp.float32,
    )
    spectral = spectral.astype(jnp.bfloat16).reshape(
        layer_group_span, parallel_group_span, meridian_position
    )
    banded = lax.all_to_all(spectral, "lat", split_axis=2, concat_axis=1, tiled=True)
    gathered = lax.all_gather(spherical_basis_table, ("lev", "sub"), axis=0, tiled=True)
    owner_slots = gathered.shape[0]
    by_slot = banded.reshape(layer_group_span, lat_total, owner_slots, 2)
    part_spec = jnp.einsum(
        "lxsc,sxn->lscn", by_slot, gathered, preferred_element_type=jnp.float32
    ).astype(jnp.bfloat16)
    column = lax.all_to_all(part_spec, ("lev", "sub"), split_axis=1, concat_axis=0, tiled=True)
    solved = jnp.einsum(
        "skl,lscn->kscn", implicit_solver_matrix, column, preferred_element_type=jnp.float32
    )
    owner_index = lax.axis_index(("lat", "lev", "sub"))
    my_waves = lax.dynamic_slice_in_dim(fourier_order_holder, owner_index * slot_count, slot_count)
    degrees = jnp.arange(wave_total, dtype=jnp.int32)
    live_mask = degrees[None, :] >= my_waves[:, None]
    solved = jnp.where(live_mask[None, :, None, :], solved, 0.0).astype(jnp.bfloat16)
    returned = lax.all_to_all(solved, ("lev", "sub"), split_axis=0, concat_axis=1, tiled=True)
    synthesized = jnp.einsum(
        "sxn,lscn->lxsc", gathered, returned, preferred_element_type=jnp.float32
    ).astype(jnp.bfloat16)
    synthesized = synthesized.reshape(layer_group_span, lat_total, 2 * owner_slots)
    grid_spec = lax.all_to_all(synthesized, "lat", split_axis=1, concat_axis=2, tiled=True)
    result = jnp.dot(
        grid_spec.reshape(layer_group_span * parallel_group_span, meridian_position),
        synthesis,
        preferred_element_type=jnp.float32,
    )
    return result.astype(jnp.bfloat16).reshape(
        layer_group_span, parallel_group_span, meridian_position
    )


def solution(mesh):
    return jax.shard_map(
        shards,
        mesh=mesh,
        in_specs=(
            P(("members", "lev", "sub"), "lat", None),
            P(("members", "lev", "sub"), "lat", None),
            P(("lat", "lev", "sub"), None, None),
            P(("lat", "lev", "sub"), None, None),
            P(),
        ),
        out_specs=P(("members", "lev", "sub"), "lat", None),
        check_vma=False,
    )
```

profile of v0, /device:TPU:11, one launch (start us, length us, event | category | flops | bytes accessed | tf_op | source)
XLA Modules:
  0.0 1049.9 jit_solution(9948861162757677807)
XLA Ops:
  6.5 0.0 copy-start
  6.5 0.0 copy-start.3
  6.5 0.0 all-gather.2.cloned.1.call-start
  6.5 0.7 all-gather.2.cloned.1.call-update
  7.3 0.1 copy-done.3
  7.4 8.2 fusion.25
  15.6 4.7 maximum_multiply_fusion
  20.3 7.3 copy.51
  27.6 4.5 convert_element_type.68
  32.0 0.0 copy-start.2
  32.0 13.6 %fusion.5 = bf16[34,128,1024]{2,1,0:T(8,128)(2,1)S(1)} fusion(bf16[34,128,1024]{2,1,0:T(8,128)(2,1)} %param.5, bf16[34,128,1024]{2,1,0:T(8,128)(2,1)} %param.6), kind=kLoop, calls=%fused_computation.10 | loop fusion | flops 53477376 | bytes 26738688 | tf_op jit(solution)/shard_map/convert_element_type | solution.py:36
  45.7 0.0 copy-done.2
  45.7 11.6 %convolution_convert_fusion.1 = bf16[4352,1024]{1,0:T(8,128)(2,1)} fusion(bf16[4352,1024]{1,0:T(8,128)(2,1)S(1)} %bitcast.63, bf16[1024,1024]{0,1:T(8,128)(2,1)S(1)} %copy-done.2), kind=kOutput, calls=%fused_computation.16 | convolution fusion | flops 9131261952 | bytes 19922944 | tf_op jit(solution)/shard_map/dot_general | solution.py:41
  57.3 15.1 %copy.52 = bf16[34,128,1024]{1,0,2:T(8,128)(2,1)} copy(bf16[34,128,1024]{2,1,0:T(8,128)(2,1)} %bitcast.61) | data formatting | bytes 17825792 | tf_op jit(solution)/shard_map/reshape | solution.py:46
  72.4 230.3 %all_to_all.66 = bf16[34,128,1024]{1,0,2:T(8,128)(2,1)S(1)} all-to-all(bf16[34,128,1024]{1,0,2:T(8,128)(2,1)} %copy.52), channel_id=1, replica_groups=mesh['members'=2,'lat'=4,'lev'=2,'sub'=2] {'lat'}, dimensions={2} | all-to-all | bytes 17825792 | tf_op jit(solution)/shard_map/all_to_all | solution.py:49
  302.7 8.5 copy.70
  311.2 16.5 %reshape.153 = bf16[34,512,128,2]{1,0,3,2:T(8,128)(2,1)} reshape(bf16[34,4,128,256]{2,1,0,3:T(4,128)(2,1)} %copy.70) | data formatting | bytes 17825792 | tf_op jit(solution)/shard_map/reshape | solution.py:52
  327.6 74.7 %all-gather.2.cloned.1.call-done = bf16[128,512,512]{2,1,0:T(8,128)(2,1)} async-done(((bf16[32,512,512]{2,1,0:T(8,128)(2,1)}), bf16[128,512,512]{2,1,0:T(8,128)(2,1)}) %all-gather.2.cloned.1.call-update) | async-done | bytes 67108880 | tf_op jit(solution)/shard_map/all_gather | solution.py:50
  402.3 30.4 %convert_bitcast_fusion = bf16[34,128,2,512]{3,0,2,1:T(8,128)(2,1)} fusion(bf16[34,512,128,2]{1,0,3,2:T(8,128)(2,1)} %reshape.153, bf16[128,512,512]{2,1,0:T(8,128)(2,1)} %all-gather.2.cloned.1.call-done), kind=kOutput, calls=%fused_computation.14 | convolution fusion | flops 4567859200 | bytes 84934656 | tf_op jit(solution)/shard_map/lxsc,sxn->lscn/dot_general | solution.py:53
  432.8 13.8 %copy.56 = bf16[34,128,2,512]{3,2,0,1:T(2,128)(2,1)} copy(bf16[34,128,2,512]{3,0,2,1:T(8,128)(2,1)} %convert_bitcast_fusion) | data formatting | bytes 17825792 | tf_op jit(solution)/shard_map/convert_element_type | solution.py:55
  446.5 7.2 all-to-all-start.1
  453.8 0.1 dynamic_slice.3
  453.9 0.1 iota_compare_fusion
  454.0 96.7 %all-to-all-done.1 = bf16[34,128,2,512]{3,2,0,1:T(2,128)(2,1)} async-done(((bf16[34,128,2,512]{3,2,0,1:T(2,128)(2,1)}), bf16[34,128,2,512]{3,2,0,1:T(2,128)(2,1)}, u32[]{:S(2)}, u32[]{:S(2)}) %all-to-all-start.1) | async-done | bytes 8912928 | tf_op jit(solution)/shard_map/all_to_all | solution.py:56
  550.7 9.5 copy.57
  560.1 8.8 copy.58
  568.9 0.0 copy-done
  568.9 16.3 %fusion.14 = bf16[136,32,2,512]{3,0,2,1:T(8,128)(2,1)S(1)} fusion(bf16[136,32,2,512]{3,1,2,0:T(8,128)(2,1)} %bitcast.62, pred[32,512]{1,0:T(8,128)(4,1)S(1)} %iota_compare_fusion, bf16[32,136,136]{2,1,0:T(8,128)(2,1)S(1)} %copy-done), kind=kOutput, calls=%fused_computation.19 | convolution fusion | flops 1221066752 | bytes 19025920 | tf_op jit(solution)/shard_map/skl,lscn->kscn/dot_general | solution.py:57
  585.2 11.6 %copy.60 = bf16[136,32,2,512]{3,2,1,0:T(2,128)(2,1)S(1)} copy(bf16[136,32,2,512]{3,0,2,1:T(8,128)(2,1)S(1)} %fusion.14) | data formatting | bytes 17825792 | tf_op jit(solution)/shard_map/convert_element_type | solution.py:64
  596.8 102.8 %all_to_all.67 = bf16[136,32,2,512]{3,2,1,0:T(2,128)(2,1)} all-to-all(bf16[136,32,2,512]{3,2,1,0:T(2,128)(2,1)S(1)} %copy.60), channel_id=1, replica_groups=mesh['members'=2,'lat'=4,'lev'=2,'sub'=2] {'lev','sub'}, dimensions={0} | all-to-all | bytes 17825792 | tf_op jit(solution)/shard_map/all_to_all | solution.py:65
  699.5 9.8 copy.61
  709.3 12.8 %copy.62 = bf16[34,4,32,2,512]{4,0,3,2,1:T(8,128)(2,1)} copy(bf16[34,4,32,2,512]{4,2,3,0,1:T(8,128)(2,1)} %bitcast.58) | data formatting | bytes 17825792 | tf_op jit(solution)/shard_map/all_to_all | solution.py:65
  722.1 33.8 %fusion.11 = bf16[128,34,2,512]{3,1,2,0:T(8,128)(2,1)} fusion(bf16[34,128,2,512]{3,0,2,1:T(8,128)(2,1)} %bitcast.55, bf16[128,512,512]{2,1,0:T(8,128)(2,1)} %all-gather.2.cloned.1.call-done), kind=kOutput, calls=%fused_computation.18 | convolution fusion | flops 4567859200 | bytes 84934656 | tf_op jit(solution)/shard_map/sxn,lscn->lxsc/dot_general | solution.py:66
  755.9 17.4 %copy.63 = bf16[34,512,256]{2,0,1:T(8,128)(2,1)} copy(bf16[34,512,256]{1,0,2:T(8,128)(2,1)} %bitcast.56) | data formatting | bytes 17825792 | tf_op jit(solution)/shard_map/reshape | solution.py:69
  773.3 6.5 all-to-all-start.3
  779.8 7.3 copy.66
  787.1 6.1 mul.115
  793.2 0.1 broadcast_in_dim.32
  793.4 0.2 mul.116
  793.5 210.7 %all-to-all-done.3 = bf16[34,512,256]{2,0,1:T(8,128)(2,1)} async-done(((bf16[34,512,256]{2,0,1:T(8,128)(2,1)}), bf16[34,512,256]{2,0,1:T(8,128)(2,1)}, u32[]{:S(2)}, u32[]{:S(2)}) %all-to-all-start.3) | async-done | bytes 8912928 | tf_op jit(solution)/shard_map/all_to_all | solution.py:70
  1004.2 12.9 %copy.65 = bf16[34,128,4,256]{3,2,1,0:T(4,128)(2,1)} copy(bf16[34,128,4,256]{3,0,1,2:T(8,128)(2,1)} %bitcast.21) | data formatting | bytes 17825792 | tf_op jit(solution)/shard_map/all_to_all | solution.py:70
  1017.1 9.9 copy.73
  1027.0 0.0 copy-start.1
  1027.0 15.6 %convolution_convert_fusion = bf16[4352,1024]{1,0:T(8,128)(2,1)} fusion(bf16[4352,1024]{1,0:T(8,128)(2,1)} %bitcast.60, f32[1024,1024]{0,1:T(8,128)} %mul.115, f32[1024]{0:T(1024)S(1)} %mul.116), kind=kOutput, calls=%fused_computation.15 | convolution fusion | flops 9133359104 | bytes 22024192 | tf_op jit(solution)/shard_map/dot_general | solution.py:71
  1042.6 0.0 copy-done.1
  (1 shorter events, 0.0 us)
Async XLA Ops:
  6.5 562.4 %copy-start = (bf16[32,136,136]{2,1,0:T(8,128)(2,1)S(1)}, bf16[32,136,136]{2,1,0:T(8,128)(2,1)}, u32[]{:S(2)}) copy-start(bf16[32,136,136]{2,1,0:T(8,128)(2,1)} %param.8) | copy-start | bytes 3551236
  6.5 0.8 copy-start.3
  6.5 395.8 %all-gather.2.cloned.1.call-start = ((), (), s32[]{:S(2)}) async-start(), calls=%async_computation.4 | async-start | bytes 83886080 | tf_op jit(solution)/shard_map/all_gather | solution.py:50
  32.0 13.7 %copy-start.2 = (bf16[1024,1024]{0,1:T(8,128)(2,1)S(1)}, bf16[1024,1024]{0,1:T(8,128)(2,1)}, u32[]{:S(2)}) copy-start(bf16[1024,1024]{0,1:T(8,128)(2,1)} %convert_element_type.68) | copy-start | bytes 6291460
  446.5 104.1 %all-to-all-start.1 = ((bf16[34,128,2,512]{3,2,0,1:T(2,128)(2,1)}), bf16[34,128,2,512]{3,2,0,1:T(2,128)(2,1)}, u32[]{:S(2)}, u32[]{:S(2)}) async-start(bf16[34,128,2,512]{3,2,0,1:T(2,128)(2,1)} %copy.56), calls=%async_computation.1 | async-start | bytes 17825792 | tf_op jit(solution)/shard_map/all_to_all | solution.py:56
  773.3 230.9 %all-to-all-start.3 = ((bf16[34,512,256]{2,0,1:T(8,128)(2,1)}), bf16[34,512,256]{2,0,1:T(8,128)(2,1)}, u32[]{:S(2)}, u32[]{:S(2)}) async-start(bf16[34,512,256]{2,0,1:T(8,128)(2,1)} %copy.63), calls=%async_computation.3 | async-start | bytes 20971520 | tf_op jit(solution)/shard_map/all_to_all | solution.py:70
  1027.0 15.6 %copy-start.1 = (bf16[32,136,136]{2,1,0:T(8,128)(2,1)S(1)}, bf16[32,136,136]{2,1,0:T(8,128)(2,1)}, u32[]{:S(2)}) copy-start(bf16[32,136,136]{2,1,0:T(8,128)(2,1)} %param.8) | copy-start | bytes 3551236
Sparse Core Ops, SparseCore 0:
  8.9 393.3 all-gather.1
where the time goes:
time: 1060 us; the launch traced here: 1050 us
  waiting for transfers between devices  383 us (36%)
  blocking collectives  333 us (31%)
  local copies, waits for them, and re-layouts  172 us (16%)
  matrix products  108 us (10%)
  other arithmetic  26.7 us (3%)
  between operations  13.9 us (1%)
  starting transfers between devices  13.7 us (1%)
    all_to_all x1, blocking collectives, shards(): lax.all_to_all(spectral, 'lat', split_axis=2, concat_axis=1, tiled=True)  230 us
    all_to_all x1, waiting for transfers between devices, shards(): lax.all_to_all(synthesized, 'lat', split_axis=1, concat_axis=2, tiled=True)  211 us
    all_to_all x1, blocking collectives, shards(): lax.all_to_all(solved, ('lev', 'sub'), split_axis=0, concat_axis=1, tiled...  103 us
    all_to_all x1, waiting for transfers between devices, shards(): lax.all_to_all(part_spec, ('lev', 'sub'), split_axis=1, concat_axis=0, ti...  96.7 us
    all_gather x1, waiting for transfers between devices, shards(): lax.all_gather(spherical_basis_table, ('lev', 'sub'), axis=0, tiled=True)  74.7 us
    dot_general x1, matrix products, shards(): jnp.einsum('sxn,lscn->lxsc', gathered, returned, preferred_element_type=j...  33.8 us
    dot_general x1, matrix products, shards(): jnp.einsum('lxsc,sxn->lscn', by_slot, gathered, preferred_element_type=jn...  30.4 us
    reshape x2, local copies, waits for them, and re-layouts, shards(): by_slot = banded.reshape(layer_group_span, lat_total, owner_slots, 2)  24.9 us
  transfers between devices with their start and end apart: 3, of which 3 were waited for; matrix products, arithmetic and copies ran while one was open for 10% of the time, Pallas kernels for 0%

commit v1 on v0

v1 whole, which is shorter than its diff:
```python
import math

import jax
import jax.numpy as jnp
from jax import lax
from jax.sharding import PartitionSpec as P

OWNERS = ("lat", "lev", "sub")


def raw_table(fourier_order_holder, lon_count):
    meridian_position = jnp.arange(lon_count, dtype=jnp.int32)
    phases = fourier_order_holder[:, None] * meridian_position[None, :] % lon_count
    angles = phases.astype(jnp.float32) * (2.0 * math.pi / lon_count)
    factor = 1.0 / math.sqrt(lon_count)
    stacked = jnp.stack([jnp.cos(angles), -jnp.sin(angles)], axis=1)
    return stacked.reshape(2 * fourier_order_holder.shape[0], lon_count) * factor


def general_shards(lat_bands, level_groups):
    def shards(
        thermal_state_grid,
        thermal_forcing,
        spherical_basis_table,
        implicit_solver_matrix,
        fourier_order_holder,
    ):
        levels, lats, lon_count = thermal_state_grid.shape
        slots, lat_total, wave_total = spherical_basis_table.shape
        owners = lat_bands * level_groups
        state = thermal_state_grid.astype(jnp.float32)
        explicit = (
            state
            + 0.5 * thermal_forcing.astype(jnp.float32)
            - 0.3 * state * state * state / (1.0 + state * state)
        ).astype(jnp.bfloat16)
        raw = raw_table(fourier_order_holder, lon_count)
        analysis = raw.astype(jnp.bfloat16)
        weights = jnp.where(fourier_order_holder == 0, 1.0, 2.0).astype(jnp.float32)
        synthesis = (raw * jnp.repeat(weights, 2)[:, None]).astype(jnp.bfloat16)
        spectral = jnp.einsum(
            "sj,lxj->slx", analysis, explicit, preferred_element_type=jnp.float32
        ).astype(jnp.bfloat16)
        spectral = spectral.reshape(owners, 2 * slots * levels, lats)
        spectral = lax.all_to_all(spectral, OWNERS, 0, 0, tiled=True)
        spectral = spectral.reshape(lat_bands, level_groups, slots, 2, levels, lats)
        spectral = spectral.transpose(2, 3, 1, 4, 0, 5)
        spectral = spectral.reshape(slots, 2 * level_groups * levels, lat_total)
        coeffs = jnp.einsum(
            "srx,sxn->srn", spectral, spherical_basis_table, preferred_element_type=jnp.float32
        ).astype(jnp.bfloat16)
        coeffs = coeffs.reshape(slots, 2, level_groups * levels, wave_total)
        solved = jnp.einsum(
            "skl,scln->sckn", implicit_solver_matrix, coeffs, preferred_element_type=jnp.float32
        )
        owner = lax.axis_index(OWNERS)
        waves = lax.dynamic_slice_in_dim(fourier_order_holder, owner * slots, slots)
        live = jnp.arange(wave_total, dtype=jnp.int32)[None, :] >= waves[:, None]
        solved = jnp.where(live[:, None, None, :], solved, 0.0).astype(jnp.bfloat16)
        solved = solved.reshape(slots, 2 * level_groups * levels, wave_total)
        back = jnp.einsum(
            "srn,sxn->srx", solved, spherical_basis_table, preferred_element_type=jnp.float32
        ).astype(jnp.bfloat16)
        back = back.reshape(slots, 2, level_groups, levels, lat_bands, lats)
        back = back.transpose(4, 2, 0, 1, 3, 5).reshape(owners, 2 * slots * levels, lats)
        back = lax.all_to_all(back, OWNERS, 0, 0, tiled=True)
        back = back.reshape(2 * slots * owners, levels, lats)
        return jnp.einsum(
            "slx,sj->lxj", back, synthesis, preferred_element_type=jnp.float32
        ).astype(jnp.bfloat16)

    return shards


def solution(mesh):
    shape = mesh.shape
    shards = general_shards(shape["lat"], shape["lev"] * shape["sub"])
    return jax.shard_map(
        shards,
        mesh=mesh,
        in_specs=(
            P(("members", "lev", "sub"), "lat", None),
            P(("members", "lev", "sub"), "lat", None),
            P(OWNERS, None, None),
            P(OWNERS, None, None),
            P(),
        ),
        out_specs=P(("members", "lev", "sub"), "lat", None),
        check_vma=False,
    )
```

time: 1060 us -> 610 us (0.58)
  blocking collectives: 333 us -> 0 us
  local copies, waits for them, and re-layouts: 172 us -> 130 us
  matrix products: 108 us -> 66.9 us
  other arithmetic: 26.7 us -> 11.7 us
  between operations: 13.9 us -> 0.49 us
    all_to_all x2 -> x0, blocking collectives: 333 us -> none  [the longest x1 230 us: shards(): lax.all_to_all(spectral, 'lat', split_axis=2, concat_axis=1, tiled=True)]
    all_gather x1 -> x0, waiting for transfers between devices: 74.7 us -> none  [shards(): lax.all_gather(spherical_basis_table, ('lev', 'sub'), axis=0, tiled=True)]
    all_to_all x2, waiting for transfers between devices: 307 us -> 379 us  [the longest x1 193 us: shards(): spectral = lax.all_to_all(spectral, OWNERS, 0, 0, tiled=True)]
    dot_general x5, matrix products: 108 us -> 66.9 us  [the longest x1 16.3 us: shards(): jnp.einsum('slx,sj->lxj', back, synthesis, preferred_element_type=jnp.flo...]
    all_to_all x5 -> x1, local copies, waits for them, and re-layouts: 53.7 us -> 18.3 us  [shards(): spectral = lax.all_to_all(spectral, OWNERS, 0, 0, tiled=True)]
    reshape x4 -> x6, local copies, waits for them, and re-layouts: 57.4 us -> 76.6 us  [the longest x2 24.1 us: shards(): back = back.reshape(slots, 2, level_groups, levels, lat_bands, lats)]
    mul x3 -> x0, local copies, waits for them, and re-layouts: 13.6 us -> none  [the longest x2 13.4 us: raw_table(): stacked.reshape(lon_count, 2 * fourier_order_holder.shape[0]) * factor]
    convert_element_type x1, other arithmetic: 13.6 us -> 1.78 us  [shards(): analysis = raw.astype(jnp.bfloat16)]
  transfers between devices with their start and end apart: 3 -> 2, of which waited for: 3 -> 2; matrix products, arithmetic and copies ran while one was open for 10% -> 1% of each run, Pallas kernels for 0% -> 0%
where the time goes in v1:
time: 610 us; the launch traced here: 600 us
  waiting for transfers between devices  379 us (62%)
  local copies, waits for them, and re-layouts  130 us (21%)
  matrix products  66.9 us (11%)
  starting transfers between devices  11.9 us (2%)
  other arithmetic  11.7 us (2%)
    all_to_all x1, waiting for transfers between devices, shards(): spectral = lax.all_to_all(spectral, OWNERS, 0, 0, tiled=True)  193 us
    all_to_all x1, waiting for transfers between devices, shards(): back = lax.all_to_all(back, OWNERS, 0, 0, tiled=True)  186 us
    reshape x2, local copies, waits for them, and re-layouts, shards(): back = back.reshape(slots, 2, level_groups, levels, lat_bands, lats)  24.1 us
    all_to_all x1, local copies, waits for them, and re-layouts, shards(): spectral = lax.all_to_all(spectral, OWNERS, 0, 0, tiled=True)  18.3 us
    dot_general x1, matrix products, shards(): jnp.einsum('slx,sj->lxj', back, synthesis, preferred_element_type=jnp.flo...  16.3 us
    dot_general x1, matrix products, shards(): jnp.einsum('sj,lxj->slx', analysis, explicit, preferred_element_type=jnp....  15.9 us
    reshape x1, local copies, waits for them, and re-layouts, shards(): spectral = spectral.reshape(owners, 2 * slots * levels, lats)  14.7 us
    reshape x1, local copies, waits for them, and re-layouts, shards(): back = back.reshape(2 * slots * owners, levels, lats)  14.5 us
  transfers between devices with their start and end apart: 2, of which 2 were waited for; matrix products, arithmetic and copies ran while one was open for 1% of the time, Pallas kernels for 0%

profile of v1, /device:TPU:11, one launch (start us, length us, event | category | flops | bytes accessed | tf_op | source)
XLA Modules:
  0.0 599.5 jit_solution(8641190963347921252)
XLA Ops:
  0.0 0.0 copy-start
  0.0 9.2 %fusion.21 = (f32[512,1,1024]{2,0,1:T(8,128)S(1)}, f32[512,1,1024]{2,0,1:T(8,128)S(1)}) fusion(s32[512]{0:T(512)} %param.9), kind=kLoop, calls=%fused_computation.31 | loop fusion | flops 7864320 | bytes 4196352 | tf_op jit(solution)/shard_map/cos | solution.py:16
  9.2 0.7 select_multiply_fusion
  9.9 1.8 multiply_convert_fusion.1
  11.6 3.5 copy.24
  15.1 4.3 reshape.177
  19.4 15.9 %fusion.8 = bf16[1024,34,128]{2,0,1:T(8,128)(2,1)} fusion(bf16[1024,1024,1]{1,0,2:T(8,128)(2,1)} %reshape.177, bf16[34,128,1024]{2,1,0:T(8,128)(2,1)} %param.5, bf16[34,128,1024]{2,1,0:T(8,128)(2,1)} %param.6), kind=kOutput, calls=%fused_computation.13 | convolution fusion | flops 9184739328 | bytes 28835840 | tf_op jit(solution)/shard_map/sj,lxj->slx/dot_general | solution.py:41
  35.3 13.4 %copy.25 = bf16[1024,34,128]{2,1,0:T(8,128)(2,1)} copy(bf16[1024,34,128]{2,0,1:T(8,128)(2,1)} %fusion.8) | data formatting | bytes 17825792 | tf_op jit(solution)/shard_map/convert_element_type | solution.py:43
  48.7 14.7 %reshape.169 = bf16[16,2176,128]{2,1,0:T(8,128)(2,1)} reshape(bf16[1024,34,128]{2,1,0:T(8,128)(2,1)} %copy.25) | data formatting | bytes 17825792 | tf_op jit(solution)/shard_map/reshape | solution.py:44
  63.3 6.9 %all-to-all-start = ((bf16[16,2176,128]{2,1,0:T(8,128)(2,1)}), bf16[16,2176,128]{2,1,0:T(8,128)(2,1)}, u32[]{:S(2)}, u32[]{:S(2)}) async-start(bf16[16,2176,128]{2,1,0:T(8,128)(2,1)} %reshape.169), calls=%async_computation | async-start | bytes 17825792 | tf_op jit(solution)/shard_map/all_to_all | solution.py:45
  70.3 0.8 dynamic_slice.3
  71.0 0.1 iota_compare_fusion
  71.1 192.6 %all-to-all-done = bf16[16,2176,128]{2,1,0:T(8,128)(2,1)} async-done(((bf16[16,2176,128]{2,1,0:T(8,128)(2,1)}), bf16[16,2176,128]{2,1,0:T(8,128)(2,1)}, u32[]{:S(2)}, u32[]{:S(2)}) %all-to-all-start) | async-done | bytes 8912928 | tf_op jit(solution)/shard_map/all_to_all | solution.py:45
  263.7 18.3 %copy.26 = bf16[16,2176,128]{2,0,1:T(8,128)(2,1)S(1)} copy(bf16[16,2176,128]{2,1,0:T(8,128)(2,1)} %all-to-all-done) | data formatting | bytes 17825792 | tf_op jit(solution)/shard_map/all_to_all | solution.py:45
  282.0 5.5 copy.27
  287.6 14.0 %reshape.171 = bf16[32,272,512]{2,1,0:T(8,128)(2,1)} reshape(bf16[32,2,4,34,4,128]{5,4,3,2,1,0:T(4,128)(2,1)} %copy.27) | data formatting | bytes 17825792 | tf_op jit(solution)/shard_map/reshape | solution.py:48
  301.5 14.4 %convolution_convert_fusion.1 = bf16[32,272,512]{2,1,0:T(8,128)(2,1)} fusion(bf16[32,272,512]{2,1,0:T(8,128)(2,1)} %reshape.171, bf16[32,512,512]{2,1,0:T(8,128)(2,1)} %param.7), kind=kOutput, calls=%fused_computation.16 | convolution fusion | flops 4567859200 | bytes 34603008 | tf_op jit(solution)/shard_map/srx,sxn->srn/dot_general | solution.py:49
  315.9 0.0 copy-done
  315.9 7.0 %select_convert_fusion = bf16[32,2,512,136]{2,3,1,0:T(8,128)(2,1)} fusion(bf16[32,2,136,512]{3,2,1,0:T(8,128)(2,1)} %bitcast.25, pred[32,512]{1,0:T(8,128)(4,1)S(1)} %iota_compare_fusion, bf16[32,136,136]{2,1,0:T(8,128)(2,1)S(1)} %copy-done), kind=kOutput, calls=%fused_computation.9 | convolution fusion | flops 1221066752 | bytes 19025920 | tf_op jit(solution)/shard_map/skl,scln->sckn/dot_general | solution.py:53
  322.9 13.3 %convolution_convert_fusion = bf16[32,272,512]{2,1,0:T(8,128)(2,1)} fusion(bf16[32,272,512]{2,1,0:T(8,128)(2,1)} %bitcast.24, bf16[32,512,512]{2,1,0:T(8,128)(2,1)} %param.7), kind=kOutput, calls=%fused_computation.15 | convolution fusion | flops 4567859200 | bytes 34603008 | tf_op jit(solution)/shard_map/srn,sxn->srx/dot_general | solution.py:61
  336.2 13.3 %reshape.174 = bf16[32,2,4,34,4,128]{5,4,3,2,1,0:T(4,128)(2,1)} reshape(bf16[32,272,512]{2,1,0:T(8,128)(2,1)} %convolution_convert_fusion) | data formatting | bytes 17825792 | tf_op jit(solution)/shard_map/reshape | solution.py:64
  349.6 10.8 %copy.28 = bf16[32,2,4,34,4,128]{5,2,4,3,1,0:T(4,128)(2,1)} copy(bf16[32,2,4,34,4,128]{5,4,3,2,1,0:T(4,128)(2,1)} %reshape.174) | data formatting | bytes 17825792 | tf_op jit(solution)/shard_map/reshape | solution.py:64
  360.4 9.3 %copy.29 = bf16[16,2176,128]{2,1,0:T(8,128)(2,1)} copy(bf16[16,2176,128]{2,0,1:T(8,128)(2,1)} %bitcast.23) | data formatting | bytes 17825792 | tf_op jit(solution)/shard_map/reshape | solution.py:65
  369.6 0.0 copy-start.2
  369.7 5.0 all-to-all-start.1
  374.7 0.0 copy-done.2
  374.7 3.5 copy.30
  378.2 4.1 reshape.179
  382.3 186.0 %all-to-all-done.1 = bf16[16,2176,128]{2,1,0:T(8,128)(2,1)} async-done(((bf16[16,2176,128]{2,1,0:T(8,128)(2,1)}), bf16[16,2176,128]{2,1,0:T(8,128)(2,1)}, u32[]{:S(2)}, u32[]{:S(2)}) %all-to-all-start.1) | async-done | bytes 8912928 | tf_op jit(solution)/shard_map/all_to_all | solution.py:66
  568.3 14.5 %reshape.176 = bf16[1024,34,128]{2,1,0:T(8,128)(2,1)} reshape(bf16[16,2176,128]{2,1,0:T(8,128)(2,1)} %all-to-all-done.1) | data formatting | bytes 17825792 | tf_op jit(solution)/shard_map/reshape | solution.py:67
  582.8 0.0 copy-start.1
  582.8 16.3 %fusion.11 = bf16[34,128,1024]{2,1,0:T(8,128)(2,1)} fusion(bf16[1024,1024,1]{1,0,2:T(8,128)(2,1)} %reshape.179, bf16[1024,34,128]{2,1,0:T(8,128)(2,1)} %reshape.176), kind=kOutput, calls=%fused_computation.14 | convolution fusion | flops 9131261952 | bytes 19922944 | tf_op jit(solution)/shard_map/slx,sj->lxj/dot_general | solution.py:68
  599.1 0.0 copy-done.1
Async XLA Ops:
  0.0 315.9 %copy-start = (bf16[32,136,136]{2,1,0:T(8,128)(2,1)S(1)}, bf16[32,136,136]{2,1,0:T(8,128)(2,1)}, u32[]{:S(2)}) copy-start(bf16[32,136,136]{2,1,0:T(8,128)(2,1)} %param.8) | copy-start | bytes 3551236
  63.3 200.4 %all-to-all-start = ((bf16[16,2176,128]{2,1,0:T(8,128)(2,1)}), bf16[16,2176,128]{2,1,0:T(8,128)(2,1)}, u32[]{:S(2)}, u32[]{:S(2)}) async-start(bf16[16,2176,128]{2,1,0:T(8,128)(2,1)} %reshape.169), calls=%async_computation | async-start | bytes 17825792 | tf_op jit(solution)/shard_map/all_to_all | solution.py:45
  369.6 5.0 copy-start.2
  369.7 198.6 %all-to-all-start.1 = ((bf16[16,2176,128]{2,1,0:T(8,128)(2,1)}), bf16[16,2176,128]{2,1,0:T(8,128)(2,1)}, u32[]{:S(2)}, u32[]{:S(2)}) async-start(bf16[16,2176,128]{2,1,0:T(8,128)(2,1)} %copy.29), calls=%async_computation.1 | async-start | bytes 17825792 | tf_op jit(solution)/shard_map/all_to_all | solution.py:66
  582.8 16.3 %copy-start.1 = (bf16[32,136,136]{2,1,0:T(8,128)(2,1)S(1)}, bf16[32,136,136]{2,1,0:T(8,128)(2,1)}, u32[]{:S(2)}) copy-start(bf16[32,136,136]{2,1,0:T(8,128)(2,1)} %param.8) | copy-start | bytes 3551236

commit v2 on v1

--- a/solution.py
+++ b/solution.py
@@ -1,11 +1,16 @@
+import functools
 import math
 
 import jax
 import jax.numpy as jnp
+import numpy as np
 from jax import lax
+from jax.experimental import pallas as pl
+from jax.experimental.pallas import tpu as pltpu
 from jax.sharding import PartitionSpec as P
 
 OWNERS = ("lat", "lev", "sub")
+CHUNKS = 2
 
 
 def raw_table(fourier_order_holder, lon_count):
@@ -72,9 +77,300 @@
     return shards
 
 
+TILE = 8
+VMEM_BYTES = 60 * 1024 * 1024
+NT = (((1,), (1,)), ((), ()))
+TN = (((0,), (0,)), ((), ()))
+
+
+def dot(a, b, dims=(((1,), (0,)), ((), ()))):
+    return lax.dot_general(a, b, dims, preferred_element_type=jnp.float32)
+
+
+def longitude_waves(lon_count):
+    half = lon_count // 2
+    waves = np.arange(half).reshape(half // 2, 2).T
+    phases = waves[:, :, None] * np.arange(half)[None, None, :] % lon_count
+    angles = phases.astype(np.float32) * np.float32(2.0 * math.pi / lon_count)
+    table = np.stack([np.cos(angles), -np.sin(angles)], axis=1) / math.sqrt(lon_count)
+    return table.astype(jnp.bfloat16)
+
+
+def analysis_kernel(
+    owners, chunks, holder_ref, waves_ref, state_ref, forcing_ref, *refs
+):
+    sends, synth_ref, table = refs[:chunks], refs[chunks], refs[chunks + 1]
+    pairs = holder_ref.shape[0]
+    per_chunk = pairs // owners // chunks
+    levels, lats, lon_count = state_ref.shape
+    half = lon_count // 2
+
+    @pl.when(pl.program_id(0) == 0)
+    def _():
+        first, second = holder_ref[:, 0:1], holder_ref[:, 1:2]
+        column = lax.broadcasted_iota(jnp.int32, (pairs, waves_ref.shape[2]), 1)
+        for parity in range(2):
+            wave = 2 * column + parity
+            pick = ((first == wave) | (second == wave)).astype(jnp.float32).astype(jnp.bfloat16)
+            weight = 2.0
+            if parity == 0:
+                weight = jnp.where((first == 0) | (second == 0), 1.0, 2.0)
+            parts, heavy = [], []
+            for c in range(2):
+                rows = dot(pick, waves_ref[parity, c])
+                parts.append(rows.reshape(owners, chunks, per_chunk, half))
+                heavy.append((rows * weight).reshape(owners, chunks, per_chunk, half))
+            for k in range(chunks):
+                rows = jnp.concatenate([part[:, k] for part in parts], axis=1)
+                table[parity, k] = rows.reshape(2 * per_chunk * owners, half).astype(jnp.bfloat16)
+                rows = jnp.concatenate([part[:, k] for part in heavy], axis=1)
+                synth_ref[parity, k] = rows.reshape(2 * per_chunk * owners, half).astype(
+                    jnp.bfloat16
+                )
+
+    state = state_ref[...].reshape(levels * lats, lon_count).astype(jnp.float32)
+    forcing = forcing_ref[...].reshape(levels * lats, lon_count).astype(jnp.float32)
+    explicit = 0.7 * state + 0.5 * forcing + 0.3 * state / (1.0 + state * state)
+    low, high = explicit[:, :half], explicit[:, half:]
+    for parity in range(2):
+        folded = (low + high if parity == 0 else low - high).astype(jnp.bfloat16)
+        for k in range(chunks):
+            found = dot(table[parity, k], folded, NT).astype(jnp.bfloat16)
+            found = found.reshape(owners, 2 * per_chunk, levels * lats)
+            rows = slice(parity * 2 * per_chunk, (parity + 1) * 2 * per_chunk)
+            for level in range(levels):
+                sends[k][:, level, rows, :] = found[:, :, level * lats : (level + 1) * lats]
+
+
+def run_analysis(owners, chunks, state, forcing, holder):
+    levels, lats, lon_count = state.shape
+    pairs = holder.shape[0] // 2
+    rows = 4 * pairs // owners // chunks
+    table = jnp.asarray(longitude_waves(lon_count))
+    step = 2 if levels % 2 == 0 else 1
+    block = pl.BlockSpec((step, lats, lon_count), lambda i: (i, 0, 0))
+    whole = lambda shape: pl.BlockSpec(shape, lambda i: (0,) * len(shape))
+    synth = (2, chunks, 2 * pairs // chunks, lon_count // 2)
+    outs = pl.pallas_call(
+        functools.partial(analysis_kernel, owners, chunks),
+        grid=(levels // step,),
+        in_specs=[whole((pairs, 2)), whole(table.shape), block, block],
+        out_specs=[pl.BlockSpec((owners, step, rows, lats), lambda i: (0, i, 0, 0))] * chunks
+        + [whole(synth)],
+        out_shape=[jax.ShapeDtypeStruct((owners, levels, rows, lats), jnp.bfloat16)] * chunks
+        + [jax.ShapeDtypeStruct(synth, jnp.bfloat16)],
+        scratch_shapes=[pltpu.VMEM(synth, jnp.bfloat16)],
+        compiler_params=pltpu.CompilerParams(vmem_limit_bytes=VMEM_BYTES),
+        cost_estimate=pl.CostEstimate(
+            flops=2 * levels * lats * lon_count * pairs * 2,
+            bytes_accessed=6 * levels * lats * lon_count,
+            transcendentals=0,
+        ),
+        name="longitude_analysis",
+    )(holder.reshape(pairs, 2), table, state, forcing)
+    return outs[:chunks], outs[chunks]
+
+
+def slot_of(k, per_chunk, i, waves):
+    first = 2 * (k * per_chunk + lax.rem(i, per_chunk))
+    odd = lax.rem(waves[first], 2)
+    return first + lax.rem(odd + i // per_chunk, 2)
+
+
+def column_kernel(
+    k, per_chunk, waves_ref, recv_ref, basis_ref, solver_ref, send_ref, spread, back
+):
+    owners, levels, rows, lats = recv_ref.shape
+    bands = spread.shape[0]
+    groups = owners // bands
+    depth = groups * levels
+    total = basis_ref.shape[1]
+    i = pl.program_id(0)
+
+    @pl.when(i == 0)
+    def _():
+        for a in range(bands):
+            for g in range(groups):
+                part = recv_ref[a * groups + g].astype(jnp.float32)
+                spread[a, g * levels * rows : (g + 1) * levels * rows, :] = part.reshape(
+                    levels * rows, lats
+                )
+
+    wave = waves_ref[slot_of(k, per_chunk, i, waves_ref)]
+    base = (i // per_chunk) * (2 * per_chunk) + lax.rem(i, per_chunk)
+    starts = [base, base + per_chunk]
+
+    def column(low):
+        count = total - low
+        taken = [
+            jnp.concatenate(
+                [spread[a, pl.ds(start, depth, stride=rows), :] for a in range(bands)], axis=1
+            )
+            for start in starts
+        ]
+        taken = jnp.concatenate(taken, axis=0).astype(jnp.bfloat16)
+        basis = basis_ref[0, :, low:]
+        coeffs = dot(taken, basis)
+        coeffs = jnp.concatenate([coeffs[:depth], coeffs[depth:]], axis=1).astype(jnp.bfloat16)
+        solved = dot(solver_ref[0], coeffs)
+        degree = low + lax.broadcasted_iota(jnp.int32, (depth, count), 1)
+        parts = [
+            jnp.where(degree >= wave, solved[:, c * count : (c + 1) * count], 0.0)
+            for c in range(2)
+        ]
+        solved = jnp.concatenate(parts, axis=0).astype(jnp.bfloat16)
+        grid = dot(solved, basis, NT)
+        for c in range(2):
+            for a in range(bands):
+                back[a, pl.ds(starts[c], depth, stride=rows), :] = grid[
+                    c * depth : (c + 1) * depth, a * lats : (a + 1) * lats
+                ]
+
+    middle = total // 2
+
+    @pl.when(wave < middle)
+    def _():
+        column(0)
+
+    @pl.when(wave >= middle)
+    def _():
+        column(middle)
+
+    @pl.when(i == pl.num_programs(0) - 1)
+    def _():
+        for a in range(bands):
+            for g in range(groups):
+                part = back[a, g * levels * rows : (g + 1) * levels * rows, :]
+                send_ref[a * groups + g] = part.reshape(levels, rows, lats).astype(jnp.bfloat16)
+
+
+def run_columns(k, per_chunk, bands, waves, received, basis, solver):
+    owners, levels, rows, lats = received.shape
+    depth = owners // bands * levels
+    total = basis.shape[1]
+    steps = 2 * per_chunk
+    slot = lambda i, waves_ref: (slot_of(k, per_chunk, i, waves_ref), 0, 0)
+    whole = pl.BlockSpec(received.shape, lambda i, waves_ref: (0, 0, 0, 0))
+    scratch = pltpu.VMEM((bands, depth * rows, lats), jnp.float32)
+    return pl.pallas_call(
+        functools.partial(column_kernel, k, per_chunk),
+        grid_spec=pltpu.PrefetchScalarGridSpec(
+            num_scalar_prefetch=1,
+            grid=(steps,),
+            in_specs=[
+                whole,
+                pl.BlockSpec((1, total, total), slot),
+                pl.BlockSpec((1, depth, depth), slot),
+            ],
+            out_specs=whole,
+            scratch_shapes=[scratch, scratch],
+        ),
+        out_shape=jax.ShapeDtypeStruct(received.shape, jnp.bfloat16),
+        compiler_params=pltpu.CompilerParams(vmem_limit_bytes=VMEM_BYTES),
+        cost_estimate=pl.CostEstimate(
+            flops=4 * steps * 2 * depth * total * total,
+            bytes_accessed=4 * received.size + 2 * steps * total * total,
+            transcendentals=0,
+        ),
+        name="legendre_solve",
+    )(waves, received, basis, solver)
+
+
+def synthesis_kernel(chunks, *refs):
+    parts, synth_ref, out_ref = refs[:chunks], refs[chunks], refs[chunks + 1]
+    owners, levels, rows, lats = parts[0].shape
+    half = synth_ref.shape[-1]
+    for level in range(levels):
+        sums = []
+        for parity in range(2):
+            total = None
+            for k in range(chunks):
+                found = parts[k][:, level, parity * (rows // 2) : (parity + 1) * (rows // 2), :]
+                term = dot(found.reshape(owners * rows // 2, lats), synth_ref[parity, k], TN)
+                total = term if total is None else total + term
+            sums.append(total)
+        out_ref[level, :, :half] = (sums[0] + sums[1]).astype(jnp.bfloat16)
+        out_ref[level, :, half:] = (sums[0] - sums[1]).astype(jnp.bfloat16)
+
+
+def run_synthesis(parts, synth):
+    owners, levels, rows, lats = parts[0].shape
+    lon_count = 2 * synth.shape[-1]
+    chunks = len(parts)
+    step = 2 if levels % 2 == 0 else 1
+    return pl.pallas_call(
+        functools.partial(synthesis_kernel, chunks),
+        grid=(levels // step,),
+        in_specs=[pl.BlockSpec((owners, step, rows, lats), lambda i: (0, i, 0, 0))] * chunks
+        + [pl.BlockSpec(synth.shape, lambda i: (0, 0, 0, 0))],
+        out_specs=pl.BlockSpec((step, lats, lon_count), lambda i: (i, 0, 0)),
+        out_shape=jax.ShapeDtypeStruct((levels, lats, lon_count), jnp.bfloat16),
+        compiler_params=pltpu.CompilerParams(vmem_limit_bytes=VMEM_BYTES),
+        cost_estimate=pl.CostEstimate(
+            flops=levels * lats * lon_count * lon_count,
+            bytes_accessed=4 * levels * lats * lon_count,
+            transcendentals=0,
+        ),
+        name="longitude_synthesis",
+    )(*parts, synth)
+
+
+def exchange(part):
+    owners, levels, rows, lats = part.shape
+    flat = part.reshape(owners, levels * rows, lats)
+    return lax.all_to_all(flat, OWNERS, 0, 0, tiled=True).reshape(part.shape)
+
+
+def chunked_shards(lat_bands, level_groups, chunks):
+    owners = lat_bands * level_groups
+
+    def shards(
+        thermal_state_grid,
+        thermal_forcing,
+        spherical_basis_table,
+        implicit_solver_matrix,
+        fourier_order_holder,
+    ):
+        slots = spherical_basis_table.shape[0]
+        per_chunk = slots // 2 // chunks
+        sends, synth = run_analysis(
+            owners, chunks, thermal_state_grid, thermal_forcing, fourier_order_holder
+        )
+        owner = lax.axis_index(OWNERS)
+        waves = lax.dynamic_slice_in_dim(fourier_order_holder, owner * slots, slots)
+        received = [exchange(part) for part in sends]
+        solved = [
+            run_columns(
+                k,
+                per_chunk,
+                lat_bands,
+                waves,
+                received[k],
+                spherical_basis_table,
+                implicit_solver_matrix,
+            )
+            for k in range(chunks)
+        ]
+        returned = [exchange(part) for part in solved]
+        return run_synthesis(returned, synth)
+
+    return shards
+
+
 def solution(mesh):
     shape = mesh.shape
-    shards = general_shards(shape["lat"], shape["lev"] * shape["sub"])
+    bands, groups = shape["lat"], shape["lev"] * shape["sub"]
+
+    def shards(state, forcing, basis, solver, holder):
+        levels, lats, lon_count = state.shape
+        pairs = basis.shape[0] // 2
+        tiled = pairs % (CHUNKS * TILE) == 0 and levels * groups % TILE == 0
+        if tiled and lats % 128 == 0 and lon_count == 2 * holder.shape[0]:
+            body = chunked_shards(bands, groups, CHUNKS)
+        else:
+            body = general_shards(bands, groups)
+        return body(state, forcing, basis, solver, holder)
+
     return jax.shard_map(
         shards,
         mesh=mesh,

time: 610 us -> 457 us (0.75); the launches traced: 600 us -> 454 us
  waiting for transfers between devices: 379 us -> 132 us
  blocking collectives: 0 us -> 207 us
  local copies, waits for them, and re-layouts: 130 us -> 2.82 us
  Pallas kernels: 0 us -> 101 us
  matrix products: 66.9 us -> 0 us
  other arithmetic: 11.7 us -> 0 us
    all_to_all x2, waiting for transfers between devices: 379 us -> 132 us  [exchange(): return lax.all_to_all(flat, OWNERS, 0, 0, tiled=True).reshape(part.shape)]
    all_to_all x0 -> x2, blocking collectives: none -> 207 us  [exchange(): return lax.all_to_all(flat, OWNERS, 0, 0, tiled=True).reshape(part.shape)]
    pallas_call x0 -> x4, Pallas kernels: none -> 101 us  [the longest x2 63.1 us: run_columns(): pl.pallas_call(functools.partial(column_kernel, k, per_chunk), grid_spec=...]
    reshape x6 -> x1, local copies, waits for them, and re-layouts: 76.6 us -> 1.47 us  [run_analysis(): holder.reshape(pairs, 2)]
    dot_general x5 -> x0, matrix products: 66.9 us -> none  [the longest x1 16.3 us: shards(): jnp.einsum('slx,sj->lxj', back, synthesis, preferred_element_type=jnp.flo...]
    convert_element_type x5 -> x0, local copies, waits for them, and re-layouts: 28.8 us -> none  [the longest x1 13.4 us: shards(): spectral = jnp.einsum('sj,lxj->slx', analysis, explicit, preferred_elemen...]
    all_to_all x1 -> x0, local copies, waits for them, and re-layouts: 18.3 us -> none  [shards(): spectral = lax.all_to_all(spectral, OWNERS, 0, 0, tiled=True)]
    cos x1 -> x0, other arithmetic: 9.17 us -> none  [raw_table(): stacked = jnp.stack([jnp.cos(angles), -jnp.sin(angles)], axis=1)]
  transfers between devices with their start and end apart: 2 -> 2, of which waited for: 2 -> 2; matrix products, arithmetic and copies ran while one was open for 1% -> 0% of each run, Pallas kernels for 0% -> 14%
where the time goes in v2:
time: 457 us; the launch traced here: 454 us
  blocking collectives  207 us (45%)
  waiting for transfers between devices  132 us (29%)
  Pallas kernels  101 us (22%)
  starting transfers between devices  10.4 us (2%)
    all_to_all x2, blocking collectives, exchange(): return lax.all_to_all(flat, OWNERS, 0, 0, tiled=True).reshape(part.shape)  207 us
    all_to_all x2, waiting for transfers between devices, exchange(): return lax.all_to_all(flat, OWNERS, 0, 0, tiled=True).reshape(part.shape)  132 us
    pallas_call x2, Pallas kernels, run_columns(): pl.pallas_call(functools.partial(column_kernel, k, per_chunk), grid_spec=...  63.1 us
    pallas_call x1, Pallas kernels, run_analysis(): pl.pallas_call(functools.partial(analysis_kernel, owners, chunks), grid=(...  21.8 us
    pallas_call x1, Pallas kernels, run_synthesis(): pl.pallas_call(functools.partial(synthesis_kernel, chunks), grid=(levels...  16.5 us
    all_to_all x2, starting transfers between devices, exchange(): return lax.all_to_all(flat, OWNERS, 0, 0, tiled=True).reshape(part.shape)  10.4 us
  transfers between devices with their start and end apart: 2, of which 2 were waited for; matrix products, arithmetic and copies ran while one was open for 0% of the time, Pallas kernels for 14%

profile of v2, /device:TPU:11, one launch (start us, length us, event | category | flops | bytes accessed | tf_op | source)
XLA Modules:
  0.0 453.8 jit_solution(4488294725997073248)
XLA Ops:
  0.0 1.5 reshape.27.holder_ref
  1.5 21.8 %longitude_analysis.1 = (bf16[16,34,32,128]{3,2,1,0:T(8,128)(2,1)}, bf16[16,34,32,128]{3,2,1,0:T(8,128)(2,1)}, bf16[2,2,256,512]{3,2,1,0:T(8,128)(2,1)}) custom-call(s32[256,2]{1,0:T(8,128)} %reshape.27.holder_ref, bf16[2,2,256,512]{3,2,1,0:T(8,128)(2,1)} %constant.23.clone.waves_ref, bf16[34,128,1024]{2,1,0:T(8,128)(2,1)} %state_ref.1, ...), custom_call_target="tpu_custom_call" | custom-call | flops 4563402752 | bytes 26738688 | tf_op jit(solution)/shard_map/longitude_analysis/pallas_call | solution.py:154
  23.3 104.5 %all_to_all.20 = bf16[16,1088,128]{2,1,0:T(8,128)(2,1)} all-to-all(bf16[16,1088,128]{2,1,0:T(8,128)(2,1)} %bitcast.13), channel_id=1, replica_groups=mesh['members'=2,'lat'=4,'lev'=2,'sub'=2] {'lat','lev','sub'}, dimensions={0} | all-to-all | bytes 8912896 | tf_op jit(solution)/shard_map/all_to_all | solution.py:321
  127.8 5.5 %all-to-all-start = ((bf16[16,1088,128]{2,1,0:T(8,128)(2,1)}), bf16[16,1088,128]{2,1,0:T(8,128)(2,1)}, u32[]{:S(2)}, u32[]{:S(2)}) async-start(bf16[16,1088,128]{2,1,0:T(8,128)(2,1)} %bitcast.12), calls=%async_computation | async-start | bytes 8912896 | tf_op jit(solution)/shard_map/all_to_all | solution.py:321
  133.3 1.3 dynamic_slice.3.waves_ref
  134.6 31.6 %legendre_solve.3 = bf16[16,34,32,128]{3,2,1,0:T(8,128)(2,1)} custom-call(s32[32]{0:T(128)} %dynamic_slice.3.waves_ref, bf16[16,34,32,128]{3,2,1,0:T(8,128)(2,1)} %bitcast.8, bf16[32,512,512]{2,1,0:T(8,128)(2,1)} %basis_ref.3, bf16[32,136,136]{2,1,0:T(8,128)(2,1)} %solver_ref.3), custom_call_target="tpu_custom_call" | custom-call | flops 4563402752 | bytes 17301504 | tf_op jit(solution)/shard_map/legendre_solve/pallas_call | solution.py:255
  166.3 65.1 %all-to-all-done = bf16[16,1088,128]{2,1,0:T(8,128)(2,1)} async-done(((bf16[16,1088,128]{2,1,0:T(8,128)(2,1)}), bf16[16,1088,128]{2,1,0:T(8,128)(2,1)}, u32[]{:S(2)}, u32[]{:S(2)}) %all-to-all-start) | async-done | bytes 4456480 | tf_op jit(solution)/shard_map/all_to_all | solution.py:321
  231.4 4.9 %all-to-all-start.3 = ((bf16[16,1088,128]{2,1,0:T(8,128)(2,1)}), bf16[16,1088,128]{2,1,0:T(8,128)(2,1)}, u32[]{:S(2)}, u32[]{:S(2)}) async-start(bf16[16,1088,128]{2,1,0:T(8,128)(2,1)} %bitcast.9), calls=%async_computation.3 | async-start | bytes 8912896 | tf_op jit(solution)/shard_map/all_to_all | solution.py:321
  236.3 31.5 %legendre_solve.2 = bf16[16,34,32,128]{3,2,1,0:T(8,128)(2,1)} custom-call(s32[32]{0:T(128)} %dynamic_slice.3.waves_ref, bf16[16,34,32,128]{3,2,1,0:T(8,128)(2,1)} %bitcast.1.recv_ref, bf16[32,512,512]{2,1,0:T(8,128)(2,1)} %basis_ref.3, bf16[32,136,136]{2,1,0:T(8,128)(2,1)} %solver_ref.3), custom_call_target="tpu_custom_call" | custom-call | flops 4563402752 | bytes 17301504 | tf_op jit(solution)/shard_map/legendre_solve/pallas_call | solution.py:255
  267.8 66.6 %all-to-all-done.3 = bf16[16,1088,128]{2,1,0:T(8,128)(2,1)} async-done(((bf16[16,1088,128]{2,1,0:T(8,128)(2,1)}), bf16[16,1088,128]{2,1,0:T(8,128)(2,1)}, u32[]{:S(2)}, u32[]{:S(2)}) %all-to-all-start.3) | async-done | bytes 4456480 | tf_op jit(solution)/shard_map/all_to_all | solution.py:321
  334.4 102.9 %all_to_all.21 = bf16[16,1088,128]{2,1,0:T(8,128)(2,1)} all-to-all(bf16[16,1088,128]{2,1,0:T(8,128)(2,1)} %bitcast.10), channel_id=1, replica_groups=mesh['members'=2,'lat'=4,'lev'=2,'sub'=2] {'lat','lev','sub'}, dimensions={0} | all-to-all | bytes 8912896 | tf_op jit(solution)/shard_map/all_to_all | solution.py:321
  437.2 16.5 %longitude_synthesis.1 = bf16[34,128,1024]{2,1,0:T(8,128)(2,1)} custom-call(bf16[16,34,32,128]{3,2,1,0:T(8,128)(2,1)} %bitcast.11, bf16[16,34,32,128]{3,2,1,0:T(8,128)(2,1)} %bitcast.7.refs_1_, bf16[2,2,256,512]{3,2,1,0:T(8,128)(2,1)} %get-tuple-element.10.refs_2_), custom_call_target="tpu_custom_call" | custom-call | flops 4563402752 | bytes 17825792 | tf_op jit(solution)/shard_map/longitude_synthesis/pallas_call | solution.py:301
Async XLA Ops:
  127.8 103.6 %all-to-all-start = ((bf16[16,1088,128]{2,1,0:T(8,128)(2,1)}), bf16[16,1088,128]{2,1,0:T(8,128)(2,1)}, u32[]{:S(2)}, u32[]{:S(2)}) async-start(bf16[16,1088,128]{2,1,0:T(8,128)(2,1)} %bitcast.12), calls=%async_computation | async-start | bytes 8912896 | tf_op jit(solution)/shard_map/all_to_all | solution.py:321
  231.4 103.0 %all-to-all-start.3 = ((bf16[16,1088,128]{2,1,0:T(8,128)(2,1)}), bf16[16,1088,128]{2,1,0:T(8,128)(2,1)}, u32[]{:S(2)}, u32[]{:S(2)}) async-start(bf16[16,1088,128]{2,1,0:T(8,128)(2,1)} %bitcast.9), calls=%async_computation.3 | async-start | bytes 8912896 | tf_op jit(solution)/shard_map/all_to_all | solution.py:321

commit v3 on v2

--- a/solution.py
+++ b/solution.py
@@ -96,79 +96,142 @@
     return table.astype(jnp.bfloat16)
 
 
+def wave_rows(owners, chunks, k, holder_ref, waves_ref, parity):
+    slots = holder_ref.shape[1]
+    per_chunk = slots // 2 // owners // chunks
+    wave = 2 * lax.broadcasted_iota(jnp.int32, (waves_ref.shape[2], slots), 0) + parity
+    held = (holder_ref[...] == wave).astype(jnp.float32).astype(jnp.bfloat16)
+    row = lax.broadcasted_iota(jnp.int32, (owners * per_chunk, slots), 0)
+    pair = (lax.div(row, per_chunk) * chunks + k) * per_chunk + lax.rem(row, per_chunk)
+    slot = lax.broadcasted_iota(jnp.int32, (owners * per_chunk, slots), 1)
+    chosen = (lax.div(slot, 2) == pair).astype(jnp.float32).astype(jnp.bfloat16)
+    pick = dot(chosen, held, NT)
+    picked = pick.astype(jnp.bfloat16)
+    parts = [
+        dot(picked, waves_ref[parity, c]).reshape(owners, per_chunk, waves_ref.shape[3])
+        for c in range(2)
+    ]
+    rows = jnp.concatenate(parts, axis=1).reshape(2 * per_chunk * owners, waves_ref.shape[3])
+    return rows, pick[:, 0:1]
+
+
 def analysis_kernel(
-    owners, chunks, holder_ref, waves_ref, state_ref, forcing_ref, *refs
+    owners, chunks, k, holder_ref, waves_ref, state_hbm, forcing_hbm, send_ref,
+    table, state, forcing, folded, arrived,
 ):
-    sends, synth_ref, table = refs[:chunks], refs[chunks], refs[chunks + 1]
-    pairs = holder_ref.shape[0]
-    per_chunk = pairs // owners // chunks
-    levels, lats, lon_count = state_ref.shape
+    steps, levels, lats, lon_count = state.shape
     half = lon_count // 2
-
-    @pl.when(pl.program_id(0) == 0)
-    def _():
-        first, second = holder_ref[:, 0:1], holder_ref[:, 1:2]
-        column = lax.broadcasted_iota(jnp.int32, (pairs, waves_ref.shape[2]), 1)
+    i = pl.program_id(0)
+
+    def copies(n):
+        rows = pl.ds(n * levels, levels)
+        return (
+            pltpu.make_async_copy(state_hbm.at[rows], state.at[n], arrived.at[n, 0]),
+            pltpu.make_async_copy(forcing_hbm.at[rows], forcing.at[n], arrived.at[n, 1]),
+        )
+
+    @pl.when(i == 0)
+    def _():
+        @pl.loop(0, steps)
+        def _(n):
+            for copy in copies(n):
+                copy.start()
+
         for parity in range(2):
-            wave = 2 * column + parity
-            pick = ((first == wave) | (second == wave)).astype(jnp.float32).astype(jnp.bfloat16)
-            weight = 2.0
-            if parity == 0:
-                weight = jnp.where((first == 0) | (second == 0), 1.0, 2.0)
-            parts, heavy = [], []
-            for c in range(2):
-                rows = dot(pick, waves_ref[parity, c])
-                parts.append(rows.reshape(owners, chunks, per_chunk, half))
-                heavy.append((rows * weight).reshape(owners, chunks, per_chunk, half))
-            for k in range(chunks):
-                rows = jnp.concatenate([part[:, k] for part in parts], axis=1)
-                table[parity, k] = rows.reshape(2 * per_chunk * owners, half).astype(jnp.bfloat16)
-                rows = jnp.concatenate([part[:, k] for part in heavy], axis=1)
-                synth_ref[parity, k] = rows.reshape(2 * per_chunk * owners, half).astype(
-                    jnp.bfloat16
-                )
-
-    state = state_ref[...].reshape(levels * lats, lon_count).astype(jnp.float32)
-    forcing = forcing_ref[...].reshape(levels * lats, lon_count).astype(jnp.float32)
-    explicit = 0.7 * state + 0.5 * forcing + 0.3 * state / (1.0 + state * state)
-    low, high = explicit[:, :half], explicit[:, half:]
-    for parity in range(2):
-        folded = (low + high if parity == 0 else low - high).astype(jnp.bfloat16)
-        for k in range(chunks):
-            found = dot(table[parity, k], folded, NT).astype(jnp.bfloat16)
-            found = found.reshape(owners, 2 * per_chunk, levels * lats)
-            rows = slice(parity * 2 * per_chunk, (parity + 1) * 2 * per_chunk)
+            rows, _ = wave_rows(owners, chunks, k, holder_ref, waves_ref, parity)
+            table[parity] = rows.astype(jnp.bfloat16)
+
+    @pl.when(i < steps)
+    def _():
+        for copy in copies(i):
+            copy.wait()
+
+    def step(now, last):
+        n = jnp.minimum(i, steps - 1)
+        for level in range(levels):
+            s = state[n, level].astype(jnp.float32)
+            f = forcing[n, level].astype(jnp.float32)
+            explicit = 0.7 * s + 0.5 * f + 0.3 * s / (1.0 + s * s)
+            low, high = explicit[:, :half], explicit[:, half:]
+            rows = slice(level * lats, (level + 1) * lats)
+            folded[now, 0, rows, :] = (low + high).astype(jnp.bfloat16)
+            folded[now, 1, rows, :] = (low - high).astype(jnp.bfloat16)
+        for parity in range(2):
+            found = dot(table[parity], folded[last, parity], NT).astype(jnp.bfloat16)
+            count = found.shape[0] // owners
+            found = found.reshape(owners, count, levels * lats)
+            rows = slice(parity * count, (parity + 1) * count)
             for level in range(levels):
-                sends[k][:, level, rows, :] = found[:, :, level * lats : (level + 1) * lats]
-
-
-def run_analysis(owners, chunks, state, forcing, holder):
+                send_ref[:, level, rows, :] = found[:, :, level * lats : (level + 1) * lats]
+
+    @pl.when(lax.rem(i, 2) == 0)
+    def _():
+        step(0, 1)
+
+    @pl.when(lax.rem(i, 2) == 1)
+    def _():
+        step(1, 0)
+
+
+def run_analysis(owners, chunks, k, state, forcing, holder, table):
     levels, lats, lon_count = state.shape
-    pairs = holder.shape[0] // 2
-    rows = 4 * pairs // owners // chunks
-    table = jnp.asarray(longitude_waves(lon_count))
-    step = 2 if levels % 2 == 0 else 1
-    block = pl.BlockSpec((step, lats, lon_count), lambda i: (i, 0, 0))
+    slots = holder.shape[1]
+    rows = 2 * slots // owners // chunks
+    count = 2 if levels % 2 == 0 else 1
+    steps = levels // count
     whole = lambda shape: pl.BlockSpec(shape, lambda i: (0,) * len(shape))
-    synth = (2, chunks, 2 * pairs // chunks, lon_count // 2)
-    outs = pl.pallas_call(
-        functools.partial(analysis_kernel, owners, chunks),
-        grid=(levels // step,),
-        in_specs=[whole((pairs, 2)), whole(table.shape), block, block],
-        out_specs=[pl.BlockSpec((owners, step, rows, lats), lambda i: (0, i, 0, 0))] * chunks
-        + [whole(synth)],
-        out_shape=[jax.ShapeDtypeStruct((owners, levels, rows, lats), jnp.bfloat16)] * chunks
-        + [jax.ShapeDtypeStruct(synth, jnp.bfloat16)],
-        scratch_shapes=[pltpu.VMEM(synth, jnp.bfloat16)],
+    kept = pltpu.VMEM((steps, count, lats, lon_count), jnp.bfloat16)
+    return pl.pallas_call(
+        functools.partial(analysis_kernel, owners, chunks, k),
+        grid=(steps + 1,),
+        in_specs=[whole(holder.shape), whole(table.shape)] + [pl.BlockSpec(memory_space=pl.ANY)] * 2,
+        out_specs=pl.BlockSpec(
+            (owners, count, rows, lats), lambda i: (0, jnp.maximum(i - 1, 0), 0, 0)
+        ),
+        out_shape=jax.ShapeDtypeStruct((owners, levels, rows, lats), jnp.bfloat16),
+        scratch_shapes=[
+            pltpu.VMEM((2, slots // chunks, lon_count // 2), jnp.bfloat16),
+            kept,
+            kept,
+            pltpu.VMEM((2, 2, count * lats, lon_count // 2), jnp.bfloat16),
+            pltpu.SemaphoreType.DMA((steps, 2)),
+        ],
         compiler_params=pltpu.CompilerParams(vmem_limit_bytes=VMEM_BYTES),
         cost_estimate=pl.CostEstimate(
-            flops=2 * levels * lats * lon_count * pairs * 2,
+            flops=2 * levels * lats * lon_count * slots // chunks,
             bytes_accessed=6 * levels * lats * lon_count,
             transcendentals=0,
         ),
         name="longitude_analysis",
-    )(holder.reshape(pairs, 2), table, state, forcing)
-    return outs[:chunks], outs[chunks]
+    )(holder, table, state, forcing)
+
+
+def synthesis_rows_kernel(owners, chunks, holder_ref, waves_ref, out_ref):
+    for parity in range(2):
+        for k in range(chunks):
+            rows, zero = wave_rows(owners, chunks, k, holder_ref, waves_ref, parity)
+            if parity == 0:
+                count = zero.shape[0] // owners
+                weight = (2.0 - zero).reshape(owners, count, 1)
+                weight = jnp.concatenate([weight, weight], axis=1).reshape(-1, 1)
+            else:
+                weight = 2.0
+            out_ref[parity, k] = (rows * weight).astype(jnp.bfloat16)
+
+
+def synthesis_rows(owners, chunks, holder, table):
+    shape = (2, chunks, holder.shape[1] // chunks, table.shape[3])
+    return pl.pallas_call(
+        functools.partial(synthesis_rows_kernel, owners, chunks),
+        out_shape=jax.ShapeDtypeStruct(shape, jnp.bfloat16),
+        compiler_params=pltpu.CompilerParams(vmem_limit_bytes=VMEM_BYTES),
+        cost_estimate=pl.CostEstimate(
+            flops=8 * holder.shape[1] * table.shape[2] * table.shape[3],
+            bytes_accessed=4 * holder.shape[1] * table.shape[3],
+            transcendentals=0,
+        ),
+        name="synthesis_rows",
+    )(holder, table)
 
 
 def slot_of(k, per_chunk, i, waves):
@@ -277,34 +340,60 @@
 
 
 def synthesis_kernel(chunks, *refs):
-    parts, synth_ref, out_ref = refs[:chunks], refs[chunks], refs[chunks + 1]
-    owners, levels, rows, lats = parts[0].shape
+    parts, (synth_ref, out_ref, kept, arrived) = refs[:chunks], refs[chunks:]
+    steps, _, owners, levels, rows, lats = kept.shape
     half = synth_ref.shape[-1]
-    for level in range(levels):
-        sums = []
-        for parity in range(2):
-            total = None
-            for k in range(chunks):
-                found = parts[k][:, level, parity * (rows // 2) : (parity + 1) * (rows // 2), :]
-                term = dot(found.reshape(owners * rows // 2, lats), synth_ref[parity, k], TN)
-                total = term if total is None else total + term
-            sums.append(total)
-        out_ref[level, :, :half] = (sums[0] + sums[1]).astype(jnp.bfloat16)
-        out_ref[level, :, half:] = (sums[0] - sums[1]).astype(jnp.bfloat16)
+    i = pl.program_id(0)
+
+    def copies(n):
+        span = pl.ds(n * levels, levels)
+        return [
+            pltpu.make_async_copy(part.at[:, span], kept.at[n, k], arrived.at[n, k])
+            for k, part in enumerate(parts)
+        ]
+
+    @pl.when(i == 0)
+    def _():
+        @pl.loop(0, steps)
+        def _(n):
+            for copy in copies(n):
+                copy.start()
+
+    for copy in copies(i):
+        copy.wait()
+    sums = []
+    for parity in range(2):
+        terms = []
+        for k in range(chunks):
+            found = kept[i, k, :, :, parity * (rows // 2) : (parity + 1) * (rows // 2), :]
+            found = jnp.concatenate(
+                [found[:, n].reshape(owners * rows // 2, lats) for n in range(levels)], axis=1
+            )
+            terms.append(dot(found, synth_ref[parity, k], TN))
+        sums.append(sum(terms[1:], terms[0]))
+    for n in range(levels):
+        even, odd = [found[n * lats : (n + 1) * lats] for found in sums]
+        out_ref[n, :, :half] = (even + odd).astype(jnp.bfloat16)
+        out_ref[n, :, half:] = (even - odd).astype(jnp.bfloat16)
 
 
 def run_synthesis(parts, synth):
     owners, levels, rows, lats = parts[0].shape
     lon_count = 2 * synth.shape[-1]
     chunks = len(parts)
-    step = 2 if levels % 2 == 0 else 1
+    count = 2 if levels % 2 == 0 else 1
+    steps = levels // count
     return pl.pallas_call(
         functools.partial(synthesis_kernel, chunks),
-        grid=(levels // step,),
-        in_specs=[pl.BlockSpec((owners, step, rows, lats), lambda i: (0, i, 0, 0))] * chunks
+        grid=(steps,),
+        in_specs=[pl.BlockSpec(memory_space=pl.ANY)] * chunks
         + [pl.BlockSpec(synth.shape, lambda i: (0, 0, 0, 0))],
-        out_specs=pl.BlockSpec((step, lats, lon_count), lambda i: (i, 0, 0)),
+        out_specs=pl.BlockSpec((count, lats, lon_count), lambda i: (i, 0, 0)),
         out_shape=jax.ShapeDtypeStruct((levels, lats, lon_count), jnp.bfloat16),
+        scratch_shapes=[
+            pltpu.VMEM((steps, chunks, owners, count, rows, lats), jnp.bfloat16),
+            pltpu.SemaphoreType.DMA((steps, chunks)),
+        ],
         compiler_params=pltpu.CompilerParams(vmem_limit_bytes=VMEM_BYTES),
         cost_estimate=pl.CostEstimate(
             flops=levels * lats * lon_count * lon_count,
@@ -333,9 +422,13 @@
     ):
         slots = spherical_basis_table.shape[0]
         per_chunk = slots // 2 // chunks
-        sends, synth = run_analysis(
-            owners, chunks, thermal_state_grid, thermal_forcing, fourier_order_holder
-        )
+        table = jnp.asarray(longitude_waves(thermal_state_grid.shape[2]))
+        holder = fourier_order_holder.reshape(1, -1)
+        sends = [
+            run_analysis(owners, chunks, k, thermal_state_grid, thermal_forcing, holder, table)
+            for k in range(chunks)
+        ]
+        synth = synthesis_rows(owners, chunks, holder, table)
         owner = lax.axis_index(OWNERS)
         waves = lax.dynamic_slice_in_dim(fourier_order_holder, owner * slots, slots)
         received = [exchange(part) for part in sends]

time: 457 us -> 444 us (0.972)
  blocking collectives: 207 us -> 0 us
  waiting for transfers between devices: 132 us -> 308 us
  Pallas kernels: 101 us -> 113 us
  starting transfers between devices: 10.4 us -> 21.3 us
    all_to_all x2 -> x0, blocking collectives: 207 us -> none  [exchange(): return lax.all_to_all(flat, OWNERS, 0, 0, tiled=True).reshape(part.shape)]
    all_to_all x2 -> x4, waiting for transfers between devices: 132 us -> 308 us  [exchange(): return lax.all_to_all(flat, OWNERS, 0, 0, tiled=True).reshape(part.shape)]
    pallas_call x2 -> x4, Pallas kernels: 38.3 us -> 49.6 us  [the longest x2 32.4 us: run_analysis(): pl.pallas_call(functools.partial(analysis_kernel, owners, chunks, k), gri...]
    all_to_all x2 -> x4, starting transfers between devices: 10.4 us -> 21.3 us  [exchange(): return lax.all_to_all(flat, OWNERS, 0, 0, tiled=True).reshape(part.shape)]
  transfers between devices with their start and end apart: 2 -> 4, of which waited for: 2 -> 4; matrix products, arithmetic and copies ran while one was open for 0% -> 0% of each run, Pallas kernels for 14% -> 19%
where the time goes in v3:
time: 444 us
  waiting for transfers between devices  308 us (69%)
  Pallas kernels  113 us (25%)
  starting transfers between devices  21.3 us (5%)
    all_to_all x4, waiting for transfers between devices, exchange(): return lax.all_to_all(flat, OWNERS, 0, 0, tiled=True).reshape(part.shape)  308 us
    pallas_call x2, Pallas kernels, run_columns(): pl.pallas_call(functools.partial(column_kernel, k, per_chunk), grid_spec=...  63.1 us
    pallas_call x2, Pallas kernels, run_analysis(): pl.pallas_call(functools.partial(analysis_kernel, owners, chunks, k), gri...  32.4 us
    all_to_all x4, starting transfers between devices, exchange(): return lax.all_to_all(flat, OWNERS, 0, 0, tiled=True).reshape(part.shape)  21.3 us
    pallas_call x1, Pallas kernels, run_synthesis(): pl.pallas_call(functools.partial(synthesis_kernel, chunks), grid=(steps,)...  14 us
  transfers between devices with their start and end apart: 4, of which 4 were waited for; matrix products, arithmetic and copies ran while one was open for 0% of the time, Pallas kernels for 19%

profile of v3, /device:TPU:11, one launch (start us, length us, event | category | flops | bytes accessed | tf_op | source)
XLA Modules:
  0.0 443.8 jit_solution(14650824593305984773)
XLA Ops:
  0.0 16.2 %longitude_analysis.3 = bf16[16,34,32,128]{3,2,1,0:T(8,128)(2,1)} custom-call(s32[1,512]{1,0:T(1,128)} %bitcast.13, bf16[2,2,256,512]{3,2,1,0:T(8,128)(2,1)} %constant.23.clone.waves_ref, bf16[34,128,1024]{2,1,0:T(8,128)(2,1)} %state_hbm.3, bf16[34,128,1024]{2,1,0:T(8,128)(2,1)} %forcing_hbm.3), custom_call_target="tpu_custom_call" | custom-call | flops 2281701376 | bytes 26738688 | tf_op jit(solution)/shard_map/longitude_analysis/pallas_call | solution.py:184
  16.2 6.6 %all-to-all-start.2 = ((bf16[16,1088,128]{2,1,0:T(8,128)(2,1)}), bf16[16,1088,128]{2,1,0:T(8,128)(2,1)}, u32[]{:S(2)}, u32[]{:S(2)}) async-start(bf16[16,1088,128]{2,1,0:T(8,128)(2,1)} %bitcast.12), calls=%async_computation.2 | async-start | bytes 8912896 | tf_op jit(solution)/shard_map/all_to_all | solution.py:410
  22.8 16.2 %longitude_analysis.2 = bf16[16,34,32,128]{3,2,1,0:T(8,128)(2,1)} custom-call(s32[1,512]{1,0:T(1,128)} %bitcast.14, bf16[2,2,256,512]{3,2,1,0:T(8,128)(2,1)} %constant.23.clone.waves_ref, bf16[34,128,1024]{2,1,0:T(8,128)(2,1)} %state_hbm.3, bf16[34,128,1024]{2,1,0:T(8,128)(2,1)} %forcing_hbm.3), custom_call_target="tpu_custom_call" | custom-call | flops 2281701376 | bytes 26738688 | tf_op jit(solution)/shard_map/longitude_analysis/pallas_call | solution.py:184
  39.0 81.9 %all-to-all-done.2 = bf16[16,1088,128]{2,1,0:T(8,128)(2,1)} async-done(((bf16[16,1088,128]{2,1,0:T(8,128)(2,1)}), bf16[16,1088,128]{2,1,0:T(8,128)(2,1)}, u32[]{:S(2)}, u32[]{:S(2)}) %all-to-all-start.2) | async-done | bytes 4456480 | tf_op jit(solution)/shard_map/all_to_all | solution.py:410
  120.9 4.9 %all-to-all-start = ((bf16[16,1088,128]{2,1,0:T(8,128)(2,1)}), bf16[16,1088,128]{2,1,0:T(8,128)(2,1)}, u32[]{:S(2)}, u32[]{:S(2)}) async-start(bf16[16,1088,128]{2,1,0:T(8,128)(2,1)} %bitcast.9), calls=%async_computation | async-start | bytes 8912896 | tf_op jit(solution)/shard_map/all_to_all | solution.py:410
  125.8 1.3 dynamic_slice.3.waves_ref
  127.1 31.6 %legendre_solve.3 = bf16[16,34,32,128]{3,2,1,0:T(8,128)(2,1)} custom-call(s32[32]{0:T(128)} %dynamic_slice.3.waves_ref, bf16[16,34,32,128]{3,2,1,0:T(8,128)(2,1)} %bitcast.6.recv_ref, bf16[32,512,512]{2,1,0:T(8,128)(2,1)} %basis_ref.3, bf16[32,136,136]{2,1,0:T(8,128)(2,1)} %solver_ref.3), custom_call_target="tpu_custom_call" | custom-call | flops 4563402752 | bytes 17301504 | tf_op jit(solution)/shard_map/legendre_solve/pallas_call | solution.py:318
  158.7 65.1 %all-to-all-done = bf16[16,1088,128]{2,1,0:T(8,128)(2,1)} async-done(((bf16[16,1088,128]{2,1,0:T(8,128)(2,1)}), bf16[16,1088,128]{2,1,0:T(8,128)(2,1)}, u32[]{:S(2)}, u32[]{:S(2)}) %all-to-all-start) | async-done | bytes 4456480 | tf_op jit(solution)/shard_map/all_to_all | solution.py:410
  223.9 4.9 %all-to-all-start.3 = ((bf16[16,1088,128]{2,1,0:T(8,128)(2,1)}), bf16[16,1088,128]{2,1,0:T(8,128)(2,1)}, u32[]{:S(2)}, u32[]{:S(2)}) async-start(bf16[16,1088,128]{2,1,0:T(8,128)(2,1)} %bitcast.10), calls=%async_computation.3 | async-start | bytes 8912896 | tf_op jit(solution)/shard_map/all_to_all | solution.py:410
  228.8 31.5 %legendre_solve.2 = bf16[16,34,32,128]{3,2,1,0:T(8,128)(2,1)} custom-call(s32[32]{0:T(128)} %dynamic_slice.3.waves_ref, bf16[16,34,32,128]{3,2,1,0:T(8,128)(2,1)} %bitcast.2.recv_ref, bf16[32,512,512]{2,1,0:T(8,128)(2,1)} %basis_ref.3, bf16[32,136,136]{2,1,0:T(8,128)(2,1)} %solver_ref.3), custom_call_target="tpu_custom_call" | custom-call | flops 4563402752 | bytes 17301504 | tf_op jit(solution)/shard_map/legendre_solve/pallas_call | solution.py:318
  260.3 66.6 %all-to-all-done.3 = bf16[16,1088,128]{2,1,0:T(8,128)(2,1)} async-done(((bf16[16,1088,128]{2,1,0:T(8,128)(2,1)}), bf16[16,1088,128]{2,1,0:T(8,128)(2,1)}, u32[]{:S(2)}, u32[]{:S(2)}) %all-to-all-start.3) | async-done | bytes 4456480 | tf_op jit(solution)/shard_map/all_to_all | solution.py:410
  326.9 4.9 %all-to-all-start.1 = ((bf16[16,1088,128]{2,1,0:T(8,128)(2,1)}), bf16[16,1088,128]{2,1,0:T(8,128)(2,1)}, u32[]{:S(2)}, u32[]{:S(2)}) async-start(bf16[16,1088,128]{2,1,0:T(8,128)(2,1)} %bitcast.11), calls=%async_computation.1 | async-start | bytes 8912896 | tf_op jit(solution)/shard_map/all_to_all | solution.py:410
  331.8 3.2 synthesis_rows.1.refs_2_
  334.9 94.9 %all-to-all-done.1 = bf16[16,1088,128]{2,1,0:T(8,128)(2,1)} async-done(((bf16[16,1088,128]{2,1,0:T(8,128)(2,1)}), bf16[16,1088,128]{2,1,0:T(8,128)(2,1)}, u32[]{:S(2)}, u32[]{:S(2)}) %all-to-all-start.1) | async-done | bytes 4456480 | tf_op jit(solution)/shard_map/all_to_all | solution.py:410
  429.9 14.0 %longitude_synthesis.1 = bf16[34,128,1024]{2,1,0:T(8,128)(2,1)} custom-call(bf16[16,34,32,128]{3,2,1,0:T(8,128)(2,1)} %bitcast.4.refs_0_, bf16[16,34,32,128]{3,2,1,0:T(8,128)(2,1)} %bitcast.8.refs_1_, bf16[2,2,256,512]{3,2,1,0:T(8,128)(2,1)} %synthesis_rows.1.refs_2_), custom_call_target="tpu_custom_call" | custom-call | flops 4563402752 | bytes 17825792 | tf_op jit(solution)/shard_map/longitude_synthesis/pallas_call | solution.py:386
Async XLA Ops:
  16.2 104.7 %all-to-all-start.2 = ((bf16[16,1088,128]{2,1,0:T(8,128)(2,1)}), bf16[16,1088,128]{2,1,0:T(8,128)(2,1)}, u32[]{:S(2)}, u32[]{:S(2)}) async-start(bf16[16,1088,128]{2,1,0:T(8,128)(2,1)} %bitcast.12), calls=%async_computation.2 | async-start | bytes 8912896 | tf_op jit(solution)/shard_map/all_to_all | solution.py:410
  120.9 103.0 %all-to-all-start = ((bf16[16,1088,128]{2,1,0:T(8,128)(2,1)}), bf16[16,1088,128]{2,1,0:T(8,128)(2,1)}, u32[]{:S(2)}, u32[]{:S(2)}) async-start(bf16[16,1088,128]{2,1,0:T(8,128)(2,1)} %bitcast.9), calls=%async_computation | async-start | bytes 8912896 | tf_op jit(solution)/shard_map/all_to_all | solution.py:410
  223.9 103.0 %all-to-all-start.3 = ((bf16[16,1088,128]{2,1,0:T(8,128)(2,1)}), bf16[16,1088,128]{2,1,0:T(8,128)(2,1)}, u32[]{:S(2)}, u32[]{:S(2)}) async-start(bf16[16,1088,128]{2,1,0:T(8,128)(2,1)} %bitcast.10), calls=%async_computation.3 | async-start | bytes 8912896 | tf_op jit(solution)/shard_map/all_to_all | solution.py:410
  326.9 103.0 %all-to-all-start.1 = ((bf16[16,1088,128]{2,1,0:T(8,128)(2,1)}), bf16[16,1088,128]{2,1,0:T(8,128)(2,1)}, u32[]{:S(2)}, u32[]{:S(2)}) async-start(bf16[16,1088,128]{2,1,0:T(8,128)(2,1)} %bitcast.11), calls=%async_computation.1 | async-start | bytes 8912896 | tf_op jit(solution)/shard_map/all_to_all | solution.py:410

commit v4 on v3

--- a/solution.py
+++ b/solution.py
@@ -116,61 +116,83 @@
 
 
 def analysis_kernel(
-    owners, chunks, k, holder_ref, waves_ref, state_hbm, forcing_hbm, send_ref,
-    table, state, forcing, folded, arrived,
+    owners, chunks, k, holder_ref, waves_hbm, state_hbm, forcing_hbm, send_hbm,
+    waves, table, state, forcing, folded, send, ready, arrived, left,
 ):
     steps, levels, lats, lon_count = state.shape
     half = lon_count // 2
-    i = pl.program_id(0)
+    rows = send.shape[2]
 
     def copies(n):
-        rows = pl.ds(n * levels, levels)
+        span = pl.ds(n * levels, levels)
         return (
-            pltpu.make_async_copy(state_hbm.at[rows], state.at[n], arrived.at[n, 0]),
-            pltpu.make_async_copy(forcing_hbm.at[rows], forcing.at[n], arrived.at[n, 1]),
+            pltpu.make_async_copy(state_hbm.at[span], state.at[n], arrived.at[n, 0]),
+            pltpu.make_async_copy(forcing_hbm.at[span], forcing.at[n], arrived.at[n, 1]),
         )
 
-    @pl.when(i == 0)
-    def _():
-        @pl.loop(0, steps)
-        def _(n):
-            for copy in copies(n):
-                copy.start()
-
-        for parity in range(2):
-            rows, _ = wave_rows(owners, chunks, k, holder_ref, waves_ref, parity)
-            table[parity] = rows.astype(jnp.bfloat16)
-
-    @pl.when(i < steps)
-    def _():
-        for copy in copies(i):
+    def leaving(n):
+        span = pl.ds(n * levels, levels)
+        return pltpu.make_async_copy(send.at[:, span], send_hbm.at[:, span], left.at[n])
+
+    fetch = pltpu.make_async_copy(waves_hbm, waves, ready)
+    fetch.start()
+
+    @pl.loop(0, steps)
+    def _(n):
+        for copy in copies(n):
+            copy.start()
+
+    fetch.wait()
+    for parity in range(2):
+        found, _ = wave_rows(owners, chunks, k, holder_ref, waves, parity)
+        table[parity] = found.astype(jnp.bfloat16)
+
+    def take(n):
+        for copy in copies(n):
             copy.wait()
 
-    def step(now, last):
-        n = jnp.minimum(i, steps - 1)
+    def fold(n, now):
         for level in range(levels):
             s = state[n, level].astype(jnp.float32)
             f = forcing[n, level].astype(jnp.float32)
             explicit = 0.7 * s + 0.5 * f + 0.3 * s / (1.0 + s * s)
             low, high = explicit[:, :half], explicit[:, half:]
-            rows = slice(level * lats, (level + 1) * lats)
-            folded[now, 0, rows, :] = (low + high).astype(jnp.bfloat16)
-            folded[now, 1, rows, :] = (low - high).astype(jnp.bfloat16)
+            span = slice(level * lats, (level + 1) * lats)
+            folded[now, 0, span, :] = (low + high).astype(jnp.bfloat16)
+            folded[now, 1, span, :] = (low - high).astype(jnp.bfloat16)
+
+    def transform(n, now):
         for parity in range(2):
-            found = dot(table[parity], folded[last, parity], NT).astype(jnp.bfloat16)
-            count = found.shape[0] // owners
-            found = found.reshape(owners, count, levels * lats)
-            rows = slice(parity * count, (parity + 1) * count)
+            found = dot(table[parity], folded[now, parity], NT).astype(jnp.bfloat16)
+            found = found.reshape(owners, rows // 2, levels * lats)
+            mine = slice(parity * (rows // 2), (parity + 1) * (rows // 2))
             for level in range(levels):
-                send_ref[:, level, rows, :] = found[:, :, level * lats : (level + 1) * lats]
-
-    @pl.when(lax.rem(i, 2) == 0)
-    def _():
-        step(0, 1)
-
-    @pl.when(lax.rem(i, 2) == 1)
-    def _():
-        step(1, 0)
+                send[:, n * levels + level, mine, :] = found[
+                    :, :, level * lats : (level + 1) * lats
+                ]
+        leaving(n).start()
+
+    take(0)
+    fold(0, 0)
+
+    @pl.loop(0, (steps - 1) // 2)
+    def _(j):
+        take(2 * j + 1)
+        take(2 * j + 2)
+        transform(2 * j, 0)
+        fold(2 * j + 1, 1)
+        transform(2 * j + 1, 1)
+        fold(2 * j + 2, 0)
+
+    if steps % 2 == 0:
+        take(steps - 1)
+        fold(steps - 1, 1)
+        transform(steps - 2, 0)
+    transform(steps - 1, (steps - 1) % 2)
+
+    @pl.loop(0, steps)
+    def _(n):
+        leaving(n).wait()
 
 
 def run_analysis(owners, chunks, k, state, forcing, holder, table):
@@ -179,22 +201,23 @@
     rows = 2 * slots // owners // chunks
     count = 2 if levels % 2 == 0 else 1
     steps = levels // count
-    whole = lambda shape: pl.BlockSpec(shape, lambda i: (0,) * len(shape))
     kept = pltpu.VMEM((steps, count, lats, lon_count), jnp.bfloat16)
+    anywhere = pl.BlockSpec(memory_space=pl.ANY)
     return pl.pallas_call(
         functools.partial(analysis_kernel, owners, chunks, k),
-        grid=(steps + 1,),
-        in_specs=[whole(holder.shape), whole(table.shape)] + [pl.BlockSpec(memory_space=pl.ANY)] * 2,
-        out_specs=pl.BlockSpec(
-            (owners, count, rows, lats), lambda i: (0, jnp.maximum(i - 1, 0), 0, 0)
-        ),
+        in_specs=[pl.BlockSpec(memory_space=pltpu.VMEM)] + [anywhere] * 3,
+        out_specs=anywhere,
         out_shape=jax.ShapeDtypeStruct((owners, levels, rows, lats), jnp.bfloat16),
         scratch_shapes=[
+            pltpu.VMEM(table.shape, jnp.bfloat16),
             pltpu.VMEM((2, slots // chunks, lon_count // 2), jnp.bfloat16),
             kept,
             kept,
             pltpu.VMEM((2, 2, count * lats, lon_count // 2), jnp.bfloat16),
+            pltpu.VMEM((owners, levels, rows, lats), jnp.bfloat16),
+            pltpu.SemaphoreType.DMA,
             pltpu.SemaphoreType.DMA((steps, 2)),
+            pltpu.SemaphoreType.DMA((steps,)),
         ],
         compiler_params=pltpu.CompilerParams(vmem_limit_bytes=VMEM_BYTES),
         cost_estimate=pl.CostEstimate(
@@ -234,96 +257,107 @@
     )(holder, table)
 
 
-def slot_of(k, per_chunk, i, waves):
-    first = 2 * (k * per_chunk + lax.rem(i, per_chunk))
-    odd = lax.rem(waves[first], 2)
-    return first + lax.rem(odd + i // per_chunk, 2)
+def pair_slots(first, waves, middle):
+    late = (waves[first] >= middle).astype(jnp.int32)
+    return first + late, first + 1 - late
 
 
 def column_kernel(
-    k, per_chunk, waves_ref, recv_ref, basis_ref, solver_ref, send_ref, spread, back
+    bands, k, waves_ref, recv_ref, low_basis, high_basis, low_solver, high_solver, send_ref,
+    spread, back,
 ):
     owners, levels, rows, lats = recv_ref.shape
-    bands = spread.shape[0]
     groups = owners // bands
+    per_chunk = rows // 4
     depth = groups * levels
-    total = basis_ref.shape[1]
+    total = low_basis.shape[1]
+    middle = total // 2
     i = pl.program_id(0)
+
+    def places():
+        size = levels * (rows + TILE)
+        for r in range(owners):
+            yield r, r // groups, slice(r % groups * size, (r % groups + 1) * size)
 
     @pl.when(i == 0)
     def _():
-        for a in range(bands):
-            for g in range(groups):
-                part = recv_ref[a * groups + g].astype(jnp.float32)
-                spread[a, g * levels * rows : (g + 1) * levels * rows, :] = part.reshape(
-                    levels * rows, lats
-                )
-
-    wave = waves_ref[slot_of(k, per_chunk, i, waves_ref)]
-    base = (i // per_chunk) * (2 * per_chunk) + lax.rem(i, per_chunk)
-    starts = [base, base + per_chunk]
-
-    def column(low):
-        count = total - low
-        taken = [
+        for r, band, span in places():
+            part = recv_ref[r].astype(jnp.float32)
+            part = jnp.concatenate([part, part[:, :TILE]], axis=1)
+            spread[band, span, :] = part.reshape(-1, lats)
+
+    slots = pair_slots(2 * (k * per_chunk + i), waves_ref, middle)
+    waves = [waves_ref[slot] for slot in slots]
+    bases = [lax.rem(wave, 2) * (2 * per_chunk) + i for wave in waves]
+    basis = [low_basis[0], high_basis[0]]
+    solvers = [low_solver[0], high_solver[0]]
+    lows = [0, middle]
+    taken, coeffs, solved, grid = [], [], [], []
+    for w in range(2):
+        parts = [
             jnp.concatenate(
-                [spread[a, pl.ds(start, depth, stride=rows), :] for a in range(bands)], axis=1
+                [
+                    spread[a, pl.ds(bases[w] + c * per_chunk, depth, stride=rows + TILE), :]
+                    for a in range(bands)
+                ],
+                axis=1,
             )
-            for start in starts
-        ]
-        taken = jnp.concatenate(taken, axis=0).astype(jnp.bfloat16)
-        basis = basis_ref[0, :, low:]
-        coeffs = dot(taken, basis)
-        coeffs = jnp.concatenate([coeffs[:depth], coeffs[depth:]], axis=1).astype(jnp.bfloat16)
-        solved = dot(solver_ref[0], coeffs)
-        degree = low + lax.broadcasted_iota(jnp.int32, (depth, count), 1)
-        parts = [
-            jnp.where(degree >= wave, solved[:, c * count : (c + 1) * count], 0.0)
             for c in range(2)
         ]
-        solved = jnp.concatenate(parts, axis=0).astype(jnp.bfloat16)
-        grid = dot(solved, basis, NT)
+        taken.append(jnp.concatenate(parts, axis=0).astype(jnp.bfloat16))
+    for w in range(2):
+        found = dot(taken[w], basis[w])
+        coeffs.append(
+            jnp.concatenate([found[:depth], found[depth:]], axis=1).astype(jnp.bfloat16)
+        )
+    for w in range(2):
+        found = dot(solvers[w], coeffs[w])
+        count = total - lows[w]
+        degree = lows[w] + lax.broadcasted_iota(jnp.int32, (depth, count), 1)
+        parts = [
+            jnp.where(degree >= waves[w], found[:, c * count : (c + 1) * count], 0.0)
+            for c in range(2)
+        ]
+        solved.append(jnp.concatenate(parts, axis=0).astype(jnp.bfloat16))
+    for w in range(2):
+        grid.append(dot(solved[w], basis[w], NT))
+    for w in range(2):
         for c in range(2):
             for a in range(bands):
-                back[a, pl.ds(starts[c], depth, stride=rows), :] = grid[
+                back[a, pl.ds(bases[w] + c * per_chunk, depth, stride=rows + TILE), :] = grid[w][
                     c * depth : (c + 1) * depth, a * lats : (a + 1) * lats
                 ]
 
-    middle = total // 2
-
-    @pl.when(wave < middle)
-    def _():
-        column(0)
-
-    @pl.when(wave >= middle)
-    def _():
-        column(middle)
-
     @pl.when(i == pl.num_programs(0) - 1)
     def _():
-        for a in range(bands):
-            for g in range(groups):
-                part = back[a, g * levels * rows : (g + 1) * levels * rows, :]
-                send_ref[a * groups + g] = part.reshape(levels, rows, lats).astype(jnp.bfloat16)
-
-
-def run_columns(k, per_chunk, bands, waves, received, basis, solver):
+        for r, band, span in places():
+            part = back[band, span, :].reshape(levels, rows + TILE, lats)
+            send_ref[r] = part[:, :rows].astype(jnp.bfloat16)
+
+
+def run_columns(k, bands, waves, received, basis, solver):
     owners, levels, rows, lats = received.shape
     depth = owners // bands * levels
     total = basis.shape[1]
-    steps = 2 * per_chunk
-    slot = lambda i, waves_ref: (slot_of(k, per_chunk, i, waves_ref), 0, 0)
+    middle = total // 2
+    steps = rows // 4
+    first = lambda i: 2 * (k * steps + i)
+    low = lambda i, waves_ref: (pair_slots(first(i), waves_ref, middle)[0], 0, 0)
+    high = lambda i, waves_ref: (pair_slots(first(i), waves_ref, middle)[1], 0, 0)
+    upper = lambda i, waves_ref: (pair_slots(first(i), waves_ref, middle)[1], 0, 1)
     whole = pl.BlockSpec(received.shape, lambda i, waves_ref: (0, 0, 0, 0))
-    scratch = pltpu.VMEM((bands, depth * rows, lats), jnp.float32)
+    scratch = pltpu.VMEM((bands, depth * (rows + TILE), lats), jnp.float32)
     return pl.pallas_call(
-        functools.partial(column_kernel, k, per_chunk),
+        functools.partial(column_kernel, bands, k),
         grid_spec=pltpu.PrefetchScalarGridSpec(
             num_scalar_prefetch=1,
             grid=(steps,),
             in_specs=[
                 whole,
-                pl.BlockSpec((1, total, total), slot),
-                pl.BlockSpec((1, depth, depth), slot),
+                pl.BlockSpec((1, total, total), low),
+                pl.BlockSpec((1, total, total - middle), upper),
+                pl.BlockSpec((1, depth, depth), low),
+                pl.BlockSpec((1, depth, depth), high),
             ],
             out_specs=whole,
             scratch_shapes=[scratch, scratch],
@@ -331,19 +365,18 @@
         out_shape=jax.ShapeDtypeStruct(received.shape, jnp.bfloat16),
         compiler_params=pltpu.CompilerParams(vmem_limit_bytes=VMEM_BYTES),
         cost_estimate=pl.CostEstimate(
-            flops=4 * steps * 2 * depth * total * total,
-            bytes_accessed=4 * received.size + 2 * steps * total * total,
+            flops=6 * steps * 2 * depth * total * total,
+            bytes_accessed=4 * received.size + 3 * steps * total * total,
             transcendentals=0,
         ),
         name="legendre_solve",
-    )(waves, received, basis, solver)
+    )(waves, received, basis, basis, solver, solver)
 
 
 def synthesis_kernel(chunks, *refs):
-    parts, (synth_ref, out_ref, kept, arrived) = refs[:chunks], refs[chunks:]
+    parts, (synth_ref, out_hbm, kept, out, arrived, left) = refs[:chunks], refs[chunks:]
     steps, _, owners, levels, rows, lats = kept.shape
     half = synth_ref.shape[-1]
-    i = pl.program_id(0)
 
     def copies(n):
         span = pl.ds(n * levels, levels)
@@ -352,29 +385,38 @@
             for k, part in enumerate(parts)
         ]
 
-    @pl.when(i == 0)
-    def _():
-        @pl.loop(0, steps)
-        def _(n):
-            for copy in copies(n):
-                copy.start()
-
-    for copy in copies(i):
-        copy.wait()
-    sums = []
-    for parity in range(2):
-        terms = []
-        for k in range(chunks):
-            found = kept[i, k, :, :, parity * (rows // 2) : (parity + 1) * (rows // 2), :]
-            found = jnp.concatenate(
-                [found[:, n].reshape(owners * rows // 2, lats) for n in range(levels)], axis=1
-            )
-            terms.append(dot(found, synth_ref[parity, k], TN))
-        sums.append(sum(terms[1:], terms[0]))
-    for n in range(levels):
-        even, odd = [found[n * lats : (n + 1) * lats] for found in sums]
-        out_ref[n, :, :half] = (even + odd).astype(jnp.bfloat16)
-        out_ref[n, :, half:] = (even - odd).astype(jnp.bfloat16)
+    def leaving(n):
+        span = pl.ds(n * levels, levels)
+        return pltpu.make_async_copy(out.at[span], out_hbm.at[span], left.at[n])
+
+    @pl.loop(0, steps)
+    def _(n):
+        for copy in copies(n):
+            copy.start()
+
+    @pl.loop(0, steps)
+    def _(i):
+        for copy in copies(i):
+            copy.wait()
+        sums = []
+        for parity in range(2):
+            terms = []
+            for k in range(chunks):
+                found = kept[i, k, :, :, parity * (rows // 2) : (parity + 1) * (rows // 2), :]
+                found = jnp.concatenate(
+                    [found[:, n].reshape(owners * rows // 2, lats) for n in range(levels)], axis=1
+                )
+                terms.append(dot(found, synth_ref[parity, k], TN))
+            sums.append(sum(terms[1:], terms[0]))
+        for n in range(levels):
+            even, odd = [found[n * lats : (n + 1) * lats] for found in sums]
+            out[i * levels + n, :, :half] = (even + odd).astype(jnp.bfloat16)
+            out[i * levels + n, :, half:] = (even - odd).astype(jnp.bfloat16)
+        leaving(i).start()
+
+    @pl.loop(0, steps)
+    def _(n):
+        leaving(n).wait()
 
 
 def run_synthesis(parts, synth):
@@ -383,16 +425,17 @@
     chunks = len(parts)
     count = 2 if levels % 2 == 0 else 1
     steps = levels // count
+    anywhere = pl.BlockSpec(memory_space=pl.ANY)
     return pl.pallas_call(
         functools.partial(synthesis_kernel, chunks),
-        grid=(steps,),
-        in_specs=[pl.BlockSpec(memory_space=pl.ANY)] * chunks
-        + [pl.BlockSpec(synth.shape, lambda i: (0, 0, 0, 0))],
-        out_specs=pl.BlockSpec((count, lats, lon_count), lambda i: (i, 0, 0)),
+        in_specs=[anywhere] * chunks + [pl.BlockSpec(memory_space=pltpu.VMEM)],
+        out_specs=anywhere,
         out_shape=jax.ShapeDtypeStruct((levels, lats, lon_count), jnp.bfloat16),
         scratch_shapes=[
             pltpu.VMEM((steps, chunks, owners, count, rows, lats), jnp.bfloat16),
+            pltpu.VMEM((levels, lats, lon_count), jnp.bfloat16),
             pltpu.SemaphoreType.DMA((steps, chunks)),
+            pltpu.SemaphoreType.DMA((steps,)),
         ],
         compiler_params=pltpu.CompilerParams(vmem_limit_bytes=VMEM_BYTES),
         cost_estimate=pl.CostEstimate(
@@ -421,7 +464,6 @@
         fourier_order_holder,
     ):
         slots = spherical_basis_table.shape[0]
-        per_chunk = slots // 2 // chunks
         table = jnp.asarray(longitude_waves(thermal_state_grid.shape[2]))
         holder = fourier_order_holder.reshape(1, -1)
         sends = [
@@ -435,7 +477,6 @@
         solved = [
             run_columns(
                 k,
-                per_chunk,
                 lat_bands,
                 waves,
                 received[k],

time: 444 us -> 440 us (level)
  Pallas kernels: 113 us -> 72.6 us
  waiting for transfers between devices: 308 us -> 344 us
    pallas_call x5, Pallas kernels: 110 us -> 69.4 us  [the longest x2 30.7 us: run_columns(): pl.pallas_call(functools.partial(column_kernel, bands, k), grid_spec=pltp...]
    all_to_all x4, waiting for transfers between devices: 308 us -> 344 us  [exchange(): return lax.all_to_all(flat, OWNERS, 0, 0, tiled=True).reshape(part.shape)]
  transfers between devices with their start and end apart: 4 -> 4, of which waited for: 4 -> 4; matrix products, arithmetic and copies ran while one was open for 0% -> 0% of each run, Pallas kernels for 19% -> 11%
where the time goes in v4:
time: 440 us; the launch traced here: 439 us
  waiting for transfers between devices  344 us (78%)
  Pallas kernels  72.6 us (16%)
  starting transfers between devices  21.3 us (5%)
    all_to_all x4, waiting for transfers between devices, exchange(): return lax.all_to_all(flat, OWNERS, 0, 0, tiled=True).reshape(part.shape)  344 us
    pallas_call x2, Pallas kernels, run_columns(): pl.pallas_call(functools.partial(column_kernel, bands, k), grid_spec=pltp...  30.7 us
    pallas_call x2, Pallas kernels, run_analysis(): pl.pallas_call(functools.partial(analysis_kernel, owners, chunks, k), in_...  27.1 us
    all_to_all x4, starting transfers between devices, exchange(): return lax.all_to_all(flat, OWNERS, 0, 0, tiled=True).reshape(part.shape)  21.3 us
    pallas_call x1, Pallas kernels, run_synthesis(): pl.pallas_call(functools.partial(synthesis_kernel, chunks), in_specs=[any...  11.7 us
  transfers between devices with their start and end apart: 4, of which 4 were waited for; matrix products, arithmetic and copies ran while one was open for 0% of the time, Pallas kernels for 11%

profile of v4, /device:TPU:11, one launch (start us, length us, event | category | flops | bytes accessed | tf_op | source)
XLA Modules:
  0.0 438.9 jit_solution(18263221217833084977)
XLA Ops:
  0.0 13.6 %longitude_analysis.3 = bf16[16,34,32,128]{3,2,1,0:T(8,128)(2,1)} custom-call(s32[1,512]{1,0:T(1,128)} %bitcast.13, bf16[2,2,256,512]{3,2,1,0:T(8,128)(2,1)} %constant.23.clone.waves_hbm.waves_ref, bf16[34,128,1024]{2,1,0:T(8,128)(2,1)} %state_hbm.3, bf16[34,128,1024]{2,1,0:T(8,128)(2,1)} %forcing_hbm.3), custom_call_target="tpu_custom_call" | custom-call | flops 2281701376 | bytes 26738688 | tf_op jit(solution)/shard_map/longitude_analysis/pallas_call | solution.py:206
  13.6 6.6 %all-to-all-start.2 = ((bf16[16,1088,128]{2,1,0:T(8,128)(2,1)}), bf16[16,1088,128]{2,1,0:T(8,128)(2,1)}, u32[]{:S(2)}, u32[]{:S(2)}) async-start(bf16[16,1088,128]{2,1,0:T(8,128)(2,1)} %bitcast.12), calls=%async_computation.2 | async-start | bytes 8912896 | tf_op jit(solution)/shard_map/all_to_all | solution.py:453
  20.1 13.6 %longitude_analysis.2 = bf16[16,34,32,128]{3,2,1,0:T(8,128)(2,1)} custom-call(s32[1,512]{1,0:T(1,128)} %bitcast.14, bf16[2,2,256,512]{3,2,1,0:T(8,128)(2,1)} %constant.23.clone.waves_hbm.waves_ref, bf16[34,128,1024]{2,1,0:T(8,128)(2,1)} %state_hbm.3, bf16[34,128,1024]{2,1,0:T(8,128)(2,1)} %forcing_hbm.3), custom_call_target="tpu_custom_call" | custom-call | flops 2281701376 | bytes 26738688 | tf_op jit(solution)/shard_map/longitude_analysis/pallas_call | solution.py:206
  33.7 84.5 %all-to-all-done.2 = bf16[16,1088,128]{2,1,0:T(8,128)(2,1)} async-done(((bf16[16,1088,128]{2,1,0:T(8,128)(2,1)}), bf16[16,1088,128]{2,1,0:T(8,128)(2,1)}, u32[]{:S(2)}, u32[]{:S(2)}) %all-to-all-start.2) | async-done | bytes 4456480 | tf_op jit(solution)/shard_map/all_to_all | solution.py:453
  118.2 4.9 %all-to-all-start = ((bf16[16,1088,128]{2,1,0:T(8,128)(2,1)}), bf16[16,1088,128]{2,1,0:T(8,128)(2,1)}, u32[]{:S(2)}, u32[]{:S(2)}) async-start(bf16[16,1088,128]{2,1,0:T(8,128)(2,1)} %bitcast.11), calls=%async_computation | async-start | bytes 8912896 | tf_op jit(solution)/shard_map/all_to_all | solution.py:453
  123.1 1.3 dynamic_slice.3.waves_ref
  124.5 15.4 %legendre_solve.3 = bf16[16,34,32,128]{3,2,1,0:T(8,128)(2,1)} custom-call(s32[32]{0:T(128)} %dynamic_slice.3.waves_ref, bf16[16,34,32,128]{3,2,1,0:T(8,128)(2,1)} %bitcast.6.recv_ref, bf16[32,512,512]{2,1,0:T(8,128)(2,1)} %high_basis.3, bf16[32,512,512]{2,1,0:T(8,128)(2,1)} %high_basis.3, bf16[32,136,136]{2,1,0:T(8,128)(2,1)} %high_solver.3, ...), custom_call_target="tpu_custom_call" | custom-call | flops 3422552064 | bytes 15204352 | tf_op jit(solution)/shard_map/legendre_solve/pallas_call | solution.py:350
  139.8 81.4 %all-to-all-done = bf16[16,1088,128]{2,1,0:T(8,128)(2,1)} async-done(((bf16[16,1088,128]{2,1,0:T(8,128)(2,1)}), bf16[16,1088,128]{2,1,0:T(8,128)(2,1)}, u32[]{:S(2)}, u32[]{:S(2)}) %all-to-all-start) | async-done | bytes 4456480 | tf_op jit(solution)/shard_map/all_to_all | solution.py:453
  221.2 4.9 %all-to-all-start.3 = ((bf16[16,1088,128]{2,1,0:T(8,128)(2,1)}), bf16[16,1088,128]{2,1,0:T(8,128)(2,1)}, u32[]{:S(2)}, u32[]{:S(2)}) async-start(bf16[16,1088,128]{2,1,0:T(8,128)(2,1)} %bitcast.9), calls=%async_computation.3 | async-start | bytes 8912896 | tf_op jit(solution)/shard_map/all_to_all | solution.py:453
  226.1 15.3 %legendre_solve.2 = bf16[16,34,32,128]{3,2,1,0:T(8,128)(2,1)} custom-call(s32[32]{0:T(128)} %dynamic_slice.3.waves_ref, bf16[16,34,32,128]{3,2,1,0:T(8,128)(2,1)} %bitcast.2.recv_ref, bf16[32,512,512]{2,1,0:T(8,128)(2,1)} %high_basis.3, bf16[32,512,512]{2,1,0:T(8,128)(2,1)} %high_basis.3, bf16[32,136,136]{2,1,0:T(8,128)(2,1)} %high_solver.3, ...), custom_call_target="tpu_custom_call" | custom-call | flops 3422552064 | bytes 15204352 | tf_op jit(solution)/shard_map/legendre_solve/pallas_call | solution.py:350
  241.4 82.8 %all-to-all-done.3 = bf16[16,1088,128]{2,1,0:T(8,128)(2,1)} async-done(((bf16[16,1088,128]{2,1,0:T(8,128)(2,1)}), bf16[16,1088,128]{2,1,0:T(8,128)(2,1)}, u32[]{:S(2)}, u32[]{:S(2)}) %all-to-all-start.3) | async-done | bytes 4456480 | tf_op jit(solution)/shard_map/all_to_all | solution.py:453
  324.2 4.9 %all-to-all-start.1 = ((bf16[16,1088,128]{2,1,0:T(8,128)(2,1)}), bf16[16,1088,128]{2,1,0:T(8,128)(2,1)}, u32[]{:S(2)}, u32[]{:S(2)}) async-start(bf16[16,1088,128]{2,1,0:T(8,128)(2,1)} %bitcast.10), calls=%async_computation.1 | async-start | bytes 8912896 | tf_op jit(solution)/shard_map/all_to_all | solution.py:453
  329.1 3.2 synthesis_rows.1.refs_2_
  332.3 94.9 %all-to-all-done.1 = bf16[16,1088,128]{2,1,0:T(8,128)(2,1)} async-done(((bf16[16,1088,128]{2,1,0:T(8,128)(2,1)}), bf16[16,1088,128]{2,1,0:T(8,128)(2,1)}, u32[]{:S(2)}, u32[]{:S(2)}) %all-to-all-start.1) | async-done | bytes 4456480 | tf_op jit(solution)/shard_map/all_to_all | solution.py:453
  427.2 11.7 %longitude_synthesis.1 = bf16[34,128,1024]{2,1,0:T(8,128)(2,1)} custom-call(bf16[16,34,32,128]{3,2,1,0:T(8,128)(2,1)} %bitcast.4.refs_0_, bf16[16,34,32,128]{3,2,1,0:T(8,128)(2,1)} %bitcast.8.refs_1_, bf16[2,2,256,512]{3,2,1,0:T(8,128)(2,1)} %synthesis_rows.1.refs_2_), custom_call_target="tpu_custom_call" | custom-call | flops 4563402752 | bytes 17825792 | tf_op jit(solution)/shard_map/longitude_synthesis/pallas_call | solution.py:429
Async XLA Ops:
  13.6 104.7 %all-to-all-start.2 = ((bf16[16,1088,128]{2,1,0:T(8,128)(2,1)}), bf16[16,1088,128]{2,1,0:T(8,128)(2,1)}, u32[]{:S(2)}, u32[]{:S(2)}) async-start(bf16[16,1088,128]{2,1,0:T(8,128)(2,1)} %bitcast.12), calls=%async_computation.2 | async-start | bytes 8912896 | tf_op jit(solution)/shard_map/all_to_all | solution.py:453
  118.2 103.0 %all-to-all-start = ((bf16[16,1088,128]{2,1,0:T(8,128)(2,1)}), bf16[16,1088,128]{2,1,0:T(8,128)(2,1)}, u32[]{:S(2)}, u32[]{:S(2)}) async-start(bf16[16,1088,128]{2,1,0:T(8,128)(2,1)} %bitcast.11), calls=%async_computation | async-start | bytes 8912896 | tf_op jit(solution)/shard_map/all_to_all | solution.py:453
  221.2 103.0 %all-to-all-start.3 = ((bf16[16,1088,128]{2,1,0:T(8,128)(2,1)}), bf16[16,1088,128]{2,1,0:T(8,128)(2,1)}, u32[]{:S(2)}, u32[]{:S(2)}) async-start(bf16[16,1088,128]{2,1,0:T(8,128)(2,1)} %bitcast.9), calls=%async_computation.3 | async-start | bytes 8912896 | tf_op jit(solution)/shard_map/all_to_all | solution.py:453
  324.2 103.0 %all-to-all-start.1 = ((bf16[16,1088,128]{2,1,0:T(8,128)(2,1)}), bf16[16,1088,128]{2,1,0:T(8,128)(2,1)}, u32[]{:S(2)}, u32[]{:S(2)}) async-start(bf16[16,1088,128]{2,1,0:T(8,128)(2,1)} %bitcast.10), calls=%async_computation.1 | async-start | bytes 8912896 | tf_op jit(solution)/shard_map/all_to_all | solution.py:453

commit v5 on v4

--- a/solution.py
+++ b/solution.py
@@ -11,6 +11,8 @@
 
 OWNERS = ("lat", "lev", "sub")
 CHUNKS = 2
+HINT = 33
+FEW = 4
 
 
 def raw_table(fourier_order_holder, lon_count):
@@ -96,13 +98,14 @@
     return table.astype(jnp.bfloat16)
 
 
-def wave_rows(owners, chunks, k, holder_ref, waves_ref, parity):
+def wave_rows(owners, chunks, k, holder_ref, waves_ref, parity, me=0):
     slots = holder_ref.shape[1]
     per_chunk = slots // 2 // owners // chunks
     wave = 2 * lax.broadcasted_iota(jnp.int32, (waves_ref.shape[2], slots), 0) + parity
     held = (holder_ref[...] == wave).astype(jnp.float32).astype(jnp.bfloat16)
     row = lax.broadcasted_iota(jnp.int32, (owners * per_chunk, slots), 0)
-    pair = (lax.div(row, per_chunk) * chunks + k) * per_chunk + lax.rem(row, per_chunk)
+    owner = lax.bitwise_xor(lax.div(row, per_chunk), me)
+    pair = (owner * chunks + k) * per_chunk + lax.rem(row, per_chunk)
     slot = lax.broadcasted_iota(jnp.int32, (owners * per_chunk, slots), 1)
     chosen = (lax.div(slot, 2) == pair).astype(jnp.float32).astype(jnp.bfloat16)
     pick = dot(chosen, held, NT)
@@ -116,15 +119,15 @@
 
 
 def analysis_kernel(
-    owners, chunks, k, holder_ref, waves_hbm, state_hbm, forcing_hbm, send_hbm,
-    waves, table, state, forcing, folded, send, ready, arrived, left,
+    owners, chunks, k, begin, apart, holder_ref, waves_hbm, state_hbm, forcing_hbm, *refs
 ):
+    send_hbm, waves, table, state, forcing, folded, send, ready, arrived, left = refs[-10:]
     steps, levels, lats, lon_count = state.shape
     half = lon_count // 2
     rows = send.shape[2]
 
     def copies(n):
-        span = pl.ds(n * levels, levels)
+        span = pl.ds(begin + n * levels, levels)
         return (
             pltpu.make_async_copy(state_hbm.at[span], state.at[n], arrived.at[n, 0]),
             pltpu.make_async_copy(forcing_hbm.at[span], forcing.at[n], arrived.at[n, 1]),
@@ -144,7 +147,8 @@
 
     fetch.wait()
     for parity in range(2):
-        found, _ = wave_rows(owners, chunks, k, holder_ref, waves, parity)
+        me = lax.axis_index(OWNERS) if apart else 0
+        found, _ = wave_rows(owners, chunks, k, holder_ref, waves, parity, me)
         table[parity] = found.astype(jnp.bfloat16)
 
     def take(n):
@@ -195,8 +199,10 @@
         leaving(n).wait()
 
 
-def run_analysis(owners, chunks, k, state, forcing, holder, table):
-    levels, lats, lon_count = state.shape
+def run_analysis(owners, chunks, k, piece, state, forcing, holder, table, before):
+    begin, end, apart = piece
+    _, lats, lon_count = state.shape
+    levels = end - begin
     slots = holder.shape[1]
     rows = 2 * slots // owners // chunks
     count = 2 if levels % 2 == 0 else 1
@@ -204,8 +210,8 @@
     kept = pltpu.VMEM((steps, count, lats, lon_count), jnp.bfloat16)
     anywhere = pl.BlockSpec(memory_space=pl.ANY)
     return pl.pallas_call(
-        functools.partial(analysis_kernel, owners, chunks, k),
-        in_specs=[pl.BlockSpec(memory_space=pltpu.VMEM)] + [anywhere] * 3,
+        functools.partial(analysis_kernel, owners, chunks, k, begin, apart),
+        in_specs=[pl.BlockSpec(memory_space=pltpu.VMEM)] + [anywhere] * (3 + len(before)),
         out_specs=anywhere,
         out_shape=jax.ShapeDtypeStruct((owners, levels, rows, lats), jnp.bfloat16),
         scratch_shapes=[
@@ -226,7 +232,7 @@
             transcendentals=0,
         ),
         name="longitude_analysis",
-    )(holder, table, state, forcing)
+    )(holder, table, state, forcing, *before)
 
 
 def synthesis_rows_kernel(owners, chunks, holder_ref, waves_ref, out_ref):
@@ -249,7 +255,7 @@
         out_shape=jax.ShapeDtypeStruct(shape, jnp.bfloat16),
         compiler_params=pltpu.CompilerParams(vmem_limit_bytes=VMEM_BYTES),
         cost_estimate=pl.CostEstimate(
-            flops=8 * holder.shape[1] * table.shape[2] * table.shape[3],
+            flops=8 * 200 * holder.shape[1] * table.shape[2] * table.shape[3],
             bytes_accessed=4 * holder.shape[1] * table.shape[3],
             transcendentals=0,
         ),
@@ -262,27 +268,37 @@
     return first + late, first + 1 - late
 
 
-def column_kernel(
-    bands, k, waves_ref, recv_ref, low_basis, high_basis, low_solver, high_solver, send_ref,
-    spread, back,
-):
-    owners, levels, rows, lats = recv_ref.shape
+def owner_blocks(owners, bands, levels, refs, pieces):
     groups = owners // bands
+    blocks = 0
+    for ref, (begin, end, apart) in zip(refs, pieces):
+        rows = ref.shape[2] + TILE
+        for r in range(ref.shape[0]):
+            place = (blocks + r) % owners
+            owner = lax.bitwise_xor(lax.axis_index(OWNERS), place) if apart else r
+            start = (lax.rem(owner, groups) * levels + begin) * rows
+            if apart:
+                start = pl.multiple_of(start, TILE)
+            yield ref.at[r], lax.div(owner, groups), pl.ds(start, (end - begin) * rows)
+        blocks += ref.shape[0]
+
+
+def column_kernel(owners, bands, k, pieces_in, pieces_out, waves_ref, *refs):
+    received, refs = refs[: len(pieces_in)], refs[len(pieces_in) :]
+    low_basis, high_basis, low_solver, high_solver = refs[:4]
+    sends, (spread, back) = refs[-2 - len(pieces_out) : -2], refs[-2:]
+    levels = pieces_in[-1][1]
+    rows, lats = received[0].shape[-2:]
     per_chunk = rows // 4
-    depth = groups * levels
+    depth = owners // bands * levels
     total = low_basis.shape[1]
     middle = total // 2
     i = pl.program_id(0)
 
-    def places():
-        size = levels * (rows + TILE)
-        for r in range(owners):
-            yield r, r // groups, slice(r % groups * size, (r % groups + 1) * size)
-
     @pl.when(i == 0)
     def _():
-        for r, band, span in places():
-            part = recv_ref[r].astype(jnp.float32)
+        for ref, band, span in owner_blocks(owners, bands, levels, received, pieces_in):
+            part = ref[...].astype(jnp.float32)
             part = jnp.concatenate([part, part[:, :TILE]], axis=1)
             spread[band, span, :] = part.reshape(-1, lats)
 
@@ -330,13 +346,14 @@
 
     @pl.when(i == pl.num_programs(0) - 1)
     def _():
-        for r, band, span in places():
-            part = back[band, span, :].reshape(levels, rows + TILE, lats)
-            send_ref[r] = part[:, :rows].astype(jnp.bfloat16)
-
-
-def run_columns(k, bands, waves, received, basis, solver):
-    owners, levels, rows, lats = received.shape
+        for ref, band, span in owner_blocks(owners, bands, levels, sends, pieces_out):
+            part = back[band, span, :].reshape(ref.shape[0], rows + TILE, lats)
+            ref[...] = part[:, :rows].astype(jnp.bfloat16)
+
+
+def run_columns(k, owners, bands, pieces_in, pieces_out, waves, received, before, basis, solver):
+    rows, lats = received[0].shape[-2:]
+    levels = pieces_in[-1][1]
     depth = owners // bands * levels
     total = basis.shape[1]
     middle = total // 2
@@ -345,58 +362,72 @@
     low = lambda i, waves_ref: (pair_slots(first(i), waves_ref, middle)[0], 0, 0)
     high = lambda i, waves_ref: (pair_slots(first(i), waves_ref, middle)[1], 0, 0)
     upper = lambda i, waves_ref: (pair_slots(first(i), waves_ref, middle)[1], 0, 1)
-    whole = pl.BlockSpec(received.shape, lambda i, waves_ref: (0, 0, 0, 0))
+    whole = lambda shape: pl.BlockSpec(shape, lambda i, waves_ref: (0, 0, 0, 0))
+    sizes = [(owners, end - begin, rows, lats) for begin, end, _ in pieces_out]
     scratch = pltpu.VMEM((bands, depth * (rows + TILE), lats), jnp.float32)
     return pl.pallas_call(
-        functools.partial(column_kernel, bands, k),
+        functools.partial(column_kernel, owners, bands, k, pieces_in, pieces_out),
         grid_spec=pltpu.PrefetchScalarGridSpec(
             num_scalar_prefetch=1,
             grid=(steps,),
-            in_specs=[
-                whole,
+            in_specs=[whole(part.shape) for part in received]
+            + [
                 pl.BlockSpec((1, total, total), low),
                 pl.BlockSpec((1, total, total - middle), upper),
                 pl.BlockSpec((1, depth, depth), low),
                 pl.BlockSpec((1, depth, depth), high),
-            ],
-            out_specs=whole,
+            ]
+            + [pl.BlockSpec(memory_space=pl.ANY)] * len(before),
+            out_specs=[whole(size) for size in sizes],
             scratch_shapes=[scratch, scratch],
         ),
-        out_shape=jax.ShapeDtypeStruct(received.shape, jnp.bfloat16),
+        out_shape=[jax.ShapeDtypeStruct(size, jnp.bfloat16) for size in sizes],
         compiler_params=pltpu.CompilerParams(vmem_limit_bytes=VMEM_BYTES),
         cost_estimate=pl.CostEstimate(
-            flops=6 * steps * 2 * depth * total * total,
-            bytes_accessed=4 * received.size + 3 * steps * total * total,
+            flops=HINT * 6 * steps * 2 * depth * total * total,
+            bytes_accessed=4 * bands * depth * rows * lats + 3 * steps * total * total,
             transcendentals=0,
         ),
         name="legendre_solve",
-    )(waves, received, basis, basis, solver, solver)
-
-
-def synthesis_kernel(chunks, *refs):
-    parts, (synth_ref, out_hbm, kept, out, arrived, left) = refs[:chunks], refs[chunks:]
-    steps, _, owners, levels, rows, lats = kept.shape
+    )(waves, *received, basis, basis, solver, solver, *before)
+
+
+def synthesis_kernel(owners, pieces, *refs):
+    taking = sum(len(some) for some in pieces)
+    parts, (synth_ref, out_hbm, kept, out, arrived, left) = refs[:taking], refs[taking:]
+    steps, chunks, _, levels, rows, lats = kept.shape
     half = synth_ref.shape[-1]
-
-    def copies(n):
-        span = pl.ds(n * levels, levels)
-        return [
-            pltpu.make_async_copy(part.at[:, span], kept.at[n, k], arrived.at[n, k])
-            for k, part in enumerate(parts)
-        ]
+    me = lax.axis_index(OWNERS)
+    cuts = sorted({end // levels for some in pieces for _, end, _ in some})
+
+    def copies(n, first, entire):
+        left = parts
+        for k, some in enumerate(pieces):
+            for part, (begin, end, apart) in zip(left, some):
+                if not begin <= first * levels < end:
+                    continue
+                span = pl.ds(n * levels - begin, levels)
+                if apart and not entire:
+                    for r in range(owners):
+                        place = kept.at[n, k, lax.bitwise_xor(me, r)]
+                        yield pltpu.make_async_copy(part.at[r, span], place, arrived.at[n, k])
+                else:
+                    yield pltpu.make_async_copy(part.at[:, span], kept.at[n, k], arrived.at[n, k])
+            left = left[len(some) :]
 
     def leaving(n):
         span = pl.ds(n * levels, levels)
         return pltpu.make_async_copy(out.at[span], out_hbm.at[span], left.at[n])
 
-    @pl.loop(0, steps)
-    def _(n):
-        for copy in copies(n):
-            copy.start()
-
-    @pl.loop(0, steps)
-    def _(i):
-        for copy in copies(i):
+    for first, last in zip([0] + cuts, cuts):
+
+        @pl.loop(first, last)
+        def _(n, first=first):
+            for copy in copies(n, first, False):
+                copy.start()
+
+    def step(i, first):
+        for copy in copies(i, first, True):
             copy.wait()
         sums = []
         for parity in range(2):
@@ -414,21 +445,25 @@
             out[i * levels + n, :, half:] = (even - odd).astype(jnp.bfloat16)
         leaving(i).start()
 
+    for first, last in zip([0] + cuts, cuts):
+        pl.loop(first, last)(functools.partial(step, first=first))
+
     @pl.loop(0, steps)
     def _(n):
         leaving(n).wait()
 
 
-def run_synthesis(parts, synth):
-    owners, levels, rows, lats = parts[0].shape
+def run_synthesis(pieces, parts, synth):
+    owners, _, rows, lats = parts[0].shape
+    levels = pieces[0][-1][1]
     lon_count = 2 * synth.shape[-1]
-    chunks = len(parts)
+    chunks = len(pieces)
     count = 2 if levels % 2 == 0 else 1
     steps = levels // count
     anywhere = pl.BlockSpec(memory_space=pl.ANY)
     return pl.pallas_call(
-        functools.partial(synthesis_kernel, chunks),
-        in_specs=[anywhere] * chunks + [pl.BlockSpec(memory_space=pltpu.VMEM)],
+        functools.partial(synthesis_kernel, owners, pieces),
+        in_specs=[anywhere] * len(parts) + [pl.BlockSpec(memory_space=pltpu.VMEM)],
         out_specs=anywhere,
         out_shape=jax.ShapeDtypeStruct((levels, lats, lon_count), jnp.bfloat16),
         scratch_shapes=[
@@ -453,8 +488,18 @@
     return lax.all_to_all(flat, OWNERS, 0, 0, tiled=True).reshape(part.shape)
 
 
+def swap(part, bits):
+    owners = part.shape[0]
+    for bit in bits:
+        halves = part.reshape((owners // 2 // bit, 2, bit) + part.shape[1:])
+        given = lax.ppermute(halves[:, 1], OWNERS, [(o, o ^ bit) for o in range(owners)])
+        part = jnp.stack([halves[:, 0], given], axis=1).reshape(part.shape)
+    return halves[0, 0], given[0]
+
+
 def chunked_shards(lat_bands, level_groups, chunks):
     owners = lat_bands * level_groups
+    far, near = owners // 2, [2**n for n in range(int(math.log2(owners)) - 1)]
 
     def shards(
         thermal_state_grid,
@@ -463,30 +508,45 @@
         implicit_solver_matrix,
         fourier_order_holder,
     ):
+        levels = thermal_state_grid.shape[0]
         slots = spherical_basis_table.shape[0]
         table = jnp.asarray(longitude_waves(thermal_state_grid.shape[2]))
         holder = fourier_order_holder.reshape(1, -1)
-        sends = [
-            run_analysis(owners, chunks, k, thermal_state_grid, thermal_forcing, holder, table)
-            for k in range(chunks)
-        ]
-        synth = synthesis_rows(owners, chunks, holder, table)
         owner = lax.axis_index(OWNERS)
         waves = lax.dynamic_slice_in_dim(fourier_order_holder, owner * slots, slots)
-        received = [exchange(part) for part in sends]
-        solved = [
-            run_columns(
-                k,
-                lat_bands,
-                waves,
-                received[k],
-                spherical_basis_table,
-                implicit_solver_matrix,
+
+        def analyse(k, piece, before):
+            return run_analysis(
+                owners, chunks, k, piece, thermal_state_grid, thermal_forcing, holder, table, before
             )
-            for k in range(chunks)
-        ]
-        returned = [exchange(part) for part in solved]
-        return run_synthesis(returned, synth)
+
+        def columns(k, pieces_in, pieces_out, received, before):
+            return run_columns(
+                k, owners, lat_bands, pieces_in, pieces_out, waves, received, before,
+                spherical_basis_table, implicit_solver_matrix,
+            )
+
+        whole = [(0, levels, False)]
+        few = levels * FEW // 34 // 2 * 2
+        cut, last = levels - 2 * few, levels - few
+        first = exchange(analyse(0, whole[0], []))
+        main = analyse(1, (0, cut, False), [])
+        rest = analyse(1, (cut, levels, True), [main])
+        early, late = rest[:, :few], rest[:, few:]
+        early = swap(early, near + [far])
+        second = exchange(main)
+        pieces = [(0, last, False), (last, levels, True)]
+        solved, aside = columns(0, whole, pieces, [first], early[1:])
+        solved, late = lax.optimization_barrier((solved, late))
+        late = swap(late, near + [far])
+        first = exchange(solved)
+        split = [(0, cut, False)] + [(cut, last, True)] * 2 + [(last, levels, True)] * 2
+        (solved,) = columns(1, split, whole, [second, *early, *late], [])
+        solved, aside = lax.optimization_barrier((solved, aside))
+        aside = jnp.concatenate(swap(aside, near + [far]))
+        second = exchange(solved)
+        synth = synthesis_rows(owners, chunks, holder, table)
+        return run_synthesis([pieces, whole], [first, aside, second], synth)
 
     return shards
 
@@ -499,7 +559,8 @@
         levels, lats, lon_count = state.shape
         pairs = basis.shape[0] // 2
         tiled = pairs % (CHUNKS * TILE) == 0 and levels * groups % TILE == 0
-        if tiled and lats % 128 == 0 and lon_count == 2 * holder.shape[0]:
+        tiled = tiled and bands > 1 and bands * groups == 2 ** int(math.log2(bands * groups))
+        if tiled and levels % 2 == 0 and lats % 128 == 0 and lon_count == 2 * holder.shape[0]:
             body = chunked_shards(bands, groups, CHUNKS)
         else:
             body = general_shards(bands, groups)

time: 440 us -> 424 us (0.964)
  waiting for transfers between devices: 344 us -> 305 us
  starting transfers between devices: 21.3 us -> 34.6 us
    all_to_all x4, waiting for transfers between devices: 344 us -> 155 us  [exchange(): return lax.all_to_all(flat, OWNERS, 0, 0, tiled=True).reshape(part.shape)]
    ppermute x0 -> x12, waiting for transfers between devices: none -> 150 us  [swap(): lax.ppermute(halves[:, 1], OWNERS, [(o, o ^ bit) for o in range(owners)])]
    ppermute x0 -> x12, starting transfers between devices: none -> 13.5 us  [swap(): lax.ppermute(halves[:, 1], OWNERS, [(o, o ^ bit) for o in range(owners)])]
    pallas_call x5 -> x6, Pallas kernels: 69.4 us -> 73.4 us  [the longest x2 30.9 us: run_columns(): pl.pallas_call(functools.partial(column_kernel, owners, bands, k, pieces_...]
  transfers between devices with their start and end apart: 4 -> 16, of which waited for: 4 -> 13; matrix products, arithmetic and copies ran while one was open for 0% -> 2% of each run, Pallas kernels for 11% -> 12%
where the time goes in v5:
time: 424 us; the launch traced here: 423 us
  waiting for transfers between devices  305 us (72%)
  Pallas kernels  76.5 us (18%)
  starting transfers between devices  34.6 us (8%)
  local copies, waits for them, and re-layouts  5.54 us (1%)
    all_to_all x4, waiting for transfers between devices, exchange(): return lax.all_to_all(flat, OWNERS, 0, 0, tiled=True).reshape(part.shape)  155 us
    ppermute x12, waiting for transfers between devices, swap(): lax.ppermute(halves[:, 1], OWNERS, [(o, o ^ bit) for o in range(owners)])  150 us
    pallas_call x2, Pallas kernels, run_columns(): pl.pallas_call(functools.partial(column_kernel, owners, bands, k, pieces_...  30.9 us
    pallas_call x3, Pallas kernels, run_analysis(): pl.pallas_call(functools.partial(analysis_kernel, owners, chunks, k, begi...  30.8 us
    all_to_all x4, starting transfers between devices, exchange(): return lax.all_to_all(flat, OWNERS, 0, 0, tiled=True).reshape(part.shape)  21 us
    ppermute x12, starting transfers between devices, swap(): lax.ppermute(halves[:, 1], OWNERS, [(o, o ^ bit) for o in range(owners)])  13.5 us
    pallas_call x1, Pallas kernels, run_synthesis(): pl.pallas_call(functools.partial(synthesis_kernel, owners, pieces), in_sp...  11.7 us
  transfers between devices with their start and end apart: 16, of which 13 were waited for; matrix products, arithmetic and copies ran while one was open for 2% of the time, Pallas kernels for 12%

profile of v5, /device:TPU:11, one launch (start us, length us, event | category | flops | bytes accessed | tf_op | source)
XLA Modules:
  0.0 423.3 jit_solution(9374866413020867992)
XLA Ops:
  0.0 13.6 %longitude_analysis.3 = bf16[16,34,32,128]{3,2,1,0:T(8,128)(2,1)} custom-call(s32[1,512]{1,0:T(1,128)} %bitcast.113, bf16[2,2,256,512]{3,2,1,0:T(8,128)(2,1)} %constant.23.clone.waves_hbm.waves_ref, bf16[34,128,1024]{2,1,0:T(8,128)(2,1)} %state_hbm.5, bf16[34,128,1024]{2,1,0:T(8,128)(2,1)} %forcing_hbm.5), custom_call_target="tpu_custom_call" | custom-call | flops 2281701376 | bytes 26738688 | tf_op jit(solution)/shard_map/longitude_analysis/pallas_call | solution.py:212
  13.6 6.6 %all-to-all-start = ((bf16[16,1088,128]{2,1,0:T(8,128)(2,1)}), bf16[16,1088,128]{2,1,0:T(8,128)(2,1)}, u32[]{:S(2)}, u32[]{:S(2)}) async-start(bf16[16,1088,128]{2,1,0:T(8,128)(2,1)} %bitcast.84), calls=%async_computation | async-start | bytes 8912896 | tf_op jit(solution)/shard_map/all_to_all | solution.py:488
  20.1 11.2 %longitude_analysis.4.refs_0_ = bf16[16,26,32,128]{3,2,1,0:T(8,128)(2,1)} custom-call(s32[1,512]{1,0:T(1,128)} %bitcast.114, bf16[2,2,256,512]{3,2,1,0:T(8,128)(2,1)} %constant.23.clone.waves_hbm.waves_ref, bf16[34,128,1024]{2,1,0:T(8,128)(2,1)} %state_hbm.5, bf16[34,128,1024]{2,1,0:T(8,128)(2,1)} %forcing_hbm.5), custom_call_target="tpu_custom_call" | custom-call | flops 1744830464 | bytes 20447232 | tf_op jit(solution)/shard_map/longitude_analysis/pallas_call | solution.py:212
  31.3 6.0 %longitude_analysis.5 = bf16[16,8,32,128]{3,2,1,0:T(8,128)(2,1)} custom-call(s32[1,512]{1,0:T(1,128)} %bitcast.115, bf16[2,2,256,512]{3,2,1,0:T(8,128)(2,1)} %constant.23.clone.waves_hbm.waves_ref, bf16[34,128,1024]{2,1,0:T(8,128)(2,1)} %state_hbm.5, bf16[34,128,1024]{2,1,0:T(8,128)(2,1)} %forcing_hbm.5, bf16[16,26,32,128]{3,2,1,0:T(8,128)(2,1)} %longitude_analysis.4.refs_0_), custom_call_target="tpu_custom_call" | custom-call | flops 536870912 | bytes 6291456 | tf_op jit(solution)/shard_map/longitude_analysis/pallas_call | solution.py:212
  37.4 2.1 fusion.9
  39.5 0.4 collective-permute-start
  39.9 1.2 collective-permute-done
  41.2 0.3 collective-permute-start.1
  41.5 11.8 %collective-permute-done.1 = bf16[4,2,4,32,128]{4,3,2,0,1:T(8,128)(2,1)S(1)} collective-permute-done((bf16[4,2,4,32,128]{4,3,2,0,1:T(8,128)(2,1)S(1)}, bf16[4,2,4,32,128]{4,3,2,0,1:T(8,128)(2,1)S(1)}, u32[]{:S(2)}, u32[]{:S(2)}) %collective-permute-start.1) | collective-permute-done | bytes 262176 | tf_op jit(solution)/shard_map/ppermute | solution.py:495
  53.3 0.1 pad_maximum_fusion
  53.4 0.4 collective-permute-start.2
  53.8 46.0 %collective-permute-done.2 = bf16[2,4,4,32,128]{4,3,2,1,0:T(8,128)(2,1)S(1)} collective-permute-done((bf16[2,4,4,32,128]{4,3,2,1,0:T(8,128)(2,1)S(1)}, bf16[2,4,4,32,128]{4,3,2,1,0:T(8,128)(2,1)S(1)}, u32[]{:S(2)}, u32[]{:S(2)}) %collective-permute-start.2) | collective-permute-done | bytes 262176 | tf_op jit(solution)/shard_map/ppermute | solution.py:495
  99.9 0.8 slice_bitcast_fusion.8
  100.7 0.3 collective-permute-start.3
  101.0 1.3 dynamic_slice.3.waves_ref
  102.3 22.1 %all-to-all-done = bf16[16,1088,128]{2,1,0:T(8,128)(2,1)} async-done(((bf16[16,1088,128]{2,1,0:T(8,128)(2,1)}), bf16[16,1088,128]{2,1,0:T(8,128)(2,1)}, u32[]{:S(2)}, u32[]{:S(2)}) %all-to-all-start) | async-done | bytes 4456480 | tf_op jit(solution)/shard_map/all_to_all | solution.py:488
  124.3 4.8 %all-to-all-start.2 = ((bf16[16,832,128]{2,1,0:T(8,128)(2,1)}), bf16[16,832,128]{2,1,0:T(8,128)(2,1)S(1)}, u32[]{:S(2)}, u32[]{:S(2)}) async-start(bf16[16,832,128]{2,1,0:T(8,128)(2,1)} %bitcast.18), calls=%async_computation.2 | async-start | bytes 6815744 | tf_op jit(solution)/shard_map/all_to_all | solution.py:488
  129.1 0.0 collective-permute-done.3
  129.1 15.4 %legendre_solve.2 = (bf16[16,30,32,128]{3,2,1,0:T(8,128)(2,1)}, bf16[16,4,32,128]{3,2,1,0:T(8,128)(2,1)}) custom-call(s32[32]{0:T(128)} %dynamic_slice.3.waves_ref, bf16[16,34,32,128]{3,2,1,0:T(8,128)(2,1)} %bitcast.2.refs_0_, bf16[32,512,512]{2,1,0:T(8,128)(2,1)} %refs_6_.1, bf16[32,512,512]{2,1,0:T(8,128)(2,1)} %refs_6_.1, bf16[32,136,136]{2,1,0:T(8,128)(2,1)} %refs_8_.1, ...), custom_call_target="tpu_custom_call" | custom-call | flops 112944218112 | bytes 15204352 | tf_op jit(solution)/shard_map/legendre_solve/pallas_call | solution.py:368
  144.6 0.4 collective-permute-start.4
  145.0 1.2 collective-permute-done.4
  146.3 0.3 collective-permute-start.5
  146.6 10.0 %collective-permute-done.5 = bf16[4,2,4,32,128]{4,3,2,0,1:T(8,128)(2,1)S(1)} collective-permute-done((bf16[4,2,4,32,128]{4,3,2,0,1:T(8,128)(2,1)S(1)}, bf16[4,2,4,32,128]{4,3,2,0,1:T(8,128)(2,1)S(1)}, u32[]{:S(2)}, u32[]{:S(2)}) %collective-permute-start.5) | collective-permute-done | bytes 262176 | tf_op jit(solution)/shard_map/ppermute | solution.py:495
  156.7 0.1 pad_maximum_fusion.2
  156.8 4.7 %collective-permute-start.6 = (bf16[2,4,4,32,128]{4,3,2,1,0:T(8,128)(2,1)S(1)}, bf16[2,4,4,32,128]{4,3,2,1,0:T(8,128)(2,1)S(1)}, u32[]{:S(2)}, u32[]{:S(2)}) collective-permute-start(bf16[2,4,4,32,128]{4,3,2,1,0:T(8,128)(2,1)S(1)} %slice_bitcast_fusion.6), channel_id=1, source_target_pairs={{0,4},{1,5},{2,6},{3,7},{4,0},{5,1},{6,2},{7,3},{8,12},{9,13},{10,... | collective-permute-start | bytes 786440 | tf_op jit(solution)/shard_map/ppermute | solution.py:495
  161.5 30.4 %collective-permute-done.6 = bf16[2,4,4,32,128]{4,3,2,1,0:T(8,128)(2,1)S(1)} collective-permute-done((bf16[2,4,4,32,128]{4,3,2,1,0:T(8,128)(2,1)S(1)}, bf16[2,4,4,32,128]{4,3,2,1,0:T(8,128)(2,1)S(1)}, u32[]{:S(2)}, u32[]{:S(2)}) %collective-permute-start.6) | collective-permute-done | bytes 262176 | tf_op jit(solution)/shard_map/ppermute | solution.py:495
  192.0 0.8 slice_bitcast_fusion.4
  192.8 0.2 collective-permute-start.7
  193.1 17.7 %all-to-all-done.2 = bf16[16,832,128]{2,1,0:T(8,128)(2,1)S(1)} async-done(((bf16[16,832,128]{2,1,0:T(8,128)(2,1)}), bf16[16,832,128]{2,1,0:T(8,128)(2,1)S(1)}, u32[]{:S(2)}, u32[]{:S(2)}) %all-to-all-start.2) | async-done | bytes 3407904 | tf_op jit(solution)/shard_map/all_to_all | solution.py:488
  210.8 4.8 %all-to-all-start.1 = ((bf16[16,960,128]{2,1,0:T(8,128)(2,1)}), bf16[16,960,128]{2,1,0:T(8,128)(2,1)}, u32[]{:S(2)}, u32[]{:S(2)}) async-start(bf16[16,960,128]{2,1,0:T(8,128)(2,1)} %bitcast.86), calls=%async_computation.1 | async-start | bytes 7864320 | tf_op jit(solution)/shard_map/all_to_all | solution.py:488
  215.6 0.0 collective-permute-done.7
  215.6 0.0 copy-done
  215.6 15.5 %legendre_solve.3 = bf16[16,34,32,128]{3,2,1,0:T(8,128)(2,1)} custom-call(s32[32]{0:T(128)} %dynamic_slice.3.waves_ref, bf16[16,26,32,128]{3,2,1,0:T(8,128)(2,1)} %bitcast.87, bf16[8,4,32,128]{3,2,1,0:T(8,128)(2,1)} %get-tuple-element.31.refs_1_, bf16[8,4,32,128]{3,2,1,0:T(8,128)(2,1)} %bitcast.15.refs_5_.refs_2_, ...), custom_call_target="tpu_custom_call" | custom-call | flops 112944218112 | bytes 15204352 | tf_op jit(solution)/shard_map/legendre_solve/pallas_call | solution.py:368
  231.2 0.4 collective-permute-start.8
  231.6 1.2 collective-permute-done.8
  232.8 0.3 collective-permute-start.9
  233.1 12.7 %collective-permute-done.9 = bf16[4,2,4,32,128]{4,3,2,0,1:T(8,128)(2,1)S(1)} collective-permute-done((bf16[4,2,4,32,128]{4,3,2,0,1:T(8,128)(2,1)S(1)}, bf16[4,2,4,32,128]{4,3,2,0,1:T(8,128)(2,1)S(1)}, u32[]{:S(2)}, u32[]{:S(2)}) %collective-permute-start.9) | collective-permute-done | bytes 262176 | tf_op jit(solution)/shard_map/ppermute | solution.py:495
  245.9 0.1 pad_maximum_fusion.4
  246.0 5.4 %collective-permute-start.10 = (bf16[2,4,4,32,128]{4,3,2,1,0:T(8,128)(2,1)S(1)}, bf16[2,4,4,32,128]{4,3,2,1,0:T(8,128)(2,1)S(1)}, u32[]{:S(2)}, u32[]{:S(2)}) collective-permute-start(bf16[2,4,4,32,128]{4,3,2,1,0:T(8,128)(2,1)S(1)} %slice_bitcast_fusion.2), channel_id=1, source_target_pairs={{0,4},{1,5},{2,6},{3,7},{4,0},{5,1},{6,2},{7,3},{8,12},{9,13},{10,... | collective-permute-start | bytes 786440 | tf_op jit(solution)/shard_map/ppermute | solution.py:495
  251.4 35.4 %collective-permute-done.10 = bf16[2,4,4,32,128]{4,3,2,1,0:T(8,128)(2,1)S(1)} collective-permute-done((bf16[2,4,4,32,128]{4,3,2,1,0:T(8,128)(2,1)S(1)}, bf16[2,4,4,32,128]{4,3,2,1,0:T(8,128)(2,1)S(1)}, u32[]{:S(2)}, u32[]{:S(2)}) %collective-permute-start.10) | collective-permute-done | bytes 262176 | tf_op jit(solution)/shard_map/ppermute | solution.py:495
  286.9 0.3 collective-permute-start.11
  287.2 21.3 %all-to-all-done.1 = bf16[16,960,128]{2,1,0:T(8,128)(2,1)} async-done(((bf16[16,960,128]{2,1,0:T(8,128)(2,1)}), bf16[16,960,128]{2,1,0:T(8,128)(2,1)}, u32[]{:S(2)}, u32[]{:S(2)}) %all-to-all-start.1) | async-done | bytes 3932192 | tf_op jit(solution)/shard_map/all_to_all | solution.py:488
  308.6 4.9 %all-to-all-start.3 = ((bf16[16,1088,128]{2,1,0:T(8,128)(2,1)}), bf16[16,1088,128]{2,1,0:T(8,128)(2,1)}, u32[]{:S(2)}, u32[]{:S(2)}) async-start(bf16[16,1088,128]{2,1,0:T(8,128)(2,1)} %bitcast.85), calls=%async_computation.3 | async-start | bytes 8912896 | tf_op jit(solution)/shard_map/all_to_all | solution.py:488
  313.4 3.2 synthesis_rows.1.refs_3_
  316.6 0.0 collective-permute-done.11
  316.6 0.9 pad_maximum_fusion.6.refs_1_
  317.5 94.0 %all-to-all-done.3 = bf16[16,1088,128]{2,1,0:T(8,128)(2,1)} async-done(((bf16[16,1088,128]{2,1,0:T(8,128)(2,1)}), bf16[16,1088,128]{2,1,0:T(8,128)(2,1)}, u32[]{:S(2)}, u32[]{:S(2)}) %all-to-all-start.3) | async-done | bytes 4456480 | tf_op jit(solution)/shard_map/all_to_all | solution.py:488
  411.5 11.7 %longitude_synthesis.1 = bf16[34,128,1024]{2,1,0:T(8,128)(2,1)} custom-call(bf16[16,30,32,128]{3,2,1,0:T(8,128)(2,1)} %bitcast.17.refs_0_, bf16[16,4,32,128]{3,2,1,0:T(8,128)(2,1)} %pad_maximum_fusion.6.refs_1_, bf16[16,34,32,128]{3,2,1,0:T(8,128)(2,1)} %bitcast.50.refs_2_, bf16[2,2,256,512]{3,2,1,0:T(8,128)(2,1)} %synthesis_rows.1.refs_3_), custom_call_target="tpu_custom_call" | custom-call | flops 4563402752 | bytes 17825792 | tf_op jit(solution)/shard_map/longitude_synthesis/pallas_call | solution.py:464
  (24 shorter events, 0.7 us)
Async XLA Ops:
  13.6 110.8 %all-to-all-start = ((bf16[16,1088,128]{2,1,0:T(8,128)(2,1)}), bf16[16,1088,128]{2,1,0:T(8,128)(2,1)}, u32[]{:S(2)}, u32[]{:S(2)}) async-start(bf16[16,1088,128]{2,1,0:T(8,128)(2,1)} %bitcast.84), calls=%async_computation | async-start | bytes 8912896 | tf_op jit(solution)/shard_map/all_to_all | solution.py:488
  39.5 1.6 collective-permute-start
  41.2 12.1 %collective-permute-start.1 = (bf16[4,2,4,32,128]{4,3,2,0,1:T(8,128)(2,1)S(1)}, bf16[4,2,4,32,128]{4,3,2,0,1:T(8,128)(2,1)S(1)}, u32[]{:S(2)}, u32[]{:S(2)}) collective-permute-start(bf16[4,2,4,32,128]{4,3,2,0,1:T(8,128)(2,1)S(1)} %get-tuple-element.34), channel_id=1, source_target_pairs={{0,2},{1,3},{2,0},{3,1},{4,6},{5,7},{6,4},{7,5},{8,10},{9,11},{10,... | collective-permute-start | bytes 786440 | tf_op jit(solution)/shard_map/ppermute | solution.py:495
  53.4 46.3 %collective-permute-start.2 = (bf16[2,4,4,32,128]{4,3,2,1,0:T(8,128)(2,1)S(1)}, bf16[2,4,4,32,128]{4,3,2,1,0:T(8,128)(2,1)S(1)}, u32[]{:S(2)}, u32[]{:S(2)}) collective-permute-start(bf16[2,4,4,32,128]{4,3,2,1,0:T(8,128)(2,1)S(1)} %slice_bitcast_fusion.10), channel_id=1, source_target_pairs={{0,4},{1,5},{2,6},{3,7},{4,0},{5,1},{6,2},{7,3},{8,12},{9,13},{10,... | collective-permute-start | bytes 786440 | tf_op jit(solution)/shard_map/ppermute | solution.py:495
  100.7 28.4 %collective-permute-start.3 = (bf16[1,8,4,32,128]{4,3,2,1,0:T(8,128)(2,1)}, bf16[1,8,4,32,128]{4,3,2,1,0:T(8,128)(2,1)}, u32[]{:S(2)}, u32[]{:S(2)}) collective-permute-start(bf16[1,8,4,32,128]{4,3,2,1,0:T(8,128)(2,1)} %get-tuple-element.32), channel_id=1, source_target_pairs={{0,8},{1,9},{2,10},{3,11},{4,12},{5,13},{6,14},{7,15},{8,0},{9,1},... | collective-permute-start | bytes 786440 | tf_op jit(solution)/shard_map/ppermute | solution.py:495
  124.3 86.4 %all-to-all-start.2 = ((bf16[16,832,128]{2,1,0:T(8,128)(2,1)}), bf16[16,832,128]{2,1,0:T(8,128)(2,1)S(1)}, u32[]{:S(2)}, u32[]{:S(2)}) async-start(bf16[16,832,128]{2,1,0:T(8,128)(2,1)} %bitcast.18), calls=%async_computation.2 | async-start | bytes 6815744 | tf_op jit(solution)/shard_map/all_to_all | solution.py:488
  129.1 15.4 %copy-start.1 = (bf16[16,4,32,128]{3,2,1,0:T(8,128)(2,1)S(1)}, bf16[16,4,32,128]{3,2,1,0:T(8,128)(2,1)}, u32[]{:S(2)}) copy-start(bf16[16,4,32,128]{3,2,1,0:T(8,128)(2,1)} %get-tuple-element.13) | copy-start | bytes 1572868
  144.6 1.6 collective-permute-start.4
  146.3 10.4 %collective-permute-start.5 = (bf16[4,2,4,32,128]{4,3,2,0,1:T(8,128)(2,1)S(1)}, bf16[4,2,4,32,128]{4,3,2,0,1:T(8,128)(2,1)S(1)}, u32[]{:S(2)}, u32[]{:S(2)}) collective-permute-start(bf16[4,2,4,32,128]{4,3,2,0,1:T(8,128)(2,1)S(1)} %get-tuple-element.28), channel_id=1, source_target_pairs={{0,2},{1,3},{2,0},{3,1},{4,6},{5,7},{6,4},{7,5},{8,10},{9,11},{10,... | collective-permute-start | bytes 786440 | tf_op jit(solution)/shard_map/ppermute | solution.py:495
  156.8 35.1 %collective-permute-start.6 = (bf16[2,4,4,32,128]{4,3,2,1,0:T(8,128)(2,1)S(1)}, bf16[2,4,4,32,128]{4,3,2,1,0:T(8,128)(2,1)S(1)}, u32[]{:S(2)}, u32[]{:S(2)}) collective-permute-start(bf16[2,4,4,32,128]{4,3,2,1,0:T(8,128)(2,1)S(1)} %slice_bitcast_fusion.6), channel_id=1, source_target_pairs={{0,4},{1,5},{2,6},{3,7},{4,0},{5,1},{6,2},{7,3},{8,12},{9,13},{10,... | collective-permute-start | bytes 786440 | tf_op jit(solution)/shard_map/ppermute | solution.py:495
  192.8 22.8 %collective-permute-start.7 = (bf16[1,8,4,32,128]{4,3,2,1,0:T(8,128)(2,1)}, bf16[1,8,4,32,128]{4,3,2,1,0:T(8,128)(2,1)}, u32[]{:S(2)}, u32[]{:S(2)}) collective-permute-start(bf16[1,8,4,32,128]{4,3,2,1,0:T(8,128)(2,1)} %get-tuple-element.25), channel_id=1, source_target_pairs={{0,8},{1,9},{2,10},{3,11},{4,12},{5,13},{6,14},{7,15},{8,0},{9,1},... | collective-permute-start | bytes 786440 | tf_op jit(solution)/shard_map/ppermute | solution.py:495
  210.8 4.8 %copy-start = (bf16[16,832,128]{2,1,0:T(8,128)(2,1)}, bf16[16,832,128]{2,1,0:T(8,128)(2,1)S(1)}, u32[]{:S(2)}) copy-start(bf16[16,832,128]{2,1,0:T(8,128)(2,1)S(1)} %all-to-all-done.2) | copy-start | bytes 10223620
  210.8 97.8 %all-to-all-start.1 = ((bf16[16,960,128]{2,1,0:T(8,128)(2,1)}), bf16[16,960,128]{2,1,0:T(8,128)(2,1)}, u32[]{:S(2)}, u32[]{:S(2)}) async-start(bf16[16,960,128]{2,1,0:T(8,128)(2,1)} %bitcast.86), calls=%async_computation.1 | async-start | bytes 7864320 | tf_op jit(solution)/shard_map/all_to_all | solution.py:488
  215.6 15.5 %copy-start.2 = (bf16[16,4,32,128]{3,2,1,0:T(8,128)(2,1)S(1)}, bf16[16,4,32,128]{3,2,1,0:T(8,128)(2,1)}, u32[]{:S(2)}) copy-start(bf16[16,4,32,128]{3,2,1,0:T(8,128)(2,1)} %get-tuple-element.15) | copy-start | bytes 1572868
  231.2 1.6 collective-permute-start.8
  232.8 13.1 %collective-permute-start.9 = (bf16[4,2,4,32,128]{4,3,2,0,1:T(8,128)(2,1)S(1)}, bf16[4,2,4,32,128]{4,3,2,0,1:T(8,128)(2,1)S(1)}, u32[]{:S(2)}, u32[]{:S(2)}) collective-permute-start(bf16[4,2,4,32,128]{4,3,2,0,1:T(8,128)(2,1)S(1)} %get-tuple-element.22), channel_id=1, source_target_pairs={{0,2},{1,3},{2,0},{3,1},{4,6},{5,7},{6,4},{7,5},{8,10},{9,11},{10,... | collective-permute-start | bytes 786440 | tf_op jit(solution)/shard_map/ppermute | solution.py:495
  246.0 40.8 %collective-permute-start.10 = (bf16[2,4,4,32,128]{4,3,2,1,0:T(8,128)(2,1)S(1)}, bf16[2,4,4,32,128]{4,3,2,1,0:T(8,128)(2,1)S(1)}, u32[]{:S(2)}, u32[]{:S(2)}) collective-permute-start(bf16[2,4,4,32,128]{4,3,2,1,0:T(8,128)(2,1)S(1)} %slice_bitcast_fusion.2), channel_id=1, source_target_pairs={{0,4},{1,5},{2,6},{3,7},{4,0},{5,1},{6,2},{7,3},{8,12},{9,13},{10,... | collective-permute-start | bytes 786440 | tf_op jit(solution)/shard_map/ppermute | solution.py:495
  286.9 29.7 %collective-permute-start.11 = (bf16[1,8,4,32,128]{4,3,2,1,0:T(8,128)(2,1)S(1)}, bf16[1,8,4,32,128]{4,3,2,1,0:T(8,128)(2,1)S(1)}, u32[]{:S(2)}, u32[]{:S(2)}) collective-permute-start(bf16[1,8,4,32,128]{4,3,2,1,0:T(8,128)(2,1)S(1)} %get-tuple-element.20), channel_id=1, source_target_pairs={{0,8},{1,9},{2,10},{3,11},{4,12},{5,13},{6,14},{7,15},{8,0},{9,1},... | collective-permute-start | bytes 786440 | tf_op jit(solution)/shard_map/ppermute | solution.py:495
  308.6 102.9 %all-to-all-start.3 = ((bf16[16,1088,128]{2,1,0:T(8,128)(2,1)}), bf16[16,1088,128]{2,1,0:T(8,128)(2,1)}, u32[]{:S(2)}, u32[]{:S(2)}) async-start(bf16[16,1088,128]{2,1,0:T(8,128)(2,1)} %bitcast.85), calls=%async_computation.3 | async-start | bytes 8912896 | tf_op jit(solution)/shard_map/all_to_all | solution.py:488

commit v6 on v5

--- a/solution.py
+++ b/solution.py
@@ -12,7 +12,7 @@
 OWNERS = ("lat", "lev", "sub")
 CHUNKS = 2
 HINT = 33
-FEW = 4
+FEW = 6
 
 
 def raw_table(fourier_order_holder, lon_count):
@@ -392,42 +392,39 @@
     )(waves, *received, basis, basis, solver, solver, *before)
 
 
-def synthesis_kernel(owners, pieces, *refs):
-    taking = sum(len(some) for some in pieces)
-    parts, (synth_ref, out_hbm, kept, out, arrived, left) = refs[:taking], refs[taking:]
+def synthesis_kernel(owners, begin, pieces, *refs):
+    parts, synth_ref, (out_hbm, kept, out, arrived, left) = (
+        refs[: len(pieces)],
+        refs[len(pieces)],
+        refs[-5:],
+    )
     steps, chunks, _, levels, rows, lats = kept.shape
     half = synth_ref.shape[-1]
     me = lax.axis_index(OWNERS)
-    cuts = sorted({end // levels for some in pieces for _, end, _ in some})
-
-    def copies(n, first, entire):
-        left = parts
-        for k, some in enumerate(pieces):
-            for part, (begin, end, apart) in zip(left, some):
-                if not begin <= first * levels < end:
-                    continue
-                span = pl.ds(n * levels - begin, levels)
-                if apart and not entire:
-                    for r in range(owners):
-                        place = kept.at[n, k, lax.bitwise_xor(me, r)]
-                        yield pltpu.make_async_copy(part.at[r, span], place, arrived.at[n, k])
-                else:
-                    yield pltpu.make_async_copy(part.at[:, span], kept.at[n, k], arrived.at[n, k])
-            left = left[len(some) :]
+
+    def copies(n, entire):
+        for k, (part, (start, apart)) in enumerate(zip(parts, pieces)):
+            span = pl.ds(begin - start + n * levels, levels)
+            if apart and not entire:
+                for r in range(owners):
+                    place = kept.at[n, k, lax.bitwise_xor(me, r)]
+                    yield pltpu.make_async_copy(part.at[r, span], place, arrived.at[n, k])
+            else:
+                yield pltpu.make_async_copy(part.at[:, span], kept.at[n, k], arrived.at[n, k])
 
     def leaving(n):
-        span = pl.ds(n * levels, levels)
-        return pltpu.make_async_copy(out.at[span], out_hbm.at[span], left.at[n])
-
-    for first, last in zip([0] + cuts, cuts):
-
-        @pl.loop(first, last)
-        def _(n, first=first):
-            for copy in copies(n, first, False):
-                copy.start()
-
-    def step(i, first):
-        for copy in copies(i, first, True):
+        mine = pl.ds(n * levels, levels)
+        span = pl.ds(begin + n * levels, levels)
+        return pltpu.make_async_copy(out.at[mine], out_hbm.at[span], left.at[n])
+
+    @pl.loop(0, steps)
+    def _(n):
+        for copy in copies(n, False):
+            copy.start()
+
+    @pl.loop(0, steps)
+    def _(i):
+        for copy in copies(i, True):
             copy.wait()
         sums = []
         for parity in range(2):
@@ -445,41 +442,41 @@
             out[i * levels + n, :, half:] = (even - odd).astype(jnp.bfloat16)
         leaving(i).start()
 
-    for first, last in zip([0] + cuts, cuts):
-        pl.loop(first, last)(functools.partial(step, first=first))
-
     @pl.loop(0, steps)
     def _(n):
         leaving(n).wait()
 
 
-def run_synthesis(pieces, parts, synth):
+def run_synthesis(begin, end, levels, pieces, parts, synth, before):
     owners, _, rows, lats = parts[0].shape
-    levels = pieces[0][-1][1]
     lon_count = 2 * synth.shape[-1]
     chunks = len(pieces)
-    count = 2 if levels % 2 == 0 else 1
-    steps = levels // count
+    count = 2 if (end - begin) % 2 == 0 else 1
+    steps = (end - begin) // count
+    given = [] if before is None else [before]
     anywhere = pl.BlockSpec(memory_space=pl.ANY)
     return pl.pallas_call(
-        functools.partial(synthesis_kernel, owners, pieces),
-        in_specs=[anywhere] * len(parts) + [pl.BlockSpec(memory_space=pltpu.VMEM)],
+        functools.partial(synthesis_kernel, owners, begin, pieces),
+        in_specs=[anywhere] * len(parts)
+        + [pl.BlockSpec(memory_space=pltpu.VMEM)]
+        + [anywhere] * len(given),
         out_specs=anywhere,
         out_shape=jax.ShapeDtypeStruct((levels, lats, lon_count), jnp.bfloat16),
         scratch_shapes=[
             pltpu.VMEM((steps, chunks, owners, count, rows, lats), jnp.bfloat16),
-            pltpu.VMEM((levels, lats, lon_count), jnp.bfloat16),
+            pltpu.VMEM((end - begin, lats, lon_count), jnp.bfloat16),
             pltpu.SemaphoreType.DMA((steps, chunks)),
             pltpu.SemaphoreType.DMA((steps,)),
         ],
         compiler_params=pltpu.CompilerParams(vmem_limit_bytes=VMEM_BYTES),
         cost_estimate=pl.CostEstimate(
-            flops=levels * lats * lon_count * lon_count,
-            bytes_accessed=4 * levels * lats * lon_count,
+            flops=(end - begin) * lats * lon_count * lon_count,
+            bytes_accessed=4 * (end - begin) * lats * lon_count,
             transcendentals=0,
         ),
+        input_output_aliases={len(parts) + 1: 0} if given else {},
         name="longitude_synthesis",
-    )(*parts, synth)
+    )(*parts, synth, *given)
 
 
 def exchange(part):
@@ -527,26 +524,29 @@
             )
 
         whole = [(0, levels, False)]
-        few = levels * FEW // 34 // 2 * 2
-        cut, last = levels - 2 * few, levels - few
-        first = exchange(analyse(0, whole[0], []))
-        main = analyse(1, (0, cut, False), [])
-        rest = analyse(1, (cut, levels, True), [main])
-        early, late = rest[:, :few], rest[:, few:]
-        early = swap(early, near + [far])
+        cut = levels - levels * FEW // 34 // 2 * 2
+        split = [(0, cut, False), (cut, levels, True)]
+        first = exchange(analyse(0, split[0], []))
+        main = analyse(1, split[0], [])
+        early = swap(analyse(0, split[1], [main]), near + [far])
+        late = analyse(1, split[1], [main])
         second = exchange(main)
-        pieces = [(0, last, False), (last, levels, True)]
-        solved, aside = columns(0, whole, pieces, [first], early[1:])
+        arriving = split[:1] + split[1:] * 2
+        (solved,) = columns(0, arriving, whole, [first, *early], [])
         solved, late = lax.optimization_barrier((solved, late))
         late = swap(late, near + [far])
         first = exchange(solved)
-        split = [(0, cut, False)] + [(cut, last, True)] * 2 + [(last, levels, True)] * 2
-        (solved,) = columns(1, split, whole, [second, *early, *late], [])
+        solved, aside = columns(1, arriving, split, [second, *late], [])
         solved, aside = lax.optimization_barrier((solved, aside))
         aside = jnp.concatenate(swap(aside, near + [far]))
         second = exchange(solved)
         synth = synthesis_rows(owners, chunks, holder, table)
-        return run_synthesis([pieces, whole], [first, aside, second], synth)
+        result = run_synthesis(
+            cut, levels, levels, [(0, False), (cut, True)], [first, aside], synth, None
+        )
+        return run_synthesis(
+            0, cut, levels, [(0, False), (0, False)], [first, second], synth, result
+        )
 
     return shards
 

time: 424 us -> 417 us (0.983)
  waiting for transfers between devices: 305 us -> 241 us
  starting transfers between devices: 34.6 us -> 82.7 us
  Pallas kernels: 76.5 us -> 82.2 us
    ppermute x12, starting transfers between devices: 13.5 us -> 62.4 us  [swap(): lax.ppermute(halves[:, 1], OWNERS, [(o, o ^ bit) for o in range(owners)])]
    all_to_all x4, waiting for transfers between devices: 155 us -> 113 us  [exchange(): return lax.all_to_all(flat, OWNERS, 0, 0, tiled=True).reshape(part.shape)]
    ppermute x12, waiting for transfers between devices: 150 us -> 129 us  [swap(): lax.ppermute(halves[:, 1], OWNERS, [(o, o ^ bit) for o in range(owners)])]
    pallas_call x3 -> x4, Pallas kernels: 30.8 us -> 33.7 us  [run_analysis(): pl.pallas_call(functools.partial(analysis_kernel, owners, chunks, k, begi...]
    pallas_call x1 -> x2, Pallas kernels: 11.7 us -> 14.6 us  [run_synthesis(): pl.pallas_call(functools.partial(synthesis_kernel, owners, begin, pieces)...]
  transfers between devices with their start and end apart: 16 -> 16, of which waited for: 13 -> 15; matrix products, arithmetic and copies ran while one was open for 2% -> 2% of each run, Pallas kernels for 12% -> 15%
where the time goes in v6:
time: 417 us; the launch traced here: 416 us
  waiting for transfers between devices  241 us (58%)
  starting transfers between devices  82.7 us (20%)
  Pallas kernels  82.2 us (20%)
  local copies, waits for them, and re-layouts  7.31 us (2%)
    ppermute x12, waiting for transfers between devices, swap(): lax.ppermute(halves[:, 1], OWNERS, [(o, o ^ bit) for o in range(owners)])  129 us
    all_to_all x4, waiting for transfers between devices, exchange(): return lax.all_to_all(flat, OWNERS, 0, 0, tiled=True).reshape(part.shape)  113 us
    ppermute x12, starting transfers between devices, swap(): lax.ppermute(halves[:, 1], OWNERS, [(o, o ^ bit) for o in range(owners)])  62.4 us
    pallas_call x4, Pallas kernels, run_analysis(): pl.pallas_call(functools.partial(analysis_kernel, owners, chunks, k, begi...  33.7 us
    pallas_call x2, Pallas kernels, run_columns(): pl.pallas_call(functools.partial(column_kernel, owners, bands, k, pieces_...  30.7 us
    all_to_all x4, starting transfers between devices, exchange(): return lax.all_to_all(flat, OWNERS, 0, 0, tiled=True).reshape(part.shape)  20.3 us
    pallas_call x2, Pallas kernels, run_synthesis(): pl.pallas_call(functools.partial(synthesis_kernel, owners, begin, pieces)...  14.6 us
  transfers between devices with their start and end apart: 16, of which 15 were waited for; matrix products, arithmetic and copies ran while one was open for 2% of the time, Pallas kernels for 15%

profile of v6, /device:TPU:11, one launch (start us, length us, event | category | flops | bytes accessed | tf_op | source)
XLA Modules:
  0.0 415.6 jit_solution(6056995764355127401)
XLA Ops:
  0.0 11.6 %longitude_analysis.4 = bf16[16,28,32,128]{3,2,1,0:T(8,128)(2,1)} custom-call(s32[1,512]{1,0:T(1,128)} %bitcast.113, bf16[2,2,256,512]{3,2,1,0:T(8,128)(2,1)} %constant.23.clone.waves_hbm.waves_ref, bf16[34,128,1024]{2,1,0:T(8,128)(2,1)} %state_hbm.7, bf16[34,128,1024]{2,1,0:T(8,128)(2,1)} %forcing_hbm.7), custom_call_target="tpu_custom_call" | custom-call | flops 1879048192 | bytes 22020096 | tf_op jit(solution)/shard_map/longitude_analysis/pallas_call | solution.py:212
  11.7 6.6 %all-to-all-start = ((bf16[16,896,128]{2,1,0:T(8,128)(2,1)}), bf16[16,896,128]{2,1,0:T(8,128)(2,1)}, u32[]{:S(2)}, u32[]{:S(2)}) async-start(bf16[16,896,128]{2,1,0:T(8,128)(2,1)} %bitcast.85), calls=%async_computation | async-start | bytes 7340032 | tf_op jit(solution)/shard_map/all_to_all | solution.py:485
  18.2 11.7 %longitude_analysis.5.refs_0_ = bf16[16,28,32,128]{3,2,1,0:T(8,128)(2,1)} custom-call(s32[1,512]{1,0:T(1,128)} %bitcast.114, bf16[2,2,256,512]{3,2,1,0:T(8,128)(2,1)} %constant.23.clone.waves_hbm.waves_ref, bf16[34,128,1024]{2,1,0:T(8,128)(2,1)} %state_hbm.7, bf16[34,128,1024]{2,1,0:T(8,128)(2,1)} %forcing_hbm.7), custom_call_target="tpu_custom_call" | custom-call | flops 1879048192 | bytes 22020096 | tf_op jit(solution)/shard_map/longitude_analysis/pallas_call | solution.py:212
  29.9 5.2 %longitude_analysis.6 = bf16[16,6,32,128]{3,2,1,0:T(8,128)(2,1)} custom-call(s32[1,512]{1,0:T(1,128)} %bitcast.115, bf16[2,2,256,512]{3,2,1,0:T(8,128)(2,1)} %constant.23.clone.waves_hbm.waves_ref, bf16[34,128,1024]{2,1,0:T(8,128)(2,1)} %state_hbm.7, bf16[34,128,1024]{2,1,0:T(8,128)(2,1)} %forcing_hbm.7, bf16[16,28,32,128]{3,2,1,0:T(8,128)(2,1)} %longitude_analysis.5.refs_0_), custom_call_target="tpu_custom_call" | custom-call | flops 402653184 | bytes 4718592 | tf_op jit(solution)/shard_map/longitude_analysis/pallas_call | solution.py:212
  35.1 1.2 fusion.11
  36.3 0.4 collective-permute-start
  36.7 1.4 collective-permute-done
  38.2 0.3 collective-permute-start.1
  38.5 14.1 %collective-permute-done.1 = bf16[4,2,6,32,128]{4,3,2,0,1:T(8,128)(2,1)S(1)} collective-permute-done((bf16[4,2,6,32,128]{4,3,2,0,1:T(8,128)(2,1)S(1)}, bf16[4,2,6,32,128]{4,3,2,0,1:T(8,128)(2,1)S(1)}, u32[]{:S(2)}, u32[]{:S(2)}) %collective-permute-start.1) | collective-permute-done | bytes 393248 | tf_op jit(solution)/shard_map/ppermute | solution.py:492
  52.6 0.1 pad_maximum_fusion
  52.8 2.6 collective-permute-start.2
  55.4 32.8 %collective-permute-done.2 = bf16[2,4,6,32,128]{4,3,2,1,0:T(8,128)(2,1)S(1)} collective-permute-done((bf16[2,4,6,32,128]{4,3,2,1,0:T(8,128)(2,1)S(1)}, bf16[2,4,6,32,128]{4,3,2,1,0:T(8,128)(2,1)S(1)}, u32[]{:S(2)}, u32[]{:S(2)}) %collective-permute-start.2) | collective-permute-done | bytes 393248 | tf_op jit(solution)/shard_map/ppermute | solution.py:492
  88.3 0.8 slice_bitcast_fusion.8
  89.2 1.2 dynamic_slice.3.waves_ref
  90.4 5.2 %longitude_analysis.7 = bf16[16,6,32,128]{3,2,1,0:T(8,128)(2,1)} custom-call(s32[1,512]{1,0:T(1,128)} %bitcast.116, bf16[2,2,256,512]{3,2,1,0:T(8,128)(2,1)} %constant.23.clone.waves_hbm.waves_ref, bf16[34,128,1024]{2,1,0:T(8,128)(2,1)} %state_hbm.7, bf16[34,128,1024]{2,1,0:T(8,128)(2,1)} %forcing_hbm.7, bf16[16,28,32,128]{3,2,1,0:T(8,128)(2,1)} %longitude_analysis.5.refs_0_), custom_call_target="tpu_custom_call" | custom-call | flops 402653184 | bytes 4718592 | tf_op jit(solution)/shard_map/longitude_analysis/pallas_call | solution.py:212
  95.6 12.8 %all-to-all-done = bf16[16,896,128]{2,1,0:T(8,128)(2,1)} async-done(((bf16[16,896,128]{2,1,0:T(8,128)(2,1)}), bf16[16,896,128]{2,1,0:T(8,128)(2,1)}, u32[]{:S(2)}, u32[]{:S(2)}) %all-to-all-start) | async-done | bytes 3670048 | tf_op jit(solution)/shard_map/all_to_all | solution.py:485
  108.4 4.8 %all-to-all-start.2 = ((bf16[16,896,128]{2,1,0:T(8,128)(2,1)}), bf16[16,896,128]{2,1,0:T(8,128)(2,1)}, u32[]{:S(2)}, u32[]{:S(2)}) async-start(bf16[16,896,128]{2,1,0:T(8,128)(2,1)} %bitcast.84), calls=%async_computation.2 | async-start | bytes 7340032 | tf_op jit(solution)/shard_map/all_to_all | solution.py:485
  113.2 0.8 collective-permute-done.3
  114.0 0.8 copy-done.1
  114.8 15.4 %legendre_solve.2 = bf16[16,34,32,128]{3,2,1,0:T(8,128)(2,1)} custom-call(s32[32]{0:T(128)} %dynamic_slice.3.waves_ref, bf16[16,28,32,128]{3,2,1,0:T(8,128)(2,1)} %bitcast.2.refs_0_, bf16[8,6,32,128]{3,2,1,0:T(8,128)(2,1)} %get-tuple-element.26.refs_1_, bf16[8,6,32,128]{3,2,1,0:T(8,128)(2,1)} %bitcast.118, bf16[32,512,512]{2,1,0:T(8,128)(2,1)} %refs_4_.3, ...), custom_call_target="tpu_custom_call" | custom-call | flops 112944218112 | bytes 15204352 | tf_op jit(solution)/shard_map/legendre_solve/pallas_call | solution.py:368
  130.2 1.4 collective-permute-start.4
  131.6 1.3 collective-permute-done.4
  133.1 0.4 collective-permute-start.5
  133.5 13.5 %collective-permute-done.5 = bf16[4,2,6,32,128]{4,3,2,0,1:T(8,128)(2,1)S(1)} collective-permute-done((bf16[4,2,6,32,128]{4,3,2,0,1:T(8,128)(2,1)S(1)}, bf16[4,2,6,32,128]{4,3,2,0,1:T(8,128)(2,1)S(1)}, u32[]{:S(2)}, u32[]{:S(2)}) %collective-permute-start.5) | collective-permute-done | bytes 393248 | tf_op jit(solution)/shard_map/ppermute | solution.py:492
  147.0 0.1 pad_maximum_fusion.2
  147.1 23.9 %collective-permute-start.6 = (bf16[2,4,6,32,128]{4,3,2,1,0:T(8,128)(2,1)S(1)}, bf16[2,4,6,32,128]{4,3,2,1,0:T(8,128)(2,1)S(1)}, u32[]{:S(2)}, u32[]{:S(2)}) collective-permute-start(bf16[2,4,6,32,128]{4,3,2,1,0:T(8,128)(2,1)S(1)} %slice_bitcast_fusion.6), channel_id=1, source_target_pairs={{0,4},{1,5},{2,6},{3,7},{4,0},{5,1},{6,2},{7,3},{8,12},{9,13},{10,... | collective-permute-start | bytes 1179656 | tf_op jit(solution)/shard_map/ppermute | solution.py:492
  171.1 21.6 %collective-permute-done.6 = bf16[2,4,6,32,128]{4,3,2,1,0:T(8,128)(2,1)S(1)} collective-permute-done((bf16[2,4,6,32,128]{4,3,2,1,0:T(8,128)(2,1)S(1)}, bf16[2,4,6,32,128]{4,3,2,1,0:T(8,128)(2,1)S(1)}, u32[]{:S(2)}, u32[]{:S(2)}) %collective-permute-start.6) | collective-permute-done | bytes 393248 | tf_op jit(solution)/shard_map/ppermute | solution.py:492
  192.8 0.8 slice_bitcast_fusion.4
  193.7 10.6 %all-to-all-done.2 = bf16[16,896,128]{2,1,0:T(8,128)(2,1)} async-done(((bf16[16,896,128]{2,1,0:T(8,128)(2,1)}), bf16[16,896,128]{2,1,0:T(8,128)(2,1)}, u32[]{:S(2)}, u32[]{:S(2)}) %all-to-all-start.2) | async-done | bytes 3670048 | tf_op jit(solution)/shard_map/all_to_all | solution.py:485
  204.3 4.5 %all-to-all-start.1 = ((bf16[16,1088,128]{2,1,0:T(8,128)(2,1)}), bf16[16,1088,128]{2,1,0:T(8,128)(2,1)}, u32[]{:S(2)}, u32[]{:S(2)}) async-start(bf16[16,1088,128]{2,1,0:T(8,128)(2,1)} %bitcast.89), calls=%async_computation.1 | async-start | bytes 8912896 | tf_op jit(solution)/shard_map/all_to_all | solution.py:485
  208.8 1.6 collective-permute-done.7
  210.4 0.7 copy-done.2
  211.2 15.3 %legendre_solve.3 = (bf16[16,28,32,128]{3,2,1,0:T(8,128)(2,1)}, bf16[16,6,32,128]{3,2,1,0:T(8,128)(2,1)}) custom-call(s32[32]{0:T(128)} %dynamic_slice.3.waves_ref, bf16[16,28,32,128]{3,2,1,0:T(8,128)(2,1)} %bitcast.20.refs_0_, bf16[8,6,32,128]{3,2,1,0:T(8,128)(2,1)} %get-tuple-element.20.refs_1_, bf16[8,6,32,128]{3,2,1,0:T(8,128)(2,1)} %bitcast.119, ...), custom_call_target="tpu_custom_call" | custom-call | flops 112944218112 | bytes 15204352 | tf_op jit(solution)/shard_map/legendre_solve/pallas_call | solution.py:368
  226.4 1.2 fusion.9
  227.6 1.7 collective-permute-start.8
  229.3 1.3 collective-permute-done.8
  230.7 0.1 collective-permute-start.9
  230.8 13.9 %collective-permute-done.9 = bf16[4,2,6,32,128]{4,3,2,0,1:T(8,128)(2,1)S(1)} collective-permute-done((bf16[4,2,6,32,128]{4,3,2,0,1:T(8,128)(2,1)S(1)}, bf16[4,2,6,32,128]{4,3,2,0,1:T(8,128)(2,1)S(1)}, u32[]{:S(2)}, u32[]{:S(2)}) %collective-permute-start.9) | collective-permute-done | bytes 393248 | tf_op jit(solution)/shard_map/ppermute | solution.py:492
  244.7 0.1 pad_maximum_fusion.4
  244.9 31.4 %collective-permute-start.10 = (bf16[2,4,6,32,128]{4,3,2,1,0:T(8,128)(2,1)S(1)}, bf16[2,4,6,32,128]{4,3,2,1,0:T(8,128)(2,1)S(1)}, u32[]{:S(2)}, u32[]{:S(2)}) collective-permute-start(bf16[2,4,6,32,128]{4,3,2,1,0:T(8,128)(2,1)S(1)} %slice_bitcast_fusion.2), channel_id=1, source_target_pairs={{0,4},{1,5},{2,6},{3,7},{4,0},{5,1},{6,2},{7,3},{8,12},{9,13},{10,... | collective-permute-start | bytes 1179656 | tf_op jit(solution)/shard_map/ppermute | solution.py:492
  276.2 26.3 %collective-permute-done.10 = bf16[2,4,6,32,128]{4,3,2,1,0:T(8,128)(2,1)S(1)} collective-permute-done((bf16[2,4,6,32,128]{4,3,2,1,0:T(8,128)(2,1)S(1)}, bf16[2,4,6,32,128]{4,3,2,1,0:T(8,128)(2,1)S(1)}, u32[]{:S(2)}, u32[]{:S(2)}) %collective-permute-start.10) | collective-permute-done | bytes 393248 | tf_op jit(solution)/shard_map/ppermute | solution.py:492
  302.9 15.3 %all-to-all-done.1 = bf16[16,1088,128]{2,1,0:T(8,128)(2,1)} async-done(((bf16[16,1088,128]{2,1,0:T(8,128)(2,1)}), bf16[16,1088,128]{2,1,0:T(8,128)(2,1)}, u32[]{:S(2)}, u32[]{:S(2)}) %all-to-all-start.1) | async-done | bytes 4456480 | tf_op jit(solution)/shard_map/all_to_all | solution.py:485
  318.2 4.4 %all-to-all-start.3 = ((bf16[16,896,128]{2,1,0:T(8,128)(2,1)}), bf16[16,896,128]{2,1,0:T(8,128)(2,1)}, u32[]{:S(2)}, u32[]{:S(2)}) async-start(bf16[16,896,128]{2,1,0:T(8,128)(2,1)} %bitcast.90), calls=%async_computation.3 | async-start | bytes 7340032 | tf_op jit(solution)/shard_map/all_to_all | solution.py:485
  322.6 3.2 synthesis_rows.1.refs_2_
  325.8 0.9 pad_maximum_fusion.6.refs_1_
  326.8 4.5 %longitude_synthesis.2.refs_3_ = bf16[34,128,1024]{2,1,0:T(8,128)(2,1)} custom-call(bf16[16,34,32,128]{3,2,1,0:T(8,128)(2,1)} %bitcast.18.refs_0_, bf16[16,6,32,128]{3,2,1,0:T(8,128)(2,1)} %pad_maximum_fusion.6.refs_1_, bf16[2,2,256,512]{3,2,1,0:T(8,128)(2,1)} %synthesis_rows.1.refs_2_), custom_call_target="tpu_custom_call" | custom-call | flops 805306368 | bytes 3145728 | tf_op jit(solution)/shard_map/longitude_synthesis/pallas_call | solution.py:458
  331.3 74.1 %all-to-all-done.3 = bf16[16,896,128]{2,1,0:T(8,128)(2,1)} async-done(((bf16[16,896,128]{2,1,0:T(8,128)(2,1)}), bf16[16,896,128]{2,1,0:T(8,128)(2,1)}, u32[]{:S(2)}, u32[]{:S(2)}) %all-to-all-start.3) | async-done | bytes 3670048 | tf_op jit(solution)/shard_map/all_to_all | solution.py:485
  405.4 10.1 %longitude_synthesis.3 = bf16[34,128,1024]{2,1,0:T(8,128)(2,1)} custom-call(bf16[16,34,32,128]{3,2,1,0:T(8,128)(2,1)} %bitcast.18.refs_0_, bf16[16,28,32,128]{3,2,1,0:T(8,128)(2,1)} %bitcast.36.refs_1_, bf16[2,2,256,512]{3,2,1,0:T(8,128)(2,1)} %synthesis_rows.1.refs_2_, bf16[34,128,1024]{2,1,0:T(8,128)(2,1)} %longitude_synthesis.2.refs_3_), custom_call_target="tpu_custom_call", output_to_operand_aliasing={{}: (3, {})} | custom-call | flops 3758096384 | bytes 14680064 | tf_op jit(solution)/shard_map/longitude_synthesis/pallas_call | solution.py:458
  (25 shorter events, 1.1 us)
Async XLA Ops:
  11.7 96.7 %all-to-all-start = ((bf16[16,896,128]{2,1,0:T(8,128)(2,1)}), bf16[16,896,128]{2,1,0:T(8,128)(2,1)}, u32[]{:S(2)}, u32[]{:S(2)}) async-start(bf16[16,896,128]{2,1,0:T(8,128)(2,1)} %bitcast.85), calls=%async_computation | async-start | bytes 7340032 | tf_op jit(solution)/shard_map/all_to_all | solution.py:485
  36.3 1.8 collective-permute-start
  38.2 14.5 %collective-permute-start.1 = (bf16[4,2,6,32,128]{4,3,2,0,1:T(8,128)(2,1)S(1)}, bf16[4,2,6,32,128]{4,3,2,0,1:T(8,128)(2,1)S(1)}, u32[]{:S(2)}, u32[]{:S(2)}) collective-permute-start(bf16[4,2,6,32,128]{4,3,2,0,1:T(8,128)(2,1)S(1)} %get-tuple-element.28), channel_id=1, source_target_pairs={{0,2},{1,3},{2,0},{3,1},{4,6},{5,7},{6,4},{7,5},{8,10},{9,11},{10,... | collective-permute-start | bytes 1179656 | tf_op jit(solution)/shard_map/ppermute | solution.py:492
  52.8 35.4 %collective-permute-start.2 = (bf16[2,4,6,32,128]{4,3,2,1,0:T(8,128)(2,1)S(1)}, bf16[2,4,6,32,128]{4,3,2,1,0:T(8,128)(2,1)S(1)}, u32[]{:S(2)}, u32[]{:S(2)}) collective-permute-start(bf16[2,4,6,32,128]{4,3,2,1,0:T(8,128)(2,1)S(1)} %slice_bitcast_fusion.10), channel_id=1, source_target_pairs={{0,4},{1,5},{2,6},{3,7},{4,0},{5,1},{6,2},{7,3},{8,12},{9,13},{10,... | collective-permute-start | bytes 1179656 | tf_op jit(solution)/shard_map/ppermute | solution.py:492
  89.1 24.9 %collective-permute-start.3 = (bf16[1,8,6,32,128]{4,3,2,1,0:T(8,128)(2,1)S(1)}, bf16[1,8,6,32,128]{4,3,2,1,0:T(8,128)(2,1)S(1)}, u32[]{:S(2)}, u32[]{:S(2)}) collective-permute-start(bf16[1,8,6,32,128]{4,3,2,1,0:T(8,128)(2,1)S(1)} %get-tuple-element.25), channel_id=1, source_target_pairs={{0,8},{1,9},{2,10},{3,11},{4,12},{5,13},{6,14},{7,15},{8,0},{9,1},... | collective-permute-start | bytes 1179656 | tf_op jit(solution)/shard_map/ppermute | solution.py:492
  108.4 95.9 %all-to-all-start.2 = ((bf16[16,896,128]{2,1,0:T(8,128)(2,1)}), bf16[16,896,128]{2,1,0:T(8,128)(2,1)}, u32[]{:S(2)}, u32[]{:S(2)}) async-start(bf16[16,896,128]{2,1,0:T(8,128)(2,1)} %bitcast.84), calls=%async_computation.2 | async-start | bytes 7340032 | tf_op jit(solution)/shard_map/all_to_all | solution.py:485
  114.0 0.8 copy-start.1
  114.8 15.4 %copy-start = (bf16[16,6,32,128]{3,2,1,0:T(8,128)(2,1)S(1)}, bf16[16,6,32,128]{3,2,1,0:T(8,128)(2,1)}, u32[]{:S(2)}) copy-start(bf16[16,6,32,128]{3,2,1,0:T(8,128)(2,1)} %longitude_analysis.7) | copy-start | bytes 2359300
  130.2 2.8 collective-permute-start.4
  133.1 13.9 %collective-permute-start.5 = (bf16[4,2,6,32,128]{4,3,2,0,1:T(8,128)(2,1)S(1)}, bf16[4,2,6,32,128]{4,3,2,0,1:T(8,128)(2,1)S(1)}, u32[]{:S(2)}, u32[]{:S(2)}) collective-permute-start(bf16[4,2,6,32,128]{4,3,2,0,1:T(8,128)(2,1)S(1)} %get-tuple-element.22), channel_id=1, source_target_pairs={{0,2},{1,3},{2,0},{3,1},{4,6},{5,7},{6,4},{7,5},{8,10},{9,11},{10,... | collective-permute-start | bytes 1179656 | tf_op jit(solution)/shard_map/ppermute | solution.py:492
  147.1 45.5 %collective-permute-start.6 = (bf16[2,4,6,32,128]{4,3,2,1,0:T(8,128)(2,1)S(1)}, bf16[2,4,6,32,128]{4,3,2,1,0:T(8,128)(2,1)S(1)}, u32[]{:S(2)}, u32[]{:S(2)}) collective-permute-start(bf16[2,4,6,32,128]{4,3,2,1,0:T(8,128)(2,1)S(1)} %slice_bitcast_fusion.6), channel_id=1, source_target_pairs={{0,4},{1,5},{2,6},{3,7},{4,0},{5,1},{6,2},{7,3},{8,12},{9,13},{10,... | collective-permute-start | bytes 1179656 | tf_op jit(solution)/shard_map/ppermute | solution.py:492
  193.7 16.7 %collective-permute-start.7 = (bf16[1,8,6,32,128]{4,3,2,1,0:T(8,128)(2,1)S(1)}, bf16[1,8,6,32,128]{4,3,2,1,0:T(8,128)(2,1)S(1)}, u32[]{:S(2)}, u32[]{:S(2)}) collective-permute-start(bf16[1,8,6,32,128]{4,3,2,1,0:T(8,128)(2,1)S(1)} %get-tuple-element.19), channel_id=1, source_target_pairs={{0,8},{1,9},{2,10},{3,11},{4,12},{5,13},{6,14},{7,15},{8,0},{9,1},... | collective-permute-start | bytes 1179656 | tf_op jit(solution)/shard_map/ppermute | solution.py:492
  204.3 113.9 %all-to-all-start.1 = ((bf16[16,1088,128]{2,1,0:T(8,128)(2,1)}), bf16[16,1088,128]{2,1,0:T(8,128)(2,1)}, u32[]{:S(2)}, u32[]{:S(2)}) async-start(bf16[16,1088,128]{2,1,0:T(8,128)(2,1)} %bitcast.89), calls=%async_computation.1 | async-start | bytes 8912896 | tf_op jit(solution)/shard_map/all_to_all | solution.py:485
  210.4 0.8 copy-start.2
  227.6 3.1 collective-permute-start.8
  230.7 13.9 %collective-permute-start.9 = (bf16[4,2,6,32,128]{4,3,2,0,1:T(8,128)(2,1)S(1)}, bf16[4,2,6,32,128]{4,3,2,0,1:T(8,128)(2,1)S(1)}, u32[]{:S(2)}, u32[]{:S(2)}) collective-permute-start(bf16[4,2,6,32,128]{4,3,2,0,1:T(8,128)(2,1)S(1)} %get-tuple-element.16), channel_id=1, source_target_pairs={{0,2},{1,3},{2,0},{3,1},{4,6},{5,7},{6,4},{7,5},{8,10},{9,11},{10,... | collective-permute-start | bytes 1179656 | tf_op jit(solution)/shard_map/ppermute | solution.py:492
  244.9 57.7 %collective-permute-start.10 = (bf16[2,4,6,32,128]{4,3,2,1,0:T(8,128)(2,1)S(1)}, bf16[2,4,6,32,128]{4,3,2,1,0:T(8,128)(2,1)S(1)}, u32[]{:S(2)}, u32[]{:S(2)}) collective-permute-start(bf16[2,4,6,32,128]{4,3,2,1,0:T(8,128)(2,1)S(1)} %slice_bitcast_fusion.2), channel_id=1, source_target_pairs={{0,4},{1,5},{2,6},{3,7},{4,0},{5,1},{6,2},{7,3},{8,12},{9,13},{10,... | collective-permute-start | bytes 1179656 | tf_op jit(solution)/shard_map/ppermute | solution.py:492
  302.8 23.0 %collective-permute-start.11 = (bf16[1,8,6,32,128]{4,3,2,1,0:T(8,128)(2,1)S(1)}, bf16[1,8,6,32,128]{4,3,2,1,0:T(8,128)(2,1)S(1)}, u32[]{:S(2)}, u32[]{:S(2)}) collective-permute-start(bf16[1,8,6,32,128]{4,3,2,1,0:T(8,128)(2,1)S(1)} %get-tuple-element.14), channel_id=1, source_target_pairs={{0,8},{1,9},{2,10},{3,11},{4,12},{5,13},{6,14},{7,15},{8,0},{9,1},... | collective-permute-start | bytes 1179656 | tf_op jit(solution)/shard_map/ppermute | solution.py:492
  318.2 87.2 %all-to-all-start.3 = ((bf16[16,896,128]{2,1,0:T(8,128)(2,1)}), bf16[16,896,128]{2,1,0:T(8,128)(2,1)}, u32[]{:S(2)}, u32[]{:S(2)}) async-start(bf16[16,896,128]{2,1,0:T(8,128)(2,1)} %bitcast.90), calls=%async_computation.3 | async-start | bytes 7340032 | tf_op jit(solution)/shard_map/all_to_all | solution.py:485

commit v7 on v6

--- a/solution.py
+++ b/solution.py
@@ -12,7 +12,7 @@
 OWNERS = ("lat", "lev", "sub")
 CHUNKS = 2
 HINT = 33
-FEW = 6
+HEAD, EARLY, LATE, LAST = 6, 4, 6, 6
 
 
 def raw_table(fourier_order_holder, lon_count):
@@ -227,7 +227,7 @@
         ],
         compiler_params=pltpu.CompilerParams(vmem_limit_bytes=VMEM_BYTES),
         cost_estimate=pl.CostEstimate(
-            flops=2 * levels * lats * lon_count * slots // chunks,
+            flops=30 * 2 * levels * lats * lon_count * slots // chunks,
             bytes_accessed=6 * levels * lats * lon_count,
             transcendentals=0,
         ),
@@ -485,13 +485,17 @@
     return lax.all_to_all(flat, OWNERS, 0, 0, tiled=True).reshape(part.shape)
 
 
+def give(part, bit):
+    owners = part.shape[0]
+    halves = part.reshape((owners // 2 // bit, 2, bit) + part.shape[1:])
+    given = lax.ppermute(halves[:, 1], OWNERS, [(o, o ^ bit) for o in range(owners)])
+    return halves[:, 0], given
+
+
 def swap(part, bits):
-    owners = part.shape[0]
     for bit in bits:
-        halves = part.reshape((owners // 2 // bit, 2, bit) + part.shape[1:])
-        given = lax.ppermute(halves[:, 1], OWNERS, [(o, o ^ bit) for o in range(owners)])
-        part = jnp.stack([halves[:, 0], given], axis=1).reshape(part.shape)
-    return halves[0, 0], given[0]
+        part = jnp.stack(give(part, bit), axis=1).reshape(part.shape)
+    return part
 
 
 def chunked_shards(lat_bands, level_groups, chunks):
@@ -523,29 +527,44 @@
                 spherical_basis_table, implicit_solver_matrix,
             )
 
+        def share(count):
+            return levels * count // 34 // 2 * 2
+
+        def across(part):
+            return [half[0] for half in give(part, far)]
+
         whole = [(0, levels, False)]
-        cut = levels - levels * FEW // 34 // 2 * 2
-        split = [(0, cut, False), (cut, levels, True)]
-        first = exchange(analyse(0, split[0], []))
-        main = analyse(1, split[0], [])
-        early = swap(analyse(0, split[1], [main]), near + [far])
-        late = analyse(1, split[1], [main])
+        head_cut, last_cut = levels - share(HEAD), levels - share(LAST)
+        late_cut = levels - share(LATE)
+        early_cut = late_cut - share(EARLY)
+        head = analyse(0, (head_cut, levels, True), [])
+        main = analyse(0, (0, head_cut, False), [head])
+        head = swap(head, [far])
+        first = exchange(main)
+        main = analyse(1, (0, early_cut, False), [])
+        rest = analyse(1, (early_cut, levels, True), [main])
+        early, late = rest[:, : late_cut - early_cut], rest[:, late_cut - early_cut :]
+        both = swap(jnp.concatenate([head, early], axis=1), near)
+        head, early = both[:, : levels - head_cut], across(both[:, levels - head_cut :])
         second = exchange(main)
-        arriving = split[:1] + split[1:] * 2
-        (solved,) = columns(0, arriving, whole, [first, *early], [])
+        pieces = [(0, head_cut, False), (head_cut, levels, True)]
+        (solved,) = columns(0, pieces, whole, [first, head], early[1:])
         solved, late = lax.optimization_barrier((solved, late))
-        late = swap(late, near + [far])
+        late = across(swap(late, near))
         first = exchange(solved)
-        solved, aside = columns(1, arriving, split, [second, *late], [])
+        pieces = [(0, early_cut, False)]
+        pieces += [(early_cut, late_cut, True)] * 2 + [(late_cut, levels, True)] * 2
+        split = [(0, last_cut, False), (last_cut, levels, True)]
+        solved, aside = columns(1, pieces, split, [second, *early, *late], [])
         solved, aside = lax.optimization_barrier((solved, aside))
-        aside = jnp.concatenate(swap(aside, near + [far]))
+        aside = jnp.concatenate(across(swap(aside, near)))
         second = exchange(solved)
         synth = synthesis_rows(owners, chunks, holder, table)
         result = run_synthesis(
-            cut, levels, levels, [(0, False), (cut, True)], [first, aside], synth, None
+            last_cut, levels, levels, [(0, False), (last_cut, True)], [first, aside], synth, None
         )
         return run_synthesis(
-            0, cut, levels, [(0, False), (0, False)], [first, second], synth, result
+            0, last_cut, levels, [(0, False), (0, False)], [first, second], synth, result
         )
 
     return shards

time: 417 us -> 411 us (0.986)
  starting transfers between devices: 82.7 us -> 52.6 us
  waiting for transfers between devices: 241 us -> 261 us
  local copies, waits for them, and re-layouts: 7.31 us -> 11.9 us
    ppermute x12 -> x13, starting transfers between devices: 62.4 us -> 30.4 us  [give(): lax.ppermute(halves[:, 1], OWNERS, [(o, o ^ bit) for o in range(owners)])]
    ppermute x12 -> x13, waiting for transfers between devices: 129 us -> 154 us  [give(): lax.ppermute(halves[:, 1], OWNERS, [(o, o ^ bit) for o in range(owners)])]
    all_to_all x4, waiting for transfers between devices: 113 us -> 107 us  [exchange(): return lax.all_to_all(flat, OWNERS, 0, 0, tiled=True).reshape(part.shape)]
  transfers between devices with their start and end apart: 16 -> 17, of which waited for: 15 -> 13; matrix products, arithmetic and copies ran while one was open for 2% -> 2% of each run, Pallas kernels for 15% -> 16%
where the time goes in v7:
time: 411 us; the launch traced here: 410 us
  waiting for transfers between devices  261 us (64%)
  Pallas kernels  82.3 us (20%)
  starting transfers between devices  52.6 us (13%)
  local copies, waits for them, and re-layouts  11.9 us (3%)
    ppermute x13, waiting for transfers between devices, give(): lax.ppermute(halves[:, 1], OWNERS, [(o, o ^ bit) for o in range(owners)])  154 us
    all_to_all x4, waiting for transfers between devices, exchange(): return lax.all_to_all(flat, OWNERS, 0, 0, tiled=True).reshape(part.shape)  107 us
    pallas_call x4, Pallas kernels, run_analysis(): pl.pallas_call(functools.partial(analysis_kernel, owners, chunks, k, begi...  33.7 us
    pallas_call x2, Pallas kernels, run_columns(): pl.pallas_call(functools.partial(column_kernel, owners, bands, k, pieces_...  30.8 us
    ppermute x13, starting transfers between devices, give(): lax.ppermute(halves[:, 1], OWNERS, [(o, o ^ bit) for o in range(owners)])  30.4 us
    all_to_all x4, starting transfers between devices, exchange(): return lax.all_to_all(flat, OWNERS, 0, 0, tiled=True).reshape(part.shape)  22.2 us
    pallas_call x2, Pallas kernels, run_synthesis(): pl.pallas_call(functools.partial(synthesis_kernel, owners, begin, pieces)...  14.6 us
  transfers between devices with their start and end apart: 17, of which 13 were waited for; matrix products, arithmetic and copies ran while one was open for 2% of the time, Pallas kernels for 16%

profile of v7, /device:TPU:11, one launch (start us, length us, event | category | flops | bytes accessed | tf_op | source)
XLA Modules:
  0.0 409.9 jit_solution(3955708812973028261)
XLA Ops:
  0.0 5.2 %longitude_analysis.4.refs_0_ = bf16[16,6,32,128]{3,2,1,0:T(8,128)(2,1)} custom-call(s32[1,512]{1,0:T(1,128)} %bitcast.121, bf16[2,2,256,512]{3,2,1,0:T(8,128)(2,1)} %constant.23.clone.waves_hbm.waves_ref, bf16[34,128,1024]{2,1,0:T(8,128)(2,1)} %state_hbm.7, bf16[34,128,1024]{2,1,0:T(8,128)(2,1)} %forcing_hbm.7), custom_call_target="tpu_custom_call" | custom-call | flops 12079595520 | bytes 4718592 | tf_op jit(solution)/shard_map/longitude_analysis/pallas_call | solution.py:212
  5.2 1.2 fusion.13
  6.4 2.4 collective-permute-start
  8.7 11.7 %longitude_analysis.5 = bf16[16,28,32,128]{3,2,1,0:T(8,128)(2,1)} custom-call(s32[1,512]{1,0:T(1,128)} %bitcast.122, bf16[2,2,256,512]{3,2,1,0:T(8,128)(2,1)} %constant.23.clone.waves_hbm.waves_ref, bf16[34,128,1024]{2,1,0:T(8,128)(2,1)} %state_hbm.7, bf16[34,128,1024]{2,1,0:T(8,128)(2,1)} %forcing_hbm.7, bf16[16,6,32,128]{3,2,1,0:T(8,128)(2,1)} %longitude_analysis.4.refs_0_), custom_call_target="tpu_custom_call" | custom-call | flops 56371445760 | bytes 22020096 | tf_op jit(solution)/shard_map/longitude_analysis/pallas_call | solution.py:212
  20.4 5.3 %all-to-all-start = ((bf16[16,896,128]{2,1,0:T(8,128)(2,1)}), bf16[16,896,128]{2,1,0:T(8,128)(2,1)}, u32[]{:S(2)}, u32[]{:S(2)}) async-start(bf16[16,896,128]{2,1,0:T(8,128)(2,1)} %bitcast.92), calls=%async_computation | async-start | bytes 7340032 | tf_op jit(solution)/shard_map/all_to_all | solution.py:485
  25.7 10.5 %longitude_analysis.6.refs_0_ = bf16[16,24,32,128]{3,2,1,0:T(8,128)(2,1)} custom-call(s32[1,512]{1,0:T(1,128)} %bitcast.123, bf16[2,2,256,512]{3,2,1,0:T(8,128)(2,1)} %constant.23.clone.waves_hbm.waves_ref, bf16[34,128,1024]{2,1,0:T(8,128)(2,1)} %state_hbm.7, bf16[34,128,1024]{2,1,0:T(8,128)(2,1)} %forcing_hbm.7), custom_call_target="tpu_custom_call" | custom-call | flops 48318382080 | bytes 18874368 | tf_op jit(solution)/shard_map/longitude_analysis/pallas_call | solution.py:212
  36.2 6.4 %longitude_analysis.7 = bf16[16,10,32,128]{3,2,1,0:T(8,128)(2,1)} custom-call(s32[1,512]{1,0:T(1,128)} %bitcast.124, bf16[2,2,256,512]{3,2,1,0:T(8,128)(2,1)} %constant.23.clone.waves_hbm.waves_ref, bf16[34,128,1024]{2,1,0:T(8,128)(2,1)} %state_hbm.7, bf16[34,128,1024]{2,1,0:T(8,128)(2,1)} %forcing_hbm.7, bf16[16,24,32,128]{3,2,1,0:T(8,128)(2,1)} %longitude_analysis.6.refs_0_), custom_call_target="tpu_custom_call" | custom-call | flops 20132659200 | bytes 7864320 | tf_op jit(solution)/shard_map/longitude_analysis/pallas_call | solution.py:212
  42.7 0.9 slice-done
  43.8 0.4 collective-permute-start.1
  44.2 1.7 collective-permute-done.1
  46.4 24.7 %collective-permute-done.2 = bf16[4,2,10,32,128]{4,3,2,0,1:T(8,128)(2,1)S(1)} collective-permute-done((bf16[4,2,10,32,128]{4,3,2,0,1:T(8,128)(2,1)S(1)}, bf16[4,2,10,32,128]{4,3,2,0,1:T(8,128)(2,1)S(1)}, u32[]{:S(2)}, u32[]{:S(2)}) %collective-permute-start.2) | collective-permute-done | bytes 655392 | tf_op jit(solution)/shard_map/ppermute | solution.py:491
  71.5 2.4 collective-permute-start.3
  73.9 27.3 %collective-permute-done.3 = bf16[2,4,10,32,128]{4,3,2,1,0:T(8,128)(2,1)S(1)} collective-permute-done((bf16[2,4,10,32,128]{4,3,2,1,0:T(8,128)(2,1)S(1)}, bf16[2,4,10,32,128]{4,3,2,1,0:T(8,128)(2,1)S(1)}, u32[]{:S(2)}, u32[]{:S(2)}) %collective-permute-start.3) | collective-permute-done | bytes 655392 | tf_op jit(solution)/shard_map/ppermute | solution.py:491
  101.8 0.8 slice_bitcast_fusion.10
  102.5 7.4 %collective-permute-start.4 = (bf16[1,8,4,32,128]{4,3,2,1,0:T(8,128)(2,1)S(1)}, bf16[1,8,4,32,128]{4,3,2,1,0:T(8,128)(2,1)}, u32[]{:S(2)}, u32[]{:S(2)}) collective-permute-start(bf16[1,8,4,32,128]{4,3,2,1,0:T(8,128)(2,1)S(1)} %get-tuple-element.32), channel_id=1, source_target_pairs={{0,8},{1,9},{2,10},{3,11},{4,12},{5,13},{6,14},{7,15},{8,0},{9,1},... | collective-permute-start | bytes 786440 | tf_op jit(solution)/shard_map/ppermute | solution.py:491
  109.9 0.9 slice.132
  110.8 1.3 dynamic_slice.3.waves_ref
  112.1 1.0 slice.129.refs_1_
  113.1 5.8 %all-to-all-start.2 = ((bf16[16,768,128]{2,1,0:T(8,128)(2,1)}), bf16[16,768,128]{2,1,0:T(8,128)(2,1)S(1)}, u32[]{:S(2)}, u32[]{:S(2)}) async-start(bf16[16,768,128]{2,1,0:T(8,128)(2,1)} %bitcast.94), calls=%async_computation.2 | async-start | bytes 6291456 | tf_op jit(solution)/shard_map/all_to_all | solution.py:485
  118.9 1.6 collective-permute-done.4
  120.5 15.4 %legendre_solve.2 = bf16[16,34,32,128]{3,2,1,0:T(8,128)(2,1)} custom-call(s32[32]{0:T(128)} %dynamic_slice.3.waves_ref, bf16[16,28,32,128]{3,2,1,0:T(8,128)(2,1)} %bitcast.2.refs_0_, bf16[16,6,32,128]{3,2,1,0:T(8,128)(2,1)} %slice.129.refs_1_, bf16[32,512,512]{2,1,0:T(8,128)(2,1)} %refs_6_.1, bf16[32,512,512]{2,1,0:T(8,128)(2,1)} %refs_6_.1, ...), custom_call_target="tpu_custom_call" | custom-call | flops 112944218112 | bytes 15204352 | tf_op jit(solution)/shard_map/legendre_solve/pallas_call | solution.py:368
  135.9 1.2 fusion.12
  137.1 0.6 collective-permute-start.5
  137.7 1.3 collective-permute-done.5
  139.1 0.7 collective-permute-start.6
  139.8 18.0 %collective-permute-done.6 = bf16[4,2,6,32,128]{4,3,2,0,1:T(8,128)(2,1)S(1)} collective-permute-done((bf16[4,2,6,32,128]{4,3,2,0,1:T(8,128)(2,1)S(1)}, bf16[4,2,6,32,128]{4,3,2,0,1:T(8,128)(2,1)S(1)}, u32[]{:S(2)}, u32[]{:S(2)}) %collective-permute-start.6) | collective-permute-done | bytes 393248 | tf_op jit(solution)/shard_map/ppermute | solution.py:491
  158.0 1.3 collective-permute-start.7
  159.4 21.1 %collective-permute-done.7 = bf16[2,4,6,32,128]{4,3,2,1,0:T(8,128)(2,1)S(1)} collective-permute-done((bf16[2,4,6,32,128]{4,3,2,1,0:T(8,128)(2,1)S(1)}, bf16[2,4,6,32,128]{4,3,2,1,0:T(8,128)(2,1)S(1)}, u32[]{:S(2)}, u32[]{:S(2)}) %collective-permute-start.7) | collective-permute-done | bytes 393248 | tf_op jit(solution)/shard_map/ppermute | solution.py:491
  180.6 0.8 slice_bitcast_fusion.5
  181.4 6.7 %collective-permute-start.8 = (bf16[1,8,6,32,128]{4,3,2,1,0:T(8,128)(2,1)S(1)}, bf16[1,8,6,32,128]{4,3,2,1,0:T(8,128)(2,1)}, u32[]{:S(2)}, u32[]{:S(2)}) collective-permute-start(bf16[1,8,6,32,128]{4,3,2,1,0:T(8,128)(2,1)S(1)} %get-tuple-element.23), channel_id=1, source_target_pairs={{0,8},{1,9},{2,10},{3,11},{4,12},{5,13},{6,14},{7,15},{8,0},{9,1},... | collective-permute-start | bytes 1179656 | tf_op jit(solution)/shard_map/ppermute | solution.py:491
  188.1 9.8 %all-to-all-done.2 = bf16[16,768,128]{2,1,0:T(8,128)(2,1)S(1)} async-done(((bf16[16,768,128]{2,1,0:T(8,128)(2,1)}), bf16[16,768,128]{2,1,0:T(8,128)(2,1)S(1)}, u32[]{:S(2)}, u32[]{:S(2)}) %all-to-all-start.2) | async-done | bytes 3145760 | tf_op jit(solution)/shard_map/all_to_all | solution.py:485
  197.9 1.7 copy-done
  199.7 6.2 %all-to-all-start.1 = ((bf16[16,1088,128]{2,1,0:T(8,128)(2,1)}), bf16[16,1088,128]{2,1,0:T(8,128)(2,1)}, u32[]{:S(2)}, u32[]{:S(2)}) async-start(bf16[16,1088,128]{2,1,0:T(8,128)(2,1)} %bitcast.91), calls=%async_computation.1 | async-start | bytes 8912896 | tf_op jit(solution)/shard_map/all_to_all | solution.py:485
  205.9 15.4 %legendre_solve.3 = (bf16[16,28,32,128]{3,2,1,0:T(8,128)(2,1)}, bf16[16,6,32,128]{3,2,1,0:T(8,128)(2,1)}) custom-call(s32[32]{0:T(128)} %dynamic_slice.3.waves_ref, bf16[16,24,32,128]{3,2,1,0:T(8,128)(2,1)} %bitcast.95, bf16[8,4,32,128]{3,2,1,0:T(8,128)(2,1)} %get-tuple-element.31.refs_1_, bf16[8,4,32,128]{3,2,1,0:T(8,128)(2,1)} %bitcast.20.refs_6_.refs_2_, ...), custom_call_target="tpu_custom_call" | custom-call | flops 112944218112 | bytes 15204352 | tf_op jit(solution)/shard_map/legendre_solve/pallas_call | solution.py:368
  221.3 1.2 fusion.11
  222.5 0.4 collective-permute-start.9
  222.9 1.4 collective-permute-done.9
  224.3 0.3 collective-permute-start.10
  224.7 16.4 %collective-permute-done.10 = bf16[4,2,6,32,128]{4,3,2,0,1:T(8,128)(2,1)S(1)} collective-permute-done((bf16[4,2,6,32,128]{4,3,2,0,1:T(8,128)(2,1)S(1)}, bf16[4,2,6,32,128]{4,3,2,0,1:T(8,128)(2,1)S(1)}, u32[]{:S(2)}, u32[]{:S(2)}) %collective-permute-start.10) | collective-permute-done | bytes 393248 | tf_op jit(solution)/shard_map/ppermute | solution.py:491
  241.3 7.1 %collective-permute-start.11 = (bf16[2,4,6,32,128]{4,3,2,1,0:T(8,128)(2,1)S(1)}, bf16[2,4,6,32,128]{4,3,2,1,0:T(8,128)(2,1)S(1)}, u32[]{:S(2)}, u32[]{:S(2)}) collective-permute-start(bf16[2,4,6,32,128]{4,3,2,1,0:T(8,128)(2,1)S(1)} %slice_bitcast_fusion.3), channel_id=1, source_target_pairs={{0,4},{1,5},{2,6},{3,7},{4,0},{5,1},{6,2},{7,3},{8,12},{9,13},{10,... | collective-permute-start | bytes 1179656 | tf_op jit(solution)/shard_map/ppermute | solution.py:491
  248.3 40.0 %collective-permute-done.11 = bf16[2,4,6,32,128]{4,3,2,1,0:T(8,128)(2,1)S(1)} collective-permute-done((bf16[2,4,6,32,128]{4,3,2,1,0:T(8,128)(2,1)S(1)}, bf16[2,4,6,32,128]{4,3,2,1,0:T(8,128)(2,1)S(1)}, u32[]{:S(2)}, u32[]{:S(2)}) %collective-permute-start.11) | collective-permute-done | bytes 393248 | tf_op jit(solution)/shard_map/ppermute | solution.py:491
  288.8 24.1 %all-to-all-done.1 = bf16[16,1088,128]{2,1,0:T(8,128)(2,1)} async-done(((bf16[16,1088,128]{2,1,0:T(8,128)(2,1)}), bf16[16,1088,128]{2,1,0:T(8,128)(2,1)}, u32[]{:S(2)}, u32[]{:S(2)}) %all-to-all-start.1) | async-done | bytes 4456480 | tf_op jit(solution)/shard_map/all_to_all | solution.py:485
  312.9 4.9 %all-to-all-start.3 = ((bf16[16,896,128]{2,1,0:T(8,128)(2,1)}), bf16[16,896,128]{2,1,0:T(8,128)(2,1)}, u32[]{:S(2)}, u32[]{:S(2)}) async-start(bf16[16,896,128]{2,1,0:T(8,128)(2,1)} %bitcast.93), calls=%async_computation.3 | async-start | bytes 7340032 | tf_op jit(solution)/shard_map/all_to_all | solution.py:485
  317.8 3.2 synthesis_rows.1.refs_2_
  321.0 0.9 pad_maximum_fusion.7.refs_1_
  321.9 4.5 %longitude_synthesis.2.refs_3_ = bf16[34,128,1024]{2,1,0:T(8,128)(2,1)} custom-call(bf16[16,34,32,128]{3,2,1,0:T(8,128)(2,1)} %bitcast.22.refs_0_, bf16[16,6,32,128]{3,2,1,0:T(8,128)(2,1)} %pad_maximum_fusion.7.refs_1_, bf16[2,2,256,512]{3,2,1,0:T(8,128)(2,1)} %synthesis_rows.1.refs_2_), custom_call_target="tpu_custom_call" | custom-call | flops 805306368 | bytes 3145728 | tf_op jit(solution)/shard_map/longitude_synthesis/pallas_call | solution.py:458
  326.4 73.2 %all-to-all-done.3 = bf16[16,896,128]{2,1,0:T(8,128)(2,1)} async-done(((bf16[16,896,128]{2,1,0:T(8,128)(2,1)}), bf16[16,896,128]{2,1,0:T(8,128)(2,1)}, u32[]{:S(2)}, u32[]{:S(2)}) %all-to-all-start.3) | async-done | bytes 3670048 | tf_op jit(solution)/shard_map/all_to_all | solution.py:485
  399.6 10.1 %longitude_synthesis.3 = bf16[34,128,1024]{2,1,0:T(8,128)(2,1)} custom-call(bf16[16,34,32,128]{3,2,1,0:T(8,128)(2,1)} %bitcast.22.refs_0_, bf16[16,28,32,128]{3,2,1,0:T(8,128)(2,1)} %bitcast.41.refs_1_, bf16[2,2,256,512]{3,2,1,0:T(8,128)(2,1)} %synthesis_rows.1.refs_2_, bf16[34,128,1024]{2,1,0:T(8,128)(2,1)} %longitude_synthesis.2.refs_3_), custom_call_target="tpu_custom_call", output_to_operand_aliasing={{}: (3, {})} | custom-call | flops 3758096384 | bytes 14680064 | tf_op jit(solution)/shard_map/longitude_synthesis/pallas_call | solution.py:458
  (32 shorter events, 2.7 us)
Async XLA Ops:
  6.4 36.3 %collective-permute-start = (bf16[1,8,6,32,128]{4,3,2,1,0:T(8,128)(2,1)S(1)}, bf16[1,8,6,32,128]{4,3,2,1,0:T(8,128)(2,1)S(1)}, u32[]{:S(2)}, u32[]{:S(2)}) collective-permute-start(bf16[1,8,6,32,128]{4,3,2,1,0:T(8,128)(2,1)S(1)} %get-tuple-element.30), channel_id=1, source_target_pairs={{0,8},{1,9},{2,10},{3,11},{4,12},{5,13},{6,14},{7,15},{8,0},{9,1},... | collective-permute-start | bytes 1179656 | tf_op jit(solution)/shard_map/ppermute | solution.py:491
  20.4 92.7 %all-to-all-start = ((bf16[16,896,128]{2,1,0:T(8,128)(2,1)}), bf16[16,896,128]{2,1,0:T(8,128)(2,1)}, u32[]{:S(2)}, u32[]{:S(2)}) async-start(bf16[16,896,128]{2,1,0:T(8,128)(2,1)} %bitcast.92), calls=%async_computation | async-start | bytes 7340032 | tf_op jit(solution)/shard_map/all_to_all | solution.py:485
  42.6 1.0 slice-start
  43.8 2.2 collective-permute-start.1
  46.1 25.0 %collective-permute-start.2 = (bf16[4,2,10,32,128]{4,3,2,0,1:T(8,128)(2,1)S(1)}, bf16[4,2,10,32,128]{4,3,2,0,1:T(8,128)(2,1)S(1)}, u32[]{:S(2)}, u32[]{:S(2)}) collective-permute-start(bf16[4,2,10,32,128]{4,3,2,0,1:T(8,128)(2,1)S(1)} %get-tuple-element.14), channel_id=1, source_target_pairs={{0,2},{1,3},{2,0},{3,1},{4,6},{5,7},{6,4},{7,5},{8,10},{9,11},{10,... | collective-permute-start | bytes 1966088 | tf_op jit(solution)/shard_map/ppermute | solution.py:491
  71.5 29.7 %collective-permute-start.3 = (bf16[2,4,10,32,128]{4,3,2,1,0:T(8,128)(2,1)S(1)}, bf16[2,4,10,32,128]{4,3,2,1,0:T(8,128)(2,1)S(1)}, u32[]{:S(2)}, u32[]{:S(2)}) collective-permute-start(bf16[2,4,10,32,128]{4,3,2,1,0:T(8,128)(2,1)S(1)} %slice_bitcast_fusion), channel_id=1, source_target_pairs={{0,4},{1,5},{2,6},{3,7},{4,0},{5,1},{6,2},{7,3},{8,12},{9,13},{10,... | collective-permute-start | bytes 1966088 | tf_op jit(solution)/shard_map/ppermute | solution.py:491
  101.7 8.2 %copy-start.1 = (bf16[16,10,32,128]{3,2,1,0:T(8,128)(2,1)S(1)}, bf16[16,10,32,128]{3,2,1,0:T(8,128)(2,1)}, u32[]{:S(2)}) copy-start(bf16[16,10,32,128]{3,2,1,0:T(8,128)(2,1)} %longitude_analysis.7) | copy-start | bytes 3932164
  102.5 18.0 %collective-permute-start.4 = (bf16[1,8,4,32,128]{4,3,2,1,0:T(8,128)(2,1)S(1)}, bf16[1,8,4,32,128]{4,3,2,1,0:T(8,128)(2,1)}, u32[]{:S(2)}, u32[]{:S(2)}) collective-permute-start(bf16[1,8,4,32,128]{4,3,2,1,0:T(8,128)(2,1)S(1)} %get-tuple-element.32), channel_id=1, source_target_pairs={{0,8},{1,9},{2,10},{3,11},{4,12},{5,13},{6,14},{7,15},{8,0},{9,1},... | collective-permute-start | bytes 786440 | tf_op jit(solution)/shard_map/ppermute | solution.py:491
  113.1 84.8 %all-to-all-start.2 = ((bf16[16,768,128]{2,1,0:T(8,128)(2,1)}), bf16[16,768,128]{2,1,0:T(8,128)(2,1)S(1)}, u32[]{:S(2)}, u32[]{:S(2)}) async-start(bf16[16,768,128]{2,1,0:T(8,128)(2,1)} %bitcast.94), calls=%async_computation.2 | async-start | bytes 6291456 | tf_op jit(solution)/shard_map/all_to_all | solution.py:485
  137.1 2.0 collective-permute-start.5
  139.1 18.7 %collective-permute-start.6 = (bf16[4,2,6,32,128]{4,3,2,0,1:T(8,128)(2,1)S(1)}, bf16[4,2,6,32,128]{4,3,2,0,1:T(8,128)(2,1)S(1)}, u32[]{:S(2)}, u32[]{:S(2)}) collective-permute-start(bf16[4,2,6,32,128]{4,3,2,0,1:T(8,128)(2,1)S(1)} %get-tuple-element.26), channel_id=1, source_target_pairs={{0,2},{1,3},{2,0},{3,1},{4,6},{5,7},{6,4},{7,5},{8,10},{9,11},{10,... | collective-permute-start | bytes 1179656 | tf_op jit(solution)/shard_map/ppermute | solution.py:491
  158.0 22.4 %collective-permute-start.7 = (bf16[2,4,6,32,128]{4,3,2,1,0:T(8,128)(2,1)S(1)}, bf16[2,4,6,32,128]{4,3,2,1,0:T(8,128)(2,1)S(1)}, u32[]{:S(2)}, u32[]{:S(2)}) collective-permute-start(bf16[2,4,6,32,128]{4,3,2,1,0:T(8,128)(2,1)S(1)} %slice_bitcast_fusion.7), channel_id=1, source_target_pairs={{0,4},{1,5},{2,6},{3,7},{4,0},{5,1},{6,2},{7,3},{8,12},{9,13},{10,... | collective-permute-start | bytes 1179656 | tf_op jit(solution)/shard_map/ppermute | solution.py:491
  181.4 24.4 %collective-permute-start.8 = (bf16[1,8,6,32,128]{4,3,2,1,0:T(8,128)(2,1)S(1)}, bf16[1,8,6,32,128]{4,3,2,1,0:T(8,128)(2,1)}, u32[]{:S(2)}, u32[]{:S(2)}) collective-permute-start(bf16[1,8,6,32,128]{4,3,2,1,0:T(8,128)(2,1)S(1)} %get-tuple-element.23), channel_id=1, source_target_pairs={{0,8},{1,9},{2,10},{3,11},{4,12},{5,13},{6,14},{7,15},{8,0},{9,1},... | collective-permute-start | bytes 1179656 | tf_op jit(solution)/shard_map/ppermute | solution.py:491
  197.9 1.7 copy-start
  199.7 113.2 %all-to-all-start.1 = ((bf16[16,1088,128]{2,1,0:T(8,128)(2,1)}), bf16[16,1088,128]{2,1,0:T(8,128)(2,1)}, u32[]{:S(2)}, u32[]{:S(2)}) async-start(bf16[16,1088,128]{2,1,0:T(8,128)(2,1)} %bitcast.91), calls=%async_computation.1 | async-start | bytes 8912896 | tf_op jit(solution)/shard_map/all_to_all | solution.py:485
  222.5 1.8 collective-permute-start.9
  224.3 16.8 %collective-permute-start.10 = (bf16[4,2,6,32,128]{4,3,2,0,1:T(8,128)(2,1)S(1)}, bf16[4,2,6,32,128]{4,3,2,0,1:T(8,128)(2,1)S(1)}, u32[]{:S(2)}, u32[]{:S(2)}) collective-permute-start(bf16[4,2,6,32,128]{4,3,2,0,1:T(8,128)(2,1)S(1)} %get-tuple-element.20), channel_id=1, source_target_pairs={{0,2},{1,3},{2,0},{3,1},{4,6},{5,7},{6,4},{7,5},{8,10},{9,11},{10,... | collective-permute-start | bytes 1179656 | tf_op jit(solution)/shard_map/ppermute | solution.py:491
  241.3 47.1 %collective-permute-start.11 = (bf16[2,4,6,32,128]{4,3,2,1,0:T(8,128)(2,1)S(1)}, bf16[2,4,6,32,128]{4,3,2,1,0:T(8,128)(2,1)S(1)}, u32[]{:S(2)}, u32[]{:S(2)}) collective-permute-start(bf16[2,4,6,32,128]{4,3,2,1,0:T(8,128)(2,1)S(1)} %slice_bitcast_fusion.3), channel_id=1, source_target_pairs={{0,4},{1,5},{2,6},{3,7},{4,0},{5,1},{6,2},{7,3},{8,12},{9,13},{10,... | collective-permute-start | bytes 1179656 | tf_op jit(solution)/shard_map/ppermute | solution.py:491
  288.6 32.4 %collective-permute-start.12 = (bf16[1,8,6,32,128]{4,3,2,1,0:T(8,128)(2,1)S(1)}, bf16[1,8,6,32,128]{4,3,2,1,0:T(8,128)(2,1)S(1)}, u32[]{:S(2)}, u32[]{:S(2)}) collective-permute-start(bf16[1,8,6,32,128]{4,3,2,1,0:T(8,128)(2,1)S(1)} %get-tuple-element.18), channel_id=1, source_target_pairs={{0,8},{1,9},{2,10},{3,11},{4,12},{5,13},{6,14},{7,15},{8,0},{9,1},... | collective-permute-start | bytes 1179656 | tf_op jit(solution)/shard_map/ppermute | solution.py:491
  312.9 86.7 %all-to-all-start.3 = ((bf16[16,896,128]{2,1,0:T(8,128)(2,1)}), bf16[16,896,128]{2,1,0:T(8,128)(2,1)}, u32[]{:S(2)}, u32[]{:S(2)}) async-start(bf16[16,896,128]{2,1,0:T(8,128)(2,1)} %bitcast.93), calls=%async_computation.3 | async-start | bytes 7340032 | tf_op jit(solution)/shard_map/all_to_all | solution.py:485

commit v8 on v7

--- a/solution.py
+++ b/solution.py
@@ -451,7 +451,7 @@
     owners, _, rows, lats = parts[0].shape
     lon_count = 2 * synth.shape[-1]
     chunks = len(pieces)
-    count = 2 if (end - begin) % 2 == 0 else 1
+    count = next(count for count in (4, 2, 1) if (end - begin) % count == 0)
     steps = (end - begin) // count
     given = [] if before is None else [before]
     anywhere = pl.BlockSpec(memory_space=pl.ANY)

time: 411 us -> 410 us (level)
  no operation moved by 1% of the time
where the time goes in v8:
time: 410 us; the launch traced here: 409 us
  waiting for transfers between devices  261 us (64%)
  Pallas kernels  81 us (20%)
  starting transfers between devices  52.6 us (13%)
  local copies, waits for them, and re-layouts  11.9 us (3%)
    ppermute x13, waiting for transfers between devices, give(): lax.ppermute(halves[:, 1], OWNERS, [(o, o ^ bit) for o in range(owners)])  154 us
    all_to_all x4, waiting for transfers between devices, exchange(): return lax.all_to_all(flat, OWNERS, 0, 0, tiled=True).reshape(part.shape)  107 us
    pallas_call x4, Pallas kernels, run_analysis(): pl.pallas_call(functools.partial(analysis_kernel, owners, chunks, k, begi...  33.7 us
    pallas_call x2, Pallas kernels, run_columns(): pl.pallas_call(functools.partial(column_kernel, owners, bands, k, pieces_...  30.8 us
    ppermute x13, starting transfers between devices, give(): lax.ppermute(halves[:, 1], OWNERS, [(o, o ^ bit) for o in range(owners)])  30.4 us
    all_to_all x4, starting transfers between devices, exchange(): return lax.all_to_all(flat, OWNERS, 0, 0, tiled=True).reshape(part.shape)  22.2 us
    pallas_call x2, Pallas kernels, run_synthesis(): pl.pallas_call(functools.partial(synthesis_kernel, owners, begin, pieces)...  13.3 us
  transfers between devices with their start and end apart: 17, of which 13 were waited for; matrix products, arithmetic and copies ran while one was open for 2% of the time, Pallas kernels for 16%

profile of v8, /device:TPU:11, one launch (start us, length us, event | category | flops | bytes accessed | tf_op | source)
XLA Modules:
  0.0 408.6 jit_solution(4657763748125085062)
XLA Ops:
  0.0 5.2 %longitude_analysis.4.refs_0_ = bf16[16,6,32,128]{3,2,1,0:T(8,128)(2,1)} custom-call(s32[1,512]{1,0:T(1,128)} %bitcast.121, bf16[2,2,256,512]{3,2,1,0:T(8,128)(2,1)} %constant.23.clone.waves_hbm.waves_ref, bf16[34,128,1024]{2,1,0:T(8,128)(2,1)} %state_hbm.7, bf16[34,128,1024]{2,1,0:T(8,128)(2,1)} %forcing_hbm.7), custom_call_target="tpu_custom_call" | custom-call | flops 12079595520 | bytes 4718592 | tf_op jit(solution)/shard_map/longitude_analysis/pallas_call | solution.py:212
  5.2 1.2 fusion.13
  6.4 2.4 collective-permute-start
  8.7 11.7 %longitude_analysis.5 = bf16[16,28,32,128]{3,2,1,0:T(8,128)(2,1)} custom-call(s32[1,512]{1,0:T(1,128)} %bitcast.122, bf16[2,2,256,512]{3,2,1,0:T(8,128)(2,1)} %constant.23.clone.waves_hbm.waves_ref, bf16[34,128,1024]{2,1,0:T(8,128)(2,1)} %state_hbm.7, bf16[34,128,1024]{2,1,0:T(8,128)(2,1)} %forcing_hbm.7, bf16[16,6,32,128]{3,2,1,0:T(8,128)(2,1)} %longitude_analysis.4.refs_0_), custom_call_target="tpu_custom_call" | custom-call | flops 56371445760 | bytes 22020096 | tf_op jit(solution)/shard_map/longitude_analysis/pallas_call | solution.py:212
  20.4 5.3 %all-to-all-start = ((bf16[16,896,128]{2,1,0:T(8,128)(2,1)}), bf16[16,896,128]{2,1,0:T(8,128)(2,1)}, u32[]{:S(2)}, u32[]{:S(2)}) async-start(bf16[16,896,128]{2,1,0:T(8,128)(2,1)} %bitcast.92), calls=%async_computation | async-start | bytes 7340032 | tf_op jit(solution)/shard_map/all_to_all | solution.py:485
  25.7 10.5 %longitude_analysis.6.refs_0_ = bf16[16,24,32,128]{3,2,1,0:T(8,128)(2,1)} custom-call(s32[1,512]{1,0:T(1,128)} %bitcast.123, bf16[2,2,256,512]{3,2,1,0:T(8,128)(2,1)} %constant.23.clone.waves_hbm.waves_ref, bf16[34,128,1024]{2,1,0:T(8,128)(2,1)} %state_hbm.7, bf16[34,128,1024]{2,1,0:T(8,128)(2,1)} %forcing_hbm.7), custom_call_target="tpu_custom_call" | custom-call | flops 48318382080 | bytes 18874368 | tf_op jit(solution)/shard_map/longitude_analysis/pallas_call | solution.py:212
  36.2 6.4 %longitude_analysis.7 = bf16[16,10,32,128]{3,2,1,0:T(8,128)(2,1)} custom-call(s32[1,512]{1,0:T(1,128)} %bitcast.124, bf16[2,2,256,512]{3,2,1,0:T(8,128)(2,1)} %constant.23.clone.waves_hbm.waves_ref, bf16[34,128,1024]{2,1,0:T(8,128)(2,1)} %state_hbm.7, bf16[34,128,1024]{2,1,0:T(8,128)(2,1)} %forcing_hbm.7, bf16[16,24,32,128]{3,2,1,0:T(8,128)(2,1)} %longitude_analysis.6.refs_0_), custom_call_target="tpu_custom_call" | custom-call | flops 20132659200 | bytes 7864320 | tf_op jit(solution)/shard_map/longitude_analysis/pallas_call | solution.py:212
  42.7 0.9 slice-done
  43.8 0.4 collective-permute-start.1
  44.2 1.7 collective-permute-done.1
  46.4 24.7 %collective-permute-done.2 = bf16[4,2,10,32,128]{4,3,2,0,1:T(8,128)(2,1)S(1)} collective-permute-done((bf16[4,2,10,32,128]{4,3,2,0,1:T(8,128)(2,1)S(1)}, bf16[4,2,10,32,128]{4,3,2,0,1:T(8,128)(2,1)S(1)}, u32[]{:S(2)}, u32[]{:S(2)}) %collective-permute-start.2) | collective-permute-done | bytes 655392 | tf_op jit(solution)/shard_map/ppermute | solution.py:491
  71.5 2.4 collective-permute-start.3
  73.9 27.3 %collective-permute-done.3 = bf16[2,4,10,32,128]{4,3,2,1,0:T(8,128)(2,1)S(1)} collective-permute-done((bf16[2,4,10,32,128]{4,3,2,1,0:T(8,128)(2,1)S(1)}, bf16[2,4,10,32,128]{4,3,2,1,0:T(8,128)(2,1)S(1)}, u32[]{:S(2)}, u32[]{:S(2)}) %collective-permute-start.3) | collective-permute-done | bytes 655392 | tf_op jit(solution)/shard_map/ppermute | solution.py:491
  101.8 0.8 slice_bitcast_fusion.10
  102.5 7.4 %collective-permute-start.4 = (bf16[1,8,4,32,128]{4,3,2,1,0:T(8,128)(2,1)S(1)}, bf16[1,8,4,32,128]{4,3,2,1,0:T(8,128)(2,1)}, u32[]{:S(2)}, u32[]{:S(2)}) collective-permute-start(bf16[1,8,4,32,128]{4,3,2,1,0:T(8,128)(2,1)S(1)} %get-tuple-element.32), channel_id=1, source_target_pairs={{0,8},{1,9},{2,10},{3,11},{4,12},{5,13},{6,14},{7,15},{8,0},{9,1},... | collective-permute-start | bytes 786440 | tf_op jit(solution)/shard_map/ppermute | solution.py:491
  109.9 0.9 slice.132
  110.8 1.3 dynamic_slice.3.waves_ref
  112.1 1.0 slice.129.refs_1_
  113.1 5.8 %all-to-all-start.2 = ((bf16[16,768,128]{2,1,0:T(8,128)(2,1)}), bf16[16,768,128]{2,1,0:T(8,128)(2,1)S(1)}, u32[]{:S(2)}, u32[]{:S(2)}) async-start(bf16[16,768,128]{2,1,0:T(8,128)(2,1)} %bitcast.94), calls=%async_computation.2 | async-start | bytes 6291456 | tf_op jit(solution)/shard_map/all_to_all | solution.py:485
  118.9 1.6 collective-permute-done.4
  120.5 15.4 %legendre_solve.2 = bf16[16,34,32,128]{3,2,1,0:T(8,128)(2,1)} custom-call(s32[32]{0:T(128)} %dynamic_slice.3.waves_ref, bf16[16,28,32,128]{3,2,1,0:T(8,128)(2,1)} %bitcast.2.refs_0_, bf16[16,6,32,128]{3,2,1,0:T(8,128)(2,1)} %slice.129.refs_1_, bf16[32,512,512]{2,1,0:T(8,128)(2,1)} %refs_6_.1, bf16[32,512,512]{2,1,0:T(8,128)(2,1)} %refs_6_.1, ...), custom_call_target="tpu_custom_call" | custom-call | flops 112944218112 | bytes 15204352 | tf_op jit(solution)/shard_map/legendre_solve/pallas_call | solution.py:368
  135.9 1.2 fusion.12
  137.1 0.6 collective-permute-start.5
  137.7 1.3 collective-permute-done.5
  139.1 0.7 collective-permute-start.6
  139.8 18.0 %collective-permute-done.6 = bf16[4,2,6,32,128]{4,3,2,0,1:T(8,128)(2,1)S(1)} collective-permute-done((bf16[4,2,6,32,128]{4,3,2,0,1:T(8,128)(2,1)S(1)}, bf16[4,2,6,32,128]{4,3,2,0,1:T(8,128)(2,1)S(1)}, u32[]{:S(2)}, u32[]{:S(2)}) %collective-permute-start.6) | collective-permute-done | bytes 393248 | tf_op jit(solution)/shard_map/ppermute | solution.py:491
  158.0 1.3 collective-permute-start.7
  159.4 21.1 %collective-permute-done.7 = bf16[2,4,6,32,128]{4,3,2,1,0:T(8,128)(2,1)S(1)} collective-permute-done((bf16[2,4,6,32,128]{4,3,2,1,0:T(8,128)(2,1)S(1)}, bf16[2,4,6,32,128]{4,3,2,1,0:T(8,128)(2,1)S(1)}, u32[]{:S(2)}, u32[]{:S(2)}) %collective-permute-start.7) | collective-permute-done | bytes 393248 | tf_op jit(solution)/shard_map/ppermute | solution.py:491
  180.6 0.8 slice_bitcast_fusion.5
  181.4 6.7 %collective-permute-start.8 = (bf16[1,8,6,32,128]{4,3,2,1,0:T(8,128)(2,1)S(1)}, bf16[1,8,6,32,128]{4,3,2,1,0:T(8,128)(2,1)}, u32[]{:S(2)}, u32[]{:S(2)}) collective-permute-start(bf16[1,8,6,32,128]{4,3,2,1,0:T(8,128)(2,1)S(1)} %get-tuple-element.23), channel_id=1, source_target_pairs={{0,8},{1,9},{2,10},{3,11},{4,12},{5,13},{6,14},{7,15},{8,0},{9,1},... | collective-permute-start | bytes 1179656 | tf_op jit(solution)/shard_map/ppermute | solution.py:491
  188.1 9.8 %all-to-all-done.2 = bf16[16,768,128]{2,1,0:T(8,128)(2,1)S(1)} async-done(((bf16[16,768,128]{2,1,0:T(8,128)(2,1)}), bf16[16,768,128]{2,1,0:T(8,128)(2,1)S(1)}, u32[]{:S(2)}, u32[]{:S(2)}) %all-to-all-start.2) | async-done | bytes 3145760 | tf_op jit(solution)/shard_map/all_to_all | solution.py:485
  197.9 1.7 copy-done
  199.7 6.2 %all-to-all-start.1 = ((bf16[16,1088,128]{2,1,0:T(8,128)(2,1)}), bf16[16,1088,128]{2,1,0:T(8,128)(2,1)}, u32[]{:S(2)}, u32[]{:S(2)}) async-start(bf16[16,1088,128]{2,1,0:T(8,128)(2,1)} %bitcast.91), calls=%async_computation.1 | async-start | bytes 8912896 | tf_op jit(solution)/shard_map/all_to_all | solution.py:485
  205.9 15.4 %legendre_solve.3 = (bf16[16,28,32,128]{3,2,1,0:T(8,128)(2,1)}, bf16[16,6,32,128]{3,2,1,0:T(8,128)(2,1)}) custom-call(s32[32]{0:T(128)} %dynamic_slice.3.waves_ref, bf16[16,24,32,128]{3,2,1,0:T(8,128)(2,1)} %bitcast.95, bf16[8,4,32,128]{3,2,1,0:T(8,128)(2,1)} %get-tuple-element.31.refs_1_, bf16[8,4,32,128]{3,2,1,0:T(8,128)(2,1)} %bitcast.20.refs_6_.refs_2_, ...), custom_call_target="tpu_custom_call" | custom-call | flops 112944218112 | bytes 15204352 | tf_op jit(solution)/shard_map/legendre_solve/pallas_call | solution.py:368
  221.3 1.2 fusion.11
  222.5 0.4 collective-permute-start.9
  222.9 1.4 collective-permute-done.9
  224.3 0.3 collective-permute-start.10
  224.7 16.4 %collective-permute-done.10 = bf16[4,2,6,32,128]{4,3,2,0,1:T(8,128)(2,1)S(1)} collective-permute-done((bf16[4,2,6,32,128]{4,3,2,0,1:T(8,128)(2,1)S(1)}, bf16[4,2,6,32,128]{4,3,2,0,1:T(8,128)(2,1)S(1)}, u32[]{:S(2)}, u32[]{:S(2)}) %collective-permute-start.10) | collective-permute-done | bytes 393248 | tf_op jit(solution)/shard_map/ppermute | solution.py:491
  241.3 7.1 %collective-permute-start.11 = (bf16[2,4,6,32,128]{4,3,2,1,0:T(8,128)(2,1)S(1)}, bf16[2,4,6,32,128]{4,3,2,1,0:T(8,128)(2,1)S(1)}, u32[]{:S(2)}, u32[]{:S(2)}) collective-permute-start(bf16[2,4,6,32,128]{4,3,2,1,0:T(8,128)(2,1)S(1)} %slice_bitcast_fusion.3), channel_id=1, source_target_pairs={{0,4},{1,5},{2,6},{3,7},{4,0},{5,1},{6,2},{7,3},{8,12},{9,13},{10,... | collective-permute-start | bytes 1179656 | tf_op jit(solution)/shard_map/ppermute | solution.py:491
  248.3 40.0 %collective-permute-done.11 = bf16[2,4,6,32,128]{4,3,2,1,0:T(8,128)(2,1)S(1)} collective-permute-done((bf16[2,4,6,32,128]{4,3,2,1,0:T(8,128)(2,1)S(1)}, bf16[2,4,6,32,128]{4,3,2,1,0:T(8,128)(2,1)S(1)}, u32[]{:S(2)}, u32[]{:S(2)}) %collective-permute-start.11) | collective-permute-done | bytes 393248 | tf_op jit(solution)/shard_map/ppermute | solution.py:491
  288.8 24.1 %all-to-all-done.1 = bf16[16,1088,128]{2,1,0:T(8,128)(2,1)} async-done(((bf16[16,1088,128]{2,1,0:T(8,128)(2,1)}), bf16[16,1088,128]{2,1,0:T(8,128)(2,1)}, u32[]{:S(2)}, u32[]{:S(2)}) %all-to-all-start.1) | async-done | bytes 4456480 | tf_op jit(solution)/shard_map/all_to_all | solution.py:485
  312.9 4.9 %all-to-all-start.3 = ((bf16[16,896,128]{2,1,0:T(8,128)(2,1)}), bf16[16,896,128]{2,1,0:T(8,128)(2,1)}, u32[]{:S(2)}, u32[]{:S(2)}) async-start(bf16[16,896,128]{2,1,0:T(8,128)(2,1)} %bitcast.93), calls=%async_computation.3 | async-start | bytes 7340032 | tf_op jit(solution)/shard_map/all_to_all | solution.py:485
  317.8 3.2 synthesis_rows.1.refs_2_
  321.0 0.9 pad_maximum_fusion.7.refs_1_
  321.9 4.5 %longitude_synthesis.2.refs_3_ = bf16[34,128,1024]{2,1,0:T(8,128)(2,1)} custom-call(bf16[16,34,32,128]{3,2,1,0:T(8,128)(2,1)} %bitcast.22.refs_0_, bf16[16,6,32,128]{3,2,1,0:T(8,128)(2,1)} %pad_maximum_fusion.7.refs_1_, bf16[2,2,256,512]{3,2,1,0:T(8,128)(2,1)} %synthesis_rows.1.refs_2_), custom_call_target="tpu_custom_call" | custom-call | flops 805306368 | bytes 3145728 | tf_op jit(solution)/shard_map/longitude_synthesis/pallas_call | solution.py:458
  326.4 73.2 %all-to-all-done.3 = bf16[16,896,128]{2,1,0:T(8,128)(2,1)} async-done(((bf16[16,896,128]{2,1,0:T(8,128)(2,1)}), bf16[16,896,128]{2,1,0:T(8,128)(2,1)}, u32[]{:S(2)}, u32[]{:S(2)}) %all-to-all-start.3) | async-done | bytes 3670048 | tf_op jit(solution)/shard_map/all_to_all | solution.py:485
  399.6 8.8 %longitude_synthesis.3 = bf16[34,128,1024]{2,1,0:T(8,128)(2,1)} custom-call(bf16[16,34,32,128]{3,2,1,0:T(8,128)(2,1)} %bitcast.22.refs_0_, bf16[16,28,32,128]{3,2,1,0:T(8,128)(2,1)} %bitcast.41.refs_1_, bf16[2,2,256,512]{3,2,1,0:T(8,128)(2,1)} %synthesis_rows.1.refs_2_, bf16[34,128,1024]{2,1,0:T(8,128)(2,1)} %longitude_synthesis.2.refs_3_), custom_call_target="tpu_custom_call", output_to_operand_aliasing={{}: (3, {})} | custom-call | flops 3758096384 | bytes 14680064 | tf_op jit(solution)/shard_map/longitude_synthesis/pallas_call | solution.py:458
  (32 shorter events, 2.7 us)
Async XLA Ops:
  6.4 36.3 %collective-permute-start = (bf16[1,8,6,32,128]{4,3,2,1,0:T(8,128)(2,1)S(1)}, bf16[1,8,6,32,128]{4,3,2,1,0:T(8,128)(2,1)S(1)}, u32[]{:S(2)}, u32[]{:S(2)}) collective-permute-start(bf16[1,8,6,32,128]{4,3,2,1,0:T(8,128)(2,1)S(1)} %get-tuple-element.30), channel_id=1, source_target_pairs={{0,8},{1,9},{2,10},{3,11},{4,12},{5,13},{6,14},{7,15},{8,0},{9,1},... | collective-permute-start | bytes 1179656 | tf_op jit(solution)/shard_map/ppermute | solution.py:491
  20.4 92.7 %all-to-all-start = ((bf16[16,896,128]{2,1,0:T(8,128)(2,1)}), bf16[16,896,128]{2,1,0:T(8,128)(2,1)}, u32[]{:S(2)}, u32[]{:S(2)}) async-start(bf16[16,896,128]{2,1,0:T(8,128)(2,1)} %bitcast.92), calls=%async_computation | async-start | bytes 7340032 | tf_op jit(solution)/shard_map/all_to_all | solution.py:485
  42.6 1.0 slice-start
  43.8 2.2 collective-permute-start.1
  46.1 25.0 %collective-permute-start.2 = (bf16[4,2,10,32,128]{4,3,2,0,1:T(8,128)(2,1)S(1)}, bf16[4,2,10,32,128]{4,3,2,0,1:T(8,128)(2,1)S(1)}, u32[]{:S(2)}, u32[]{:S(2)}) collective-permute-start(bf16[4,2,10,32,128]{4,3,2,0,1:T(8,128)(2,1)S(1)} %get-tuple-element.14), channel_id=1, source_target_pairs={{0,2},{1,3},{2,0},{3,1},{4,6},{5,7},{6,4},{7,5},{8,10},{9,11},{10,... | collective-permute-start | bytes 1966088 | tf_op jit(solution)/shard_map/ppermute | solution.py:491
  71.5 29.7 %collective-permute-start.3 = (bf16[2,4,10,32,128]{4,3,2,1,0:T(8,128)(2,1)S(1)}, bf16[2,4,10,32,128]{4,3,2,1,0:T(8,128)(2,1)S(1)}, u32[]{:S(2)}, u32[]{:S(2)}) collective-permute-start(bf16[2,4,10,32,128]{4,3,2,1,0:T(8,128)(2,1)S(1)} %slice_bitcast_fusion), channel_id=1, source_target_pairs={{0,4},{1,5},{2,6},{3,7},{4,0},{5,1},{6,2},{7,3},{8,12},{9,13},{10,... | collective-permute-start | bytes 1966088 | tf_op jit(solution)/shard_map/ppermute | solution.py:491
  101.7 8.2 %copy-start.1 = (bf16[16,10,32,128]{3,2,1,0:T(8,128)(2,1)S(1)}, bf16[16,10,32,128]{3,2,1,0:T(8,128)(2,1)}, u32[]{:S(2)}) copy-start(bf16[16,10,32,128]{3,2,1,0:T(8,128)(2,1)} %longitude_analysis.7) | copy-start | bytes 3932164
  102.5 18.0 %collective-permute-start.4 = (bf16[1,8,4,32,128]{4,3,2,1,0:T(8,128)(2,1)S(1)}, bf16[1,8,4,32,128]{4,3,2,1,0:T(8,128)(2,1)}, u32[]{:S(2)}, u32[]{:S(2)}) collective-permute-start(bf16[1,8,4,32,128]{4,3,2,1,0:T(8,128)(2,1)S(1)} %get-tuple-element.32), channel_id=1, source_target_pairs={{0,8},{1,9},{2,10},{3,11},{4,12},{5,13},{6,14},{7,15},{8,0},{9,1},... | collective-permute-start | bytes 786440 | tf_op jit(solution)/shard_map/ppermute | solution.py:491
  113.1 84.8 %all-to-all-start.2 = ((bf16[16,768,128]{2,1,0:T(8,128)(2,1)}), bf16[16,768,128]{2,1,0:T(8,128)(2,1)S(1)}, u32[]{:S(2)}, u32[]{:S(2)}) async-start(bf16[16,768,128]{2,1,0:T(8,128)(2,1)} %bitcast.94), calls=%async_computation.2 | async-start | bytes 6291456 | tf_op jit(solution)/shard_map/all_to_all | solution.py:485
  137.1 2.0 collective-permute-start.5
  139.1 18.7 %collective-permute-start.6 = (bf16[4,2,6,32,128]{4,3,2,0,1:T(8,128)(2,1)S(1)}, bf16[4,2,6,32,128]{4,3,2,0,1:T(8,128)(2,1)S(1)}, u32[]{:S(2)}, u32[]{:S(2)}) collective-permute-start(bf16[4,2,6,32,128]{4,3,2,0,1:T(8,128)(2,1)S(1)} %get-tuple-element.26), channel_id=1, source_target_pairs={{0,2},{1,3},{2,0},{3,1},{4,6},{5,7},{6,4},{7,5},{8,10},{9,11},{10,... | collective-permute-start | bytes 1179656 | tf_op jit(solution)/shard_map/ppermute | solution.py:491
  158.0 22.4 %collective-permute-start.7 = (bf16[2,4,6,32,128]{4,3,2,1,0:T(8,128)(2,1)S(1)}, bf16[2,4,6,32,128]{4,3,2,1,0:T(8,128)(2,1)S(1)}, u32[]{:S(2)}, u32[]{:S(2)}) collective-permute-start(bf16[2,4,6,32,128]{4,3,2,1,0:T(8,128)(2,1)S(1)} %slice_bitcast_fusion.7), channel_id=1, source_target_pairs={{0,4},{1,5},{2,6},{3,7},{4,0},{5,1},{6,2},{7,3},{8,12},{9,13},{10,... | collective-permute-start | bytes 1179656 | tf_op jit(solution)/shard_map/ppermute | solution.py:491
  181.4 24.4 %collective-permute-start.8 = (bf16[1,8,6,32,128]{4,3,2,1,0:T(8,128)(2,1)S(1)}, bf16[1,8,6,32,128]{4,3,2,1,0:T(8,128)(2,1)}, u32[]{:S(2)}, u32[]{:S(2)}) collective-permute-start(bf16[1,8,6,32,128]{4,3,2,1,0:T(8,128)(2,1)S(1)} %get-tuple-element.23), channel_id=1, source_target_pairs={{0,8},{1,9},{2,10},{3,11},{4,12},{5,13},{6,14},{7,15},{8,0},{9,1},... | collective-permute-start | bytes 1179656 | tf_op jit(solution)/shard_map/ppermute | solution.py:491
  197.9 1.7 copy-start
  199.7 113.2 %all-to-all-start.1 = ((bf16[16,1088,128]{2,1,0:T(8,128)(2,1)}), bf16[16,1088,128]{2,1,0:T(8,128)(2,1)}, u32[]{:S(2)}, u32[]{:S(2)}) async-start(bf16[16,1088,128]{2,1,0:T(8,128)(2,1)} %bitcast.91), calls=%async_computation.1 | async-start | bytes 8912896 | tf_op jit(solution)/shard_map/all_to_all | solution.py:485
  222.5 1.8 collective-permute-start.9
  224.3 16.8 %collective-permute-start.10 = (bf16[4,2,6,32,128]{4,3,2,0,1:T(8,128)(2,1)S(1)}, bf16[4,2,6,32,128]{4,3,2,0,1:T(8,128)(2,1)S(1)}, u32[]{:S(2)}, u32[]{:S(2)}) collective-permute-start(bf16[4,2,6,32,128]{4,3,2,0,1:T(8,128)(2,1)S(1)} %get-tuple-element.20), channel_id=1, source_target_pairs={{0,2},{1,3},{2,0},{3,1},{4,6},{5,7},{6,4},{7,5},{8,10},{9,11},{10,... | collective-permute-start | bytes 1179656 | tf_op jit(solution)/shard_map/ppermute | solution.py:491
  241.3 47.1 %collective-permute-start.11 = (bf16[2,4,6,32,128]{4,3,2,1,0:T(8,128)(2,1)S(1)}, bf16[2,4,6,32,128]{4,3,2,1,0:T(8,128)(2,1)S(1)}, u32[]{:S(2)}, u32[]{:S(2)}) collective-permute-start(bf16[2,4,6,32,128]{4,3,2,1,0:T(8,128)(2,1)S(1)} %slice_bitcast_fusion.3), channel_id=1, source_target_pairs={{0,4},{1,5},{2,6},{3,7},{4,0},{5,1},{6,2},{7,3},{8,12},{9,13},{10,... | collective-permute-start | bytes 1179656 | tf_op jit(solution)/shard_map/ppermute | solution.py:491
  288.6 32.4 %collective-permute-start.12 = (bf16[1,8,6,32,128]{4,3,2,1,0:T(8,128)(2,1)S(1)}, bf16[1,8,6,32,128]{4,3,2,1,0:T(8,128)(2,1)S(1)}, u32[]{:S(2)}, u32[]{:S(2)}) collective-permute-start(bf16[1,8,6,32,128]{4,3,2,1,0:T(8,128)(2,1)S(1)} %get-tuple-element.18), channel_id=1, source_target_pairs={{0,8},{1,9},{2,10},{3,11},{4,12},{5,13},{6,14},{7,15},{8,0},{9,1},... | collective-permute-start | bytes 1179656 | tf_op jit(solution)/shard_map/ppermute | solution.py:491
  312.9 86.7 %all-to-all-start.3 = ((bf16[16,896,128]{2,1,0:T(8,128)(2,1)}), bf16[16,896,128]{2,1,0:T(8,128)(2,1)}, u32[]{:S(2)}, u32[]{:S(2)}) async-start(bf16[16,896,128]{2,1,0:T(8,128)(2,1)} %bitcast.93), calls=%async_computation.3 | async-start | bytes 7340032 | tf_op jit(solution)/shard_map/all_to_all | solution.py:485

commit v9 on v8

--- a/solution.py
+++ b/solution.py
@@ -11,7 +11,7 @@
 
 OWNERS = ("lat", "lev", "sub")
 CHUNKS = 2
-HINT = 33
+HINT, ANALYSIS_HINT = 33, 30
 HEAD, EARLY, LATE, LAST = 6, 4, 6, 6
 
 
@@ -159,7 +159,7 @@
         for level in range(levels):
             s = state[n, level].astype(jnp.float32)
             f = forcing[n, level].astype(jnp.float32)
-            explicit = 0.7 * s + 0.5 * f + 0.3 * s / (1.0 + s * s)
+            explicit = s * (0.7 + 0.3 / (1.0 + s * s)) + 0.5 * f
             low, high = explicit[:, :half], explicit[:, half:]
             span = slice(level * lats, (level + 1) * lats)
             folded[now, 0, span, :] = (low + high).astype(jnp.bfloat16)
@@ -227,7 +227,7 @@
         ],
         compiler_params=pltpu.CompilerParams(vmem_limit_bytes=VMEM_BYTES),
         cost_estimate=pl.CostEstimate(
-            flops=30 * 2 * levels * lats * lon_count * slots // chunks,
+            flops=ANALYSIS_HINT * 2 * levels * lats * lon_count * slots // chunks,
             bytes_accessed=6 * levels * lats * lon_count,
             transcendentals=0,
         ),
@@ -364,7 +364,7 @@
     upper = lambda i, waves_ref: (pair_slots(first(i), waves_ref, middle)[1], 0, 1)
     whole = lambda shape: pl.BlockSpec(shape, lambda i, waves_ref: (0, 0, 0, 0))
     sizes = [(owners, end - begin, rows, lats) for begin, end, _ in pieces_out]
-    scratch = pltpu.VMEM((bands, depth * (rows + TILE), lats), jnp.float32)
+    scratch = pltpu.VMEM((bands, (depth + 1) * (rows + TILE), lats), jnp.float32)
     return pl.pallas_call(
         functools.partial(column_kernel, owners, bands, k, pieces_in, pieces_out),
         grid_spec=pltpu.PrefetchScalarGridSpec(

time: 410 us -> 409 us (level)
  waiting for transfers between devices: 261 us -> 267 us
  starting transfers between devices: 52.6 us -> 47.1 us
    all_to_all x4, waiting for transfers between devices: 107 us -> 114 us  [exchange(): return lax.all_to_all(flat, OWNERS, 0, 0, tiled=True).reshape(part.shape)]
    ppermute x13, starting transfers between devices: 30.4 us -> 24.6 us  [give(): lax.ppermute(halves[:, 1], OWNERS, [(o, o ^ bit) for o in range(owners)])]
where the time goes in v9:
time: 409 us; the launch traced here: 408 us
  waiting for transfers between devices  267 us (65%)
  Pallas kernels  79.9 us (20%)
  starting transfers between devices  47.1 us (12%)
  local copies, waits for them, and re-layouts  11.9 us (3%)
    ppermute x13, waiting for transfers between devices, give(): lax.ppermute(halves[:, 1], OWNERS, [(o, o ^ bit) for o in range(owners)])  153 us
    all_to_all x4, waiting for transfers between devices, exchange(): return lax.all_to_all(flat, OWNERS, 0, 0, tiled=True).reshape(part.shape)  114 us
    pallas_call x4, Pallas kernels, run_analysis(): pl.pallas_call(functools.partial(analysis_kernel, owners, chunks, k, begi...  32.6 us
    pallas_call x2, Pallas kernels, run_columns(): pl.pallas_call(functools.partial(column_kernel, owners, bands, k, pieces_...  30.8 us
    ppermute x13, starting transfers between devices, give(): lax.ppermute(halves[:, 1], OWNERS, [(o, o ^ bit) for o in range(owners)])  24.6 us
    all_to_all x4, starting transfers between devices, exchange(): return lax.all_to_all(flat, OWNERS, 0, 0, tiled=True).reshape(part.shape)  22.4 us
    pallas_call x2, Pallas kernels, run_synthesis(): pl.pallas_call(functools.partial(synthesis_kernel, owners, begin, pieces)...  13.3 us
  transfers between devices with their start and end apart: 17, of which 13 were waited for; matrix products, arithmetic and copies ran while one was open for 2% of the time, Pallas kernels for 16%

profile of v9, /device:TPU:11, one launch (start us, length us, event | category | flops | bytes accessed | tf_op | source)
XLA Modules:
  0.0 408.2 jit_solution(6788011210954314307)
XLA Ops:
  0.0 5.2 %longitude_analysis.4.refs_0_ = bf16[16,6,32,128]{3,2,1,0:T(8,128)(2,1)} custom-call(s32[1,512]{1,0:T(1,128)} %bitcast.121, bf16[2,2,256,512]{3,2,1,0:T(8,128)(2,1)} %constant.23.clone.waves_hbm.waves_ref, bf16[34,128,1024]{2,1,0:T(8,128)(2,1)} %state_hbm.7, bf16[34,128,1024]{2,1,0:T(8,128)(2,1)} %forcing_hbm.7), custom_call_target="tpu_custom_call" | custom-call | flops 12079595520 | bytes 4718592 | tf_op jit(solution)/shard_map/longitude_analysis/pallas_call | solution.py:212
  5.2 1.2 fusion.13
  6.3 2.4 collective-permute-start
  8.7 11.2 %longitude_analysis.5 = bf16[16,28,32,128]{3,2,1,0:T(8,128)(2,1)} custom-call(s32[1,512]{1,0:T(1,128)} %bitcast.122, bf16[2,2,256,512]{3,2,1,0:T(8,128)(2,1)} %constant.23.clone.waves_hbm.waves_ref, bf16[34,128,1024]{2,1,0:T(8,128)(2,1)} %state_hbm.7, bf16[34,128,1024]{2,1,0:T(8,128)(2,1)} %forcing_hbm.7, bf16[16,6,32,128]{3,2,1,0:T(8,128)(2,1)} %longitude_analysis.4.refs_0_), custom_call_target="tpu_custom_call" | custom-call | flops 56371445760 | bytes 22020096 | tf_op jit(solution)/shard_map/longitude_analysis/pallas_call | solution.py:212
  19.9 5.3 %all-to-all-start = ((bf16[16,896,128]{2,1,0:T(8,128)(2,1)}), bf16[16,896,128]{2,1,0:T(8,128)(2,1)}, u32[]{:S(2)}, u32[]{:S(2)}) async-start(bf16[16,896,128]{2,1,0:T(8,128)(2,1)} %bitcast.92), calls=%async_computation | async-start | bytes 7340032 | tf_op jit(solution)/shard_map/all_to_all | solution.py:485
  25.2 10.1 %longitude_analysis.6.refs_0_ = bf16[16,24,32,128]{3,2,1,0:T(8,128)(2,1)} custom-call(s32[1,512]{1,0:T(1,128)} %bitcast.123, bf16[2,2,256,512]{3,2,1,0:T(8,128)(2,1)} %constant.23.clone.waves_hbm.waves_ref, bf16[34,128,1024]{2,1,0:T(8,128)(2,1)} %state_hbm.7, bf16[34,128,1024]{2,1,0:T(8,128)(2,1)} %forcing_hbm.7), custom_call_target="tpu_custom_call" | custom-call | flops 48318382080 | bytes 18874368 | tf_op jit(solution)/shard_map/longitude_analysis/pallas_call | solution.py:212
  35.2 6.3 %longitude_analysis.7 = bf16[16,10,32,128]{3,2,1,0:T(8,128)(2,1)} custom-call(s32[1,512]{1,0:T(1,128)} %bitcast.124, bf16[2,2,256,512]{3,2,1,0:T(8,128)(2,1)} %constant.23.clone.waves_hbm.waves_ref, bf16[34,128,1024]{2,1,0:T(8,128)(2,1)} %state_hbm.7, bf16[34,128,1024]{2,1,0:T(8,128)(2,1)} %forcing_hbm.7, bf16[16,24,32,128]{3,2,1,0:T(8,128)(2,1)} %longitude_analysis.6.refs_0_), custom_call_target="tpu_custom_call" | custom-call | flops 20132659200 | bytes 7864320 | tf_op jit(solution)/shard_map/longitude_analysis/pallas_call | solution.py:212
  41.6 0.9 slice-done
  42.7 0.4 collective-permute-start.1
  43.1 1.7 collective-permute-done.1
  45.0 0.3 collective-permute-start.2
  45.3 24.7 %collective-permute-done.2 = bf16[4,2,10,32,128]{4,3,2,0,1:T(8,128)(2,1)S(1)} collective-permute-done((bf16[4,2,10,32,128]{4,3,2,0,1:T(8,128)(2,1)S(1)}, bf16[4,2,10,32,128]{4,3,2,0,1:T(8,128)(2,1)S(1)}, u32[]{:S(2)}, u32[]{:S(2)}) %collective-permute-start.2) | collective-permute-done | bytes 655392 | tf_op jit(solution)/shard_map/ppermute | solution.py:491
  70.4 3.1 collective-permute-start.3
  73.5 27.2 %collective-permute-done.3 = bf16[2,4,10,32,128]{4,3,2,1,0:T(8,128)(2,1)S(1)} collective-permute-done((bf16[2,4,10,32,128]{4,3,2,1,0:T(8,128)(2,1)S(1)}, bf16[2,4,10,32,128]{4,3,2,1,0:T(8,128)(2,1)S(1)}, u32[]{:S(2)}, u32[]{:S(2)}) %collective-permute-start.3) | collective-permute-done | bytes 655392 | tf_op jit(solution)/shard_map/ppermute | solution.py:491
  101.2 0.8 slice_bitcast_fusion.10
  102.0 7.4 %collective-permute-start.4 = (bf16[1,8,4,32,128]{4,3,2,1,0:T(8,128)(2,1)S(1)}, bf16[1,8,4,32,128]{4,3,2,1,0:T(8,128)(2,1)}, u32[]{:S(2)}, u32[]{:S(2)}) collective-permute-start(bf16[1,8,4,32,128]{4,3,2,1,0:T(8,128)(2,1)S(1)} %get-tuple-element.32), channel_id=1, source_target_pairs={{0,8},{1,9},{2,10},{3,11},{4,12},{5,13},{6,14},{7,15},{8,0},{9,1},... | collective-permute-start | bytes 786440 | tf_op jit(solution)/shard_map/ppermute | solution.py:491
  109.4 0.9 slice.132
  110.3 1.3 dynamic_slice.3.waves_ref
  111.6 1.0 slice.129.refs_1_
  112.6 5.7 %all-to-all-start.2 = ((bf16[16,768,128]{2,1,0:T(8,128)(2,1)}), bf16[16,768,128]{2,1,0:T(8,128)(2,1)S(1)}, u32[]{:S(2)}, u32[]{:S(2)}) async-start(bf16[16,768,128]{2,1,0:T(8,128)(2,1)} %bitcast.94), calls=%async_computation.2 | async-start | bytes 6291456 | tf_op jit(solution)/shard_map/all_to_all | solution.py:485
  118.3 1.7 collective-permute-done.4
  120.0 15.4 %legendre_solve.2 = bf16[16,34,32,128]{3,2,1,0:T(8,128)(2,1)} custom-call(s32[32]{0:T(128)} %dynamic_slice.3.waves_ref, bf16[16,28,32,128]{3,2,1,0:T(8,128)(2,1)} %bitcast.2.refs_0_, bf16[16,6,32,128]{3,2,1,0:T(8,128)(2,1)} %slice.129.refs_1_, bf16[32,512,512]{2,1,0:T(8,128)(2,1)} %refs_6_.1, bf16[32,512,512]{2,1,0:T(8,128)(2,1)} %refs_6_.1, ...), custom_call_target="tpu_custom_call" | custom-call | flops 112944218112 | bytes 15204352 | tf_op jit(solution)/shard_map/legendre_solve/pallas_call | solution.py:368
  135.4 1.2 fusion.12
  136.6 0.6 collective-permute-start.5
  137.2 1.3 collective-permute-done.5
  138.6 0.7 collective-permute-start.6
  139.3 18.0 %collective-permute-done.6 = bf16[4,2,6,32,128]{4,3,2,0,1:T(8,128)(2,1)S(1)} collective-permute-done((bf16[4,2,6,32,128]{4,3,2,0,1:T(8,128)(2,1)S(1)}, bf16[4,2,6,32,128]{4,3,2,0,1:T(8,128)(2,1)S(1)}, u32[]{:S(2)}, u32[]{:S(2)}) %collective-permute-start.6) | collective-permute-done | bytes 393248 | tf_op jit(solution)/shard_map/ppermute | solution.py:491
  157.4 1.5 collective-permute-start.7
  158.9 20.9 %collective-permute-done.7 = bf16[2,4,6,32,128]{4,3,2,1,0:T(8,128)(2,1)S(1)} collective-permute-done((bf16[2,4,6,32,128]{4,3,2,1,0:T(8,128)(2,1)S(1)}, bf16[2,4,6,32,128]{4,3,2,1,0:T(8,128)(2,1)S(1)}, u32[]{:S(2)}, u32[]{:S(2)}) %collective-permute-start.7) | collective-permute-done | bytes 393248 | tf_op jit(solution)/shard_map/ppermute | solution.py:491
  179.9 0.8 slice_bitcast_fusion.5
  180.9 16.2 %all-to-all-done.2 = bf16[16,768,128]{2,1,0:T(8,128)(2,1)S(1)} async-done(((bf16[16,768,128]{2,1,0:T(8,128)(2,1)}), bf16[16,768,128]{2,1,0:T(8,128)(2,1)S(1)}, u32[]{:S(2)}, u32[]{:S(2)}) %all-to-all-start.2) | async-done | bytes 3145760 | tf_op jit(solution)/shard_map/all_to_all | solution.py:485
  197.1 1.7 copy-done
  198.9 6.6 %all-to-all-start.1 = ((bf16[16,1088,128]{2,1,0:T(8,128)(2,1)}), bf16[16,1088,128]{2,1,0:T(8,128)(2,1)}, u32[]{:S(2)}, u32[]{:S(2)}) async-start(bf16[16,1088,128]{2,1,0:T(8,128)(2,1)} %bitcast.91), calls=%async_computation.1 | async-start | bytes 8912896 | tf_op jit(solution)/shard_map/all_to_all | solution.py:485
  205.5 15.4 %legendre_solve.3 = (bf16[16,28,32,128]{3,2,1,0:T(8,128)(2,1)}, bf16[16,6,32,128]{3,2,1,0:T(8,128)(2,1)}) custom-call(s32[32]{0:T(128)} %dynamic_slice.3.waves_ref, bf16[16,24,32,128]{3,2,1,0:T(8,128)(2,1)} %bitcast.95, bf16[8,4,32,128]{3,2,1,0:T(8,128)(2,1)} %get-tuple-element.31.refs_1_, bf16[8,4,32,128]{3,2,1,0:T(8,128)(2,1)} %bitcast.20.refs_6_.refs_2_, ...), custom_call_target="tpu_custom_call" | custom-call | flops 112944218112 | bytes 15204352 | tf_op jit(solution)/shard_map/legendre_solve/pallas_call | solution.py:368
  220.9 1.2 fusion.11
  222.1 0.4 collective-permute-start.9
  222.5 1.4 collective-permute-done.9
  223.9 0.3 collective-permute-start.10
  224.3 16.4 %collective-permute-done.10 = bf16[4,2,6,32,128]{4,3,2,0,1:T(8,128)(2,1)S(1)} collective-permute-done((bf16[4,2,6,32,128]{4,3,2,0,1:T(8,128)(2,1)S(1)}, bf16[4,2,6,32,128]{4,3,2,0,1:T(8,128)(2,1)S(1)}, u32[]{:S(2)}, u32[]{:S(2)}) %collective-permute-start.10) | collective-permute-done | bytes 393248 | tf_op jit(solution)/shard_map/ppermute | solution.py:491
  240.8 7.1 %collective-permute-start.11 = (bf16[2,4,6,32,128]{4,3,2,1,0:T(8,128)(2,1)S(1)}, bf16[2,4,6,32,128]{4,3,2,1,0:T(8,128)(2,1)S(1)}, u32[]{:S(2)}, u32[]{:S(2)}) collective-permute-start(bf16[2,4,6,32,128]{4,3,2,1,0:T(8,128)(2,1)S(1)} %slice_bitcast_fusion.3), channel_id=1, source_target_pairs={{0,4},{1,5},{2,6},{3,7},{4,0},{5,1},{6,2},{7,3},{8,12},{9,13},{10,... | collective-permute-start | bytes 1179656 | tf_op jit(solution)/shard_map/ppermute | solution.py:491
  247.9 40.0 %collective-permute-done.11 = bf16[2,4,6,32,128]{4,3,2,1,0:T(8,128)(2,1)S(1)} collective-permute-done((bf16[2,4,6,32,128]{4,3,2,1,0:T(8,128)(2,1)S(1)}, bf16[2,4,6,32,128]{4,3,2,1,0:T(8,128)(2,1)S(1)}, u32[]{:S(2)}, u32[]{:S(2)}) %collective-permute-start.11) | collective-permute-done | bytes 393248 | tf_op jit(solution)/shard_map/ppermute | solution.py:491
  288.4 24.1 %all-to-all-done.1 = bf16[16,1088,128]{2,1,0:T(8,128)(2,1)} async-done(((bf16[16,1088,128]{2,1,0:T(8,128)(2,1)}), bf16[16,1088,128]{2,1,0:T(8,128)(2,1)}, u32[]{:S(2)}, u32[]{:S(2)}) %all-to-all-start.1) | async-done | bytes 4456480 | tf_op jit(solution)/shard_map/all_to_all | solution.py:485
  312.5 4.9 %all-to-all-start.3 = ((bf16[16,896,128]{2,1,0:T(8,128)(2,1)}), bf16[16,896,128]{2,1,0:T(8,128)(2,1)}, u32[]{:S(2)}, u32[]{:S(2)}) async-start(bf16[16,896,128]{2,1,0:T(8,128)(2,1)} %bitcast.93), calls=%async_computation.3 | async-start | bytes 7340032 | tf_op jit(solution)/shard_map/all_to_all | solution.py:485
  317.3 3.2 synthesis_rows.1.refs_2_
  320.6 0.9 pad_maximum_fusion.7.refs_1_
  321.5 4.5 %longitude_synthesis.2.refs_3_ = bf16[34,128,1024]{2,1,0:T(8,128)(2,1)} custom-call(bf16[16,34,32,128]{3,2,1,0:T(8,128)(2,1)} %bitcast.22.refs_0_, bf16[16,6,32,128]{3,2,1,0:T(8,128)(2,1)} %pad_maximum_fusion.7.refs_1_, bf16[2,2,256,512]{3,2,1,0:T(8,128)(2,1)} %synthesis_rows.1.refs_2_), custom_call_target="tpu_custom_call" | custom-call | flops 805306368 | bytes 3145728 | tf_op jit(solution)/shard_map/longitude_synthesis/pallas_call | solution.py:458
  326.0 73.2 %all-to-all-done.3 = bf16[16,896,128]{2,1,0:T(8,128)(2,1)} async-done(((bf16[16,896,128]{2,1,0:T(8,128)(2,1)}), bf16[16,896,128]{2,1,0:T(8,128)(2,1)}, u32[]{:S(2)}, u32[]{:S(2)}) %all-to-all-start.3) | async-done | bytes 3670048 | tf_op jit(solution)/shard_map/all_to_all | solution.py:485
  399.2 8.8 %longitude_synthesis.3 = bf16[34,128,1024]{2,1,0:T(8,128)(2,1)} custom-call(bf16[16,34,32,128]{3,2,1,0:T(8,128)(2,1)} %bitcast.22.refs_0_, bf16[16,28,32,128]{3,2,1,0:T(8,128)(2,1)} %bitcast.41.refs_1_, bf16[2,2,256,512]{3,2,1,0:T(8,128)(2,1)} %synthesis_rows.1.refs_2_, bf16[34,128,1024]{2,1,0:T(8,128)(2,1)} %longitude_synthesis.2.refs_3_), custom_call_target="tpu_custom_call", output_to_operand_aliasing={{}: (3, {})} | custom-call | flops 3758096384 | bytes 14680064 | tf_op jit(solution)/shard_map/longitude_synthesis/pallas_call | solution.py:458
  (32 shorter events, 2.5 us)
Async XLA Ops:
  6.3 35.2 %collective-permute-start = (bf16[1,8,6,32,128]{4,3,2,1,0:T(8,128)(2,1)S(1)}, bf16[1,8,6,32,128]{4,3,2,1,0:T(8,128)(2,1)S(1)}, u32[]{:S(2)}, u32[]{:S(2)}) collective-permute-start(bf16[1,8,6,32,128]{4,3,2,1,0:T(8,128)(2,1)S(1)} %get-tuple-element.30), channel_id=1, source_target_pairs={{0,8},{1,9},{2,10},{3,11},{4,12},{5,13},{6,14},{7,15},{8,0},{9,1},... | collective-permute-start | bytes 1179656 | tf_op jit(solution)/shard_map/ppermute | solution.py:491
  19.9 92.7 %all-to-all-start = ((bf16[16,896,128]{2,1,0:T(8,128)(2,1)}), bf16[16,896,128]{2,1,0:T(8,128)(2,1)}, u32[]{:S(2)}, u32[]{:S(2)}) async-start(bf16[16,896,128]{2,1,0:T(8,128)(2,1)} %bitcast.92), calls=%async_computation | async-start | bytes 7340032 | tf_op jit(solution)/shard_map/all_to_all | solution.py:485
  41.5 1.0 slice-start
  42.7 2.2 collective-permute-start.1
  45.0 25.0 %collective-permute-start.2 = (bf16[4,2,10,32,128]{4,3,2,0,1:T(8,128)(2,1)S(1)}, bf16[4,2,10,32,128]{4,3,2,0,1:T(8,128)(2,1)S(1)}, u32[]{:S(2)}, u32[]{:S(2)}) collective-permute-start(bf16[4,2,10,32,128]{4,3,2,0,1:T(8,128)(2,1)S(1)} %get-tuple-element.14), channel_id=1, source_target_pairs={{0,2},{1,3},{2,0},{3,1},{4,6},{5,7},{6,4},{7,5},{8,10},{9,11},{10,... | collective-permute-start | bytes 1966088 | tf_op jit(solution)/shard_map/ppermute | solution.py:491
  70.4 30.3 %collective-permute-start.3 = (bf16[2,4,10,32,128]{4,3,2,1,0:T(8,128)(2,1)S(1)}, bf16[2,4,10,32,128]{4,3,2,1,0:T(8,128)(2,1)S(1)}, u32[]{:S(2)}, u32[]{:S(2)}) collective-permute-start(bf16[2,4,10,32,128]{4,3,2,1,0:T(8,128)(2,1)S(1)} %slice_bitcast_fusion), channel_id=1, source_target_pairs={{0,4},{1,5},{2,6},{3,7},{4,0},{5,1},{6,2},{7,3},{8,12},{9,13},{10,... | collective-permute-start | bytes 1966088 | tf_op jit(solution)/shard_map/ppermute | solution.py:491
  101.2 8.2 %copy-start.1 = (bf16[16,10,32,128]{3,2,1,0:T(8,128)(2,1)S(1)}, bf16[16,10,32,128]{3,2,1,0:T(8,128)(2,1)}, u32[]{:S(2)}) copy-start(bf16[16,10,32,128]{3,2,1,0:T(8,128)(2,1)} %longitude_analysis.7) | copy-start | bytes 3932164
  102.0 18.0 %collective-permute-start.4 = (bf16[1,8,4,32,128]{4,3,2,1,0:T(8,128)(2,1)S(1)}, bf16[1,8,4,32,128]{4,3,2,1,0:T(8,128)(2,1)}, u32[]{:S(2)}, u32[]{:S(2)}) collective-permute-start(bf16[1,8,4,32,128]{4,3,2,1,0:T(8,128)(2,1)S(1)} %get-tuple-element.32), channel_id=1, source_target_pairs={{0,8},{1,9},{2,10},{3,11},{4,12},{5,13},{6,14},{7,15},{8,0},{9,1},... | collective-permute-start | bytes 786440 | tf_op jit(solution)/shard_map/ppermute | solution.py:491
  112.6 84.5 %all-to-all-start.2 = ((bf16[16,768,128]{2,1,0:T(8,128)(2,1)}), bf16[16,768,128]{2,1,0:T(8,128)(2,1)S(1)}, u32[]{:S(2)}, u32[]{:S(2)}) async-start(bf16[16,768,128]{2,1,0:T(8,128)(2,1)} %bitcast.94), calls=%async_computation.2 | async-start | bytes 6291456 | tf_op jit(solution)/shard_map/all_to_all | solution.py:485
  136.6 2.0 collective-permute-start.5
  138.6 18.6 %collective-permute-start.6 = (bf16[4,2,6,32,128]{4,3,2,0,1:T(8,128)(2,1)S(1)}, bf16[4,2,6,32,128]{4,3,2,0,1:T(8,128)(2,1)S(1)}, u32[]{:S(2)}, u32[]{:S(2)}) collective-permute-start(bf16[4,2,6,32,128]{4,3,2,0,1:T(8,128)(2,1)S(1)} %get-tuple-element.26), channel_id=1, source_target_pairs={{0,2},{1,3},{2,0},{3,1},{4,6},{5,7},{6,4},{7,5},{8,10},{9,11},{10,... | collective-permute-start | bytes 1179656 | tf_op jit(solution)/shard_map/ppermute | solution.py:491
  157.4 22.4 %collective-permute-start.7 = (bf16[2,4,6,32,128]{4,3,2,1,0:T(8,128)(2,1)S(1)}, bf16[2,4,6,32,128]{4,3,2,1,0:T(8,128)(2,1)S(1)}, u32[]{:S(2)}, u32[]{:S(2)}) collective-permute-start(bf16[2,4,6,32,128]{4,3,2,1,0:T(8,128)(2,1)S(1)} %slice_bitcast_fusion.7), channel_id=1, source_target_pairs={{0,4},{1,5},{2,6},{3,7},{4,0},{5,1},{6,2},{7,3},{8,12},{9,13},{10,... | collective-permute-start | bytes 1179656 | tf_op jit(solution)/shard_map/ppermute | solution.py:491
  180.8 24.7 %collective-permute-start.8 = (bf16[1,8,6,32,128]{4,3,2,1,0:T(8,128)(2,1)S(1)}, bf16[1,8,6,32,128]{4,3,2,1,0:T(8,128)(2,1)}, u32[]{:S(2)}, u32[]{:S(2)}) collective-permute-start(bf16[1,8,6,32,128]{4,3,2,1,0:T(8,128)(2,1)S(1)} %get-tuple-element.23), channel_id=1, source_target_pairs={{0,8},{1,9},{2,10},{3,11},{4,12},{5,13},{6,14},{7,15},{8,0},{9,1},... | collective-permute-start | bytes 1179656 | tf_op jit(solution)/shard_map/ppermute | solution.py:491
  197.1 1.7 copy-start
  198.9 113.6 %all-to-all-start.1 = ((bf16[16,1088,128]{2,1,0:T(8,128)(2,1)}), bf16[16,1088,128]{2,1,0:T(8,128)(2,1)}, u32[]{:S(2)}, u32[]{:S(2)}) async-start(bf16[16,1088,128]{2,1,0:T(8,128)(2,1)} %bitcast.91), calls=%async_computation.1 | async-start | bytes 8912896 | tf_op jit(solution)/shard_map/all_to_all | solution.py:485
  222.1 1.8 collective-permute-start.9
  223.9 16.8 %collective-permute-start.10 = (bf16[4,2,6,32,128]{4,3,2,0,1:T(8,128)(2,1)S(1)}, bf16[4,2,6,32,128]{4,3,2,0,1:T(8,128)(2,1)S(1)}, u32[]{:S(2)}, u32[]{:S(2)}) collective-permute-start(bf16[4,2,6,32,128]{4,3,2,0,1:T(8,128)(2,1)S(1)} %get-tuple-element.20), channel_id=1, source_target_pairs={{0,2},{1,3},{2,0},{3,1},{4,6},{5,7},{6,4},{7,5},{8,10},{9,11},{10,... | collective-permute-start | bytes 1179656 | tf_op jit(solution)/shard_map/ppermute | solution.py:491
  240.8 47.1 %collective-permute-start.11 = (bf16[2,4,6,32,128]{4,3,2,1,0:T(8,128)(2,1)S(1)}, bf16[2,4,6,32,128]{4,3,2,1,0:T(8,128)(2,1)S(1)}, u32[]{:S(2)}, u32[]{:S(2)}) collective-permute-start(bf16[2,4,6,32,128]{4,3,2,1,0:T(8,128)(2,1)S(1)} %slice_bitcast_fusion.3), channel_id=1, source_target_pairs={{0,4},{1,5},{2,6},{3,7},{4,0},{5,1},{6,2},{7,3},{8,12},{9,13},{10,... | collective-permute-start | bytes 1179656 | tf_op jit(solution)/shard_map/ppermute | solution.py:491
  288.2 32.4 %collective-permute-start.12 = (bf16[1,8,6,32,128]{4,3,2,1,0:T(8,128)(2,1)S(1)}, bf16[1,8,6,32,128]{4,3,2,1,0:T(8,128)(2,1)S(1)}, u32[]{:S(2)}, u32[]{:S(2)}) collective-permute-start(bf16[1,8,6,32,128]{4,3,2,1,0:T(8,128)(2,1)S(1)} %get-tuple-element.18), channel_id=1, source_target_pairs={{0,8},{1,9},{2,10},{3,11},{4,12},{5,13},{6,14},{7,15},{8,0},{9,1},... | collective-permute-start | bytes 1179656 | tf_op jit(solution)/shard_map/ppermute | solution.py:491
  312.5 86.7 %all-to-all-start.3 = ((bf16[16,896,128]{2,1,0:T(8,128)(2,1)}), bf16[16,896,128]{2,1,0:T(8,128)(2,1)}, u32[]{:S(2)}, u32[]{:S(2)}) async-start(bf16[16,896,128]{2,1,0:T(8,128)(2,1)} %bitcast.93), calls=%async_computation.3 | async-start | bytes 7340032 | tf_op jit(solution)/shard_map/all_to_all | solution.py:485

commit v10 on v9

--- a/solution.py
+++ b/solution.py
@@ -12,7 +12,7 @@
 OWNERS = ("lat", "lev", "sub")
 CHUNKS = 2
 HINT, ANALYSIS_HINT = 33, 30
-HEAD, EARLY, LATE, LAST = 6, 4, 6, 6
+HEAD, EARLY, LATE, LAST = 6, 2, 6, 6
 
 
 def raw_table(fourier_order_holder, lon_count):

time: 409 us -> 409 us (level)
  transfers between devices with their start and end apart: 17 -> 17, of which waited for: 13 -> 13; matrix products, arithmetic and copies ran while one was open for 2% -> 3% of each run, Pallas kernels for 16% -> 16%
where the time goes in v10:
time: 409 us; the launch traced here: 408 us
  waiting for transfers between devices  269 us (66%)
  Pallas kernels  80.2 us (20%)
  starting transfers between devices  45 us (11%)
  local copies, waits for them, and re-layouts  11.8 us (3%)
    ppermute x13, waiting for transfers between devices, give(): lax.ppermute(halves[:, 1], OWNERS, [(o, o ^ bit) for o in range(owners)])  152 us
    all_to_all x4, waiting for transfers between devices, exchange(): return lax.all_to_all(flat, OWNERS, 0, 0, tiled=True).reshape(part.shape)  117 us
    pallas_call x4, Pallas kernels, run_analysis(): pl.pallas_call(functools.partial(analysis_kernel, owners, chunks, k, begi...  33 us
    pallas_call x2, Pallas kernels, run_columns(): pl.pallas_call(functools.partial(column_kernel, owners, bands, k, pieces_...  30.7 us
    ppermute x13, starting transfers between devices, give(): lax.ppermute(halves[:, 1], OWNERS, [(o, o ^ bit) for o in range(owners)])  25.3 us
    all_to_all x4, starting transfers between devices, exchange(): return lax.all_to_all(flat, OWNERS, 0, 0, tiled=True).reshape(part.shape)  19.8 us
    pallas_call x2, Pallas kernels, run_synthesis(): pl.pallas_call(functools.partial(synthesis_kernel, owners, begin, pieces)...  13.3 us
  transfers between devices with their start and end apart: 17, of which 13 were waited for; matrix products, arithmetic and copies ran while one was open for 3% of the time, Pallas kernels for 16%

profile of v10, /device:TPU:11, one launch (start us, length us, event | category | flops | bytes accessed | tf_op | source)
XLA Modules:
  0.0 408.3 jit_solution(7606308979009784391)
XLA Ops:
  0.0 5.2 %longitude_analysis.4.refs_0_ = bf16[16,6,32,128]{3,2,1,0:T(8,128)(2,1)} custom-call(s32[1,512]{1,0:T(1,128)} %bitcast.121, bf16[2,2,256,512]{3,2,1,0:T(8,128)(2,1)} %constant.23.clone.waves_hbm.waves_ref, bf16[34,128,1024]{2,1,0:T(8,128)(2,1)} %state_hbm.7, bf16[34,128,1024]{2,1,0:T(8,128)(2,1)} %forcing_hbm.7), custom_call_target="tpu_custom_call" | custom-call | flops 12079595520 | bytes 4718592 | tf_op jit(solution)/shard_map/longitude_analysis/pallas_call | solution.py:212
  5.2 1.2 fusion.13
  6.3 2.4 collective-permute-start
  8.7 11.2 %longitude_analysis.5 = bf16[16,28,32,128]{3,2,1,0:T(8,128)(2,1)} custom-call(s32[1,512]{1,0:T(1,128)} %bitcast.122, bf16[2,2,256,512]{3,2,1,0:T(8,128)(2,1)} %constant.23.clone.waves_hbm.waves_ref, bf16[34,128,1024]{2,1,0:T(8,128)(2,1)} %state_hbm.7, bf16[34,128,1024]{2,1,0:T(8,128)(2,1)} %forcing_hbm.7, bf16[16,6,32,128]{3,2,1,0:T(8,128)(2,1)} %longitude_analysis.4.refs_0_), custom_call_target="tpu_custom_call" | custom-call | flops 56371445760 | bytes 22020096 | tf_op jit(solution)/shard_map/longitude_analysis/pallas_call | solution.py:212
  19.9 5.3 %all-to-all-start = ((bf16[16,896,128]{2,1,0:T(8,128)(2,1)}), bf16[16,896,128]{2,1,0:T(8,128)(2,1)}, u32[]{:S(2)}, u32[]{:S(2)}) async-start(bf16[16,896,128]{2,1,0:T(8,128)(2,1)} %bitcast.92), calls=%async_computation | async-start | bytes 7340032 | tf_op jit(solution)/shard_map/all_to_all | solution.py:485
  25.2 10.7 %longitude_analysis.6.refs_0_ = bf16[16,26,32,128]{3,2,1,0:T(8,128)(2,1)} custom-call(s32[1,512]{1,0:T(1,128)} %bitcast.123, bf16[2,2,256,512]{3,2,1,0:T(8,128)(2,1)} %constant.23.clone.waves_hbm.waves_ref, bf16[34,128,1024]{2,1,0:T(8,128)(2,1)} %state_hbm.7, bf16[34,128,1024]{2,1,0:T(8,128)(2,1)} %forcing_hbm.7), custom_call_target="tpu_custom_call" | custom-call | flops 52344913920 | bytes 20447232 | tf_op jit(solution)/shard_map/longitude_analysis/pallas_call | solution.py:212
  35.9 6.0 %longitude_analysis.7 = bf16[16,8,32,128]{3,2,1,0:T(8,128)(2,1)} custom-call(s32[1,512]{1,0:T(1,128)} %bitcast.124, bf16[2,2,256,512]{3,2,1,0:T(8,128)(2,1)} %constant.23.clone.waves_hbm.waves_ref, bf16[34,128,1024]{2,1,0:T(8,128)(2,1)} %state_hbm.7, bf16[34,128,1024]{2,1,0:T(8,128)(2,1)} %forcing_hbm.7, bf16[16,26,32,128]{3,2,1,0:T(8,128)(2,1)} %longitude_analysis.6.refs_0_), custom_call_target="tpu_custom_call" | custom-call | flops 16106127360 | bytes 6291456 | tf_op jit(solution)/shard_map/longitude_analysis/pallas_call | solution.py:212
  41.9 1.0 slice.122
  43.1 0.4 collective-permute-start.1
  43.5 1.5 collective-permute-done.1
  45.2 0.3 collective-permute-start.2
  45.5 16.9 %collective-permute-done.2 = bf16[4,2,8,32,128]{4,3,2,0,1:T(8,128)(2,1)S(1)} collective-permute-done((bf16[4,2,8,32,128]{4,3,2,0,1:T(8,128)(2,1)S(1)}, bf16[4,2,8,32,128]{4,3,2,0,1:T(8,128)(2,1)S(1)}, u32[]{:S(2)}, u32[]{:S(2)}) %collective-permute-start.2) | collective-permute-done | bytes 524320 | tf_op jit(solution)/shard_map/ppermute | solution.py:491
  62.6 5.3 %collective-permute-start.3 = (bf16[2,4,8,32,128]{4,3,2,1,0:T(8,128)(2,1)S(1)}, bf16[2,4,8,32,128]{4,3,2,1,0:T(8,128)(2,1)S(1)}, u32[]{:S(2)}, u32[]{:S(2)}) collective-permute-start(bf16[2,4,8,32,128]{4,3,2,1,0:T(8,128)(2,1)S(1)} %slice_bitcast_fusion), channel_id=1, source_target_pairs={{0,4},{1,5},{2,6},{3,7},{4,0},{5,1},{6,2},{7,3},{8,12},{9,13},{10,... | collective-permute-start | bytes 1572872 | tf_op jit(solution)/shard_map/ppermute | solution.py:491
  68.0 29.9 %collective-permute-done.3 = bf16[2,4,8,32,128]{4,3,2,1,0:T(8,128)(2,1)S(1)} collective-permute-done((bf16[2,4,8,32,128]{4,3,2,1,0:T(8,128)(2,1)S(1)}, bf16[2,4,8,32,128]{4,3,2,1,0:T(8,128)(2,1)S(1)}, u32[]{:S(2)}, u32[]{:S(2)}) %collective-permute-start.3) | collective-permute-done | bytes 524320 | tf_op jit(solution)/shard_map/ppermute | solution.py:491
  98.1 0.7 slice_bitcast_fusion.10
  98.8 5.1 %collective-permute-start.4 = (bf16[1,8,2,32,128]{4,3,2,1,0:T(8,128)(2,1)S(1)}, bf16[1,8,2,32,128]{4,3,2,1,0:T(8,128)(2,1)}, u32[]{:S(2)}, u32[]{:S(2)}) collective-permute-start(bf16[1,8,2,32,128]{4,3,2,1,0:T(8,128)(2,1)S(1)} %get-tuple-element.32), channel_id=1, source_target_pairs={{0,8},{1,9},{2,10},{3,11},{4,12},{5,13},{6,14},{7,15},{8,0},{9,1},... | collective-permute-start | bytes 393224 | tf_op jit(solution)/shard_map/ppermute | solution.py:491
  104.0 1.0 slice.132
  104.9 1.3 dynamic_slice.3.waves_ref
  106.2 1.0 slice.129.refs_1_
  107.3 2.5 all-to-all-done
  109.8 4.8 %all-to-all-start.2 = ((bf16[16,832,128]{2,1,0:T(8,128)(2,1)}), bf16[16,832,128]{2,1,0:T(8,128)(2,1)S(1)}, u32[]{:S(2)}, u32[]{:S(2)}) async-start(bf16[16,832,128]{2,1,0:T(8,128)(2,1)} %bitcast.94), calls=%async_computation.2 | async-start | bytes 6815744 | tf_op jit(solution)/shard_map/all_to_all | solution.py:485
  114.6 15.4 %legendre_solve.2 = bf16[16,34,32,128]{3,2,1,0:T(8,128)(2,1)} custom-call(s32[32]{0:T(128)} %dynamic_slice.3.waves_ref, bf16[16,28,32,128]{3,2,1,0:T(8,128)(2,1)} %bitcast.2.refs_0_, bf16[16,6,32,128]{3,2,1,0:T(8,128)(2,1)} %slice.129.refs_1_, bf16[32,512,512]{2,1,0:T(8,128)(2,1)} %refs_6_.1, bf16[32,512,512]{2,1,0:T(8,128)(2,1)} %refs_6_.1, ...), custom_call_target="tpu_custom_call" | custom-call | flops 112944218112 | bytes 15204352 | tf_op jit(solution)/shard_map/legendre_solve/pallas_call | solution.py:368
  130.0 1.2 fusion.12
  131.1 0.4 collective-permute-start.5
  131.6 1.4 collective-permute-done.5
  133.0 0.3 collective-permute-start.6
  133.3 13.8 %collective-permute-done.6 = bf16[4,2,6,32,128]{4,3,2,0,1:T(8,128)(2,1)S(1)} collective-permute-done((bf16[4,2,6,32,128]{4,3,2,0,1:T(8,128)(2,1)S(1)}, bf16[4,2,6,32,128]{4,3,2,0,1:T(8,128)(2,1)S(1)}, u32[]{:S(2)}, u32[]{:S(2)}) %collective-permute-start.6) | collective-permute-done | bytes 393248 | tf_op jit(solution)/shard_map/ppermute | solution.py:491
  147.3 2.7 collective-permute-start.7
  150.0 30.3 %collective-permute-done.7 = bf16[2,4,6,32,128]{4,3,2,1,0:T(8,128)(2,1)S(1)} collective-permute-done((bf16[2,4,6,32,128]{4,3,2,1,0:T(8,128)(2,1)S(1)}, bf16[2,4,6,32,128]{4,3,2,1,0:T(8,128)(2,1)S(1)}, u32[]{:S(2)}, u32[]{:S(2)}) %collective-permute-start.7) | collective-permute-done | bytes 393248 | tf_op jit(solution)/shard_map/ppermute | solution.py:491
  180.5 1.0 slice_bitcast_fusion.5
  181.5 17.5 %all-to-all-done.2 = bf16[16,832,128]{2,1,0:T(8,128)(2,1)S(1)} async-done(((bf16[16,832,128]{2,1,0:T(8,128)(2,1)}), bf16[16,832,128]{2,1,0:T(8,128)(2,1)S(1)}, u32[]{:S(2)}, u32[]{:S(2)}) %all-to-all-start.2) | async-done | bytes 3407904 | tf_op jit(solution)/shard_map/all_to_all | solution.py:485
  199.0 1.8 copy-done
  200.8 4.8 %all-to-all-start.1 = ((bf16[16,1088,128]{2,1,0:T(8,128)(2,1)}), bf16[16,1088,128]{2,1,0:T(8,128)(2,1)}, u32[]{:S(2)}, u32[]{:S(2)}) async-start(bf16[16,1088,128]{2,1,0:T(8,128)(2,1)} %bitcast.89), calls=%async_computation.1 | async-start | bytes 8912896 | tf_op jit(solution)/shard_map/all_to_all | solution.py:485
  205.6 15.3 %legendre_solve.3 = (bf16[16,28,32,128]{3,2,1,0:T(8,128)(2,1)}, bf16[16,6,32,128]{3,2,1,0:T(8,128)(2,1)}) custom-call(s32[32]{0:T(128)} %dynamic_slice.3.waves_ref, bf16[16,26,32,128]{3,2,1,0:T(8,128)(2,1)} %bitcast.95, bf16[8,2,32,128]{3,2,1,0:T(8,128)(2,1)} %get-tuple-element.31.refs_1_, bf16[8,2,32,128]{3,2,1,0:T(8,128)(2,1)} %bitcast.20.refs_6_.refs_2_, ...), custom_call_target="tpu_custom_call" | custom-call | flops 112944218112 | bytes 15204352 | tf_op jit(solution)/shard_map/legendre_solve/pallas_call | solution.py:368
  221.0 1.2 fusion.11
  222.1 0.4 collective-permute-start.9
  222.6 1.4 collective-permute-done.9
  224.0 0.3 collective-permute-start.10
  224.3 16.4 %collective-permute-done.10 = bf16[4,2,6,32,128]{4,3,2,0,1:T(8,128)(2,1)S(1)} collective-permute-done((bf16[4,2,6,32,128]{4,3,2,0,1:T(8,128)(2,1)S(1)}, bf16[4,2,6,32,128]{4,3,2,0,1:T(8,128)(2,1)S(1)}, u32[]{:S(2)}, u32[]{:S(2)}) %collective-permute-start.10) | collective-permute-done | bytes 393248 | tf_op jit(solution)/shard_map/ppermute | solution.py:491
  241.0 7.1 %collective-permute-start.11 = (bf16[2,4,6,32,128]{4,3,2,1,0:T(8,128)(2,1)S(1)}, bf16[2,4,6,32,128]{4,3,2,1,0:T(8,128)(2,1)S(1)}, u32[]{:S(2)}, u32[]{:S(2)}) collective-permute-start(bf16[2,4,6,32,128]{4,3,2,1,0:T(8,128)(2,1)S(1)} %slice_bitcast_fusion.3), channel_id=1, source_target_pairs={{0,4},{1,5},{2,6},{3,7},{4,0},{5,1},{6,2},{7,3},{8,12},{9,13},{10,... | collective-permute-start | bytes 1179656 | tf_op jit(solution)/shard_map/ppermute | solution.py:491
  248.0 40.0 %collective-permute-done.11 = bf16[2,4,6,32,128]{4,3,2,1,0:T(8,128)(2,1)S(1)} collective-permute-done((bf16[2,4,6,32,128]{4,3,2,1,0:T(8,128)(2,1)S(1)}, bf16[2,4,6,32,128]{4,3,2,1,0:T(8,128)(2,1)S(1)}, u32[]{:S(2)}, u32[]{:S(2)}) %collective-permute-start.11) | collective-permute-done | bytes 393248 | tf_op jit(solution)/shard_map/ppermute | solution.py:491
  288.6 24.1 %all-to-all-done.1 = bf16[16,1088,128]{2,1,0:T(8,128)(2,1)} async-done(((bf16[16,1088,128]{2,1,0:T(8,128)(2,1)}), bf16[16,1088,128]{2,1,0:T(8,128)(2,1)}, u32[]{:S(2)}, u32[]{:S(2)}) %all-to-all-start.1) | async-done | bytes 4456480 | tf_op jit(solution)/shard_map/all_to_all | solution.py:485
  312.6 4.9 %all-to-all-start.3 = ((bf16[16,896,128]{2,1,0:T(8,128)(2,1)}), bf16[16,896,128]{2,1,0:T(8,128)(2,1)}, u32[]{:S(2)}, u32[]{:S(2)}) async-start(bf16[16,896,128]{2,1,0:T(8,128)(2,1)} %bitcast.93), calls=%async_computation.3 | async-start | bytes 7340032 | tf_op jit(solution)/shard_map/all_to_all | solution.py:485
  317.5 3.2 synthesis_rows.1.refs_2_
  320.7 1.0 pad_maximum_fusion.7.refs_1_
  321.7 4.5 %longitude_synthesis.2.refs_3_ = bf16[34,128,1024]{2,1,0:T(8,128)(2,1)} custom-call(bf16[16,34,32,128]{3,2,1,0:T(8,128)(2,1)} %bitcast.22.refs_0_, bf16[16,6,32,128]{3,2,1,0:T(8,128)(2,1)} %pad_maximum_fusion.7.refs_1_, bf16[2,2,256,512]{3,2,1,0:T(8,128)(2,1)} %synthesis_rows.1.refs_2_), custom_call_target="tpu_custom_call" | custom-call | flops 805306368 | bytes 3145728 | tf_op jit(solution)/shard_map/longitude_synthesis/pallas_call | solution.py:458
  326.2 73.2 %all-to-all-done.3 = bf16[16,896,128]{2,1,0:T(8,128)(2,1)} async-done(((bf16[16,896,128]{2,1,0:T(8,128)(2,1)}), bf16[16,896,128]{2,1,0:T(8,128)(2,1)}, u32[]{:S(2)}, u32[]{:S(2)}) %all-to-all-start.3) | async-done | bytes 3670048 | tf_op jit(solution)/shard_map/all_to_all | solution.py:485
  399.4 8.8 %longitude_synthesis.3 = bf16[34,128,1024]{2,1,0:T(8,128)(2,1)} custom-call(bf16[16,34,32,128]{3,2,1,0:T(8,128)(2,1)} %bitcast.22.refs_0_, bf16[16,28,32,128]{3,2,1,0:T(8,128)(2,1)} %bitcast.41.refs_1_, bf16[2,2,256,512]{3,2,1,0:T(8,128)(2,1)} %synthesis_rows.1.refs_2_, bf16[34,128,1024]{2,1,0:T(8,128)(2,1)} %longitude_synthesis.2.refs_3_), custom_call_target="tpu_custom_call", output_to_operand_aliasing={{}: (3, {})} | custom-call | flops 3758096384 | bytes 14680064 | tf_op jit(solution)/shard_map/longitude_synthesis/pallas_call | solution.py:458
  (31 shorter events, 1.8 us)
Async XLA Ops:
  6.3 36.6 %collective-permute-start = (bf16[1,8,6,32,128]{4,3,2,1,0:T(8,128)(2,1)S(1)}, bf16[1,8,6,32,128]{4,3,2,1,0:T(8,128)(2,1)S(1)}, u32[]{:S(2)}, u32[]{:S(2)}) collective-permute-start(bf16[1,8,6,32,128]{4,3,2,1,0:T(8,128)(2,1)S(1)} %get-tuple-element.30), channel_id=1, source_target_pairs={{0,8},{1,9},{2,10},{3,11},{4,12},{5,13},{6,14},{7,15},{8,0},{9,1},... | collective-permute-start | bytes 1179656 | tf_op jit(solution)/shard_map/ppermute | solution.py:491
  19.9 89.9 %all-to-all-start = ((bf16[16,896,128]{2,1,0:T(8,128)(2,1)}), bf16[16,896,128]{2,1,0:T(8,128)(2,1)}, u32[]{:S(2)}, u32[]{:S(2)}) async-start(bf16[16,896,128]{2,1,0:T(8,128)(2,1)} %bitcast.92), calls=%async_computation | async-start | bytes 7340032 | tf_op jit(solution)/shard_map/all_to_all | solution.py:485
  43.1 2.0 collective-permute-start.1
  45.2 17.2 %collective-permute-start.2 = (bf16[4,2,8,32,128]{4,3,2,0,1:T(8,128)(2,1)S(1)}, bf16[4,2,8,32,128]{4,3,2,0,1:T(8,128)(2,1)S(1)}, u32[]{:S(2)}, u32[]{:S(2)}) collective-permute-start(bf16[4,2,8,32,128]{4,3,2,0,1:T(8,128)(2,1)S(1)} %get-tuple-element.14), channel_id=1, source_target_pairs={{0,2},{1,3},{2,0},{3,1},{4,6},{5,7},{6,4},{7,5},{8,10},{9,11},{10,... | collective-permute-start | bytes 1572872 | tf_op jit(solution)/shard_map/ppermute | solution.py:491
  62.6 41.4 %copy-start.1 = (bf16[16,8,32,128]{3,2,1,0:T(8,128)(2,1)S(1)}, bf16[16,8,32,128]{3,2,1,0:T(8,128)(2,1)}, u32[]{:S(2)}) copy-start(bf16[16,8,32,128]{3,2,1,0:T(8,128)(2,1)} %longitude_analysis.7) | copy-start | bytes 3145732
  62.6 35.3 %collective-permute-start.3 = (bf16[2,4,8,32,128]{4,3,2,1,0:T(8,128)(2,1)S(1)}, bf16[2,4,8,32,128]{4,3,2,1,0:T(8,128)(2,1)S(1)}, u32[]{:S(2)}, u32[]{:S(2)}) collective-permute-start(bf16[2,4,8,32,128]{4,3,2,1,0:T(8,128)(2,1)S(1)} %slice_bitcast_fusion), channel_id=1, source_target_pairs={{0,4},{1,5},{2,6},{3,7},{4,0},{5,1},{6,2},{7,3},{8,12},{9,13},{10,... | collective-permute-start | bytes 1572872 | tf_op jit(solution)/shard_map/ppermute | solution.py:491
  98.8 15.8 %collective-permute-start.4 = (bf16[1,8,2,32,128]{4,3,2,1,0:T(8,128)(2,1)S(1)}, bf16[1,8,2,32,128]{4,3,2,1,0:T(8,128)(2,1)}, u32[]{:S(2)}, u32[]{:S(2)}) collective-permute-start(bf16[1,8,2,32,128]{4,3,2,1,0:T(8,128)(2,1)S(1)} %get-tuple-element.32), channel_id=1, source_target_pairs={{0,8},{1,9},{2,10},{3,11},{4,12},{5,13},{6,14},{7,15},{8,0},{9,1},... | collective-permute-start | bytes 393224 | tf_op jit(solution)/shard_map/ppermute | solution.py:491
  109.8 89.2 %all-to-all-start.2 = ((bf16[16,832,128]{2,1,0:T(8,128)(2,1)}), bf16[16,832,128]{2,1,0:T(8,128)(2,1)S(1)}, u32[]{:S(2)}, u32[]{:S(2)}) async-start(bf16[16,832,128]{2,1,0:T(8,128)(2,1)} %bitcast.94), calls=%async_computation.2 | async-start | bytes 6815744 | tf_op jit(solution)/shard_map/all_to_all | solution.py:485
  131.1 1.8 collective-permute-start.5
  133.0 14.1 %collective-permute-start.6 = (bf16[4,2,6,32,128]{4,3,2,0,1:T(8,128)(2,1)S(1)}, bf16[4,2,6,32,128]{4,3,2,0,1:T(8,128)(2,1)S(1)}, u32[]{:S(2)}, u32[]{:S(2)}) collective-permute-start(bf16[4,2,6,32,128]{4,3,2,0,1:T(8,128)(2,1)S(1)} %get-tuple-element.26), channel_id=1, source_target_pairs={{0,2},{1,3},{2,0},{3,1},{4,6},{5,7},{6,4},{7,5},{8,10},{9,11},{10,... | collective-permute-start | bytes 1179656 | tf_op jit(solution)/shard_map/ppermute | solution.py:491
  147.3 33.0 %collective-permute-start.7 = (bf16[2,4,6,32,128]{4,3,2,1,0:T(8,128)(2,1)S(1)}, bf16[2,4,6,32,128]{4,3,2,1,0:T(8,128)(2,1)S(1)}, u32[]{:S(2)}, u32[]{:S(2)}) collective-permute-start(bf16[2,4,6,32,128]{4,3,2,1,0:T(8,128)(2,1)S(1)} %slice_bitcast_fusion.7), channel_id=1, source_target_pairs={{0,4},{1,5},{2,6},{3,7},{4,0},{5,1},{6,2},{7,3},{8,12},{9,13},{10,... | collective-permute-start | bytes 1179656 | tf_op jit(solution)/shard_map/ppermute | solution.py:491
  181.4 24.2 %collective-permute-start.8 = (bf16[1,8,6,32,128]{4,3,2,1,0:T(8,128)(2,1)}, bf16[1,8,6,32,128]{4,3,2,1,0:T(8,128)(2,1)}, u32[]{:S(2)}, u32[]{:S(2)}) collective-permute-start(bf16[1,8,6,32,128]{4,3,2,1,0:T(8,128)(2,1)} %get-tuple-element.23), channel_id=1, source_target_pairs={{0,8},{1,9},{2,10},{3,11},{4,12},{5,13},{6,14},{7,15},{8,0},{9,1},... | collective-permute-start | bytes 1179656 | tf_op jit(solution)/shard_map/ppermute | solution.py:491
  199.0 1.8 copy-start
  200.8 111.8 %all-to-all-start.1 = ((bf16[16,1088,128]{2,1,0:T(8,128)(2,1)}), bf16[16,1088,128]{2,1,0:T(8,128)(2,1)}, u32[]{:S(2)}, u32[]{:S(2)}) async-start(bf16[16,1088,128]{2,1,0:T(8,128)(2,1)} %bitcast.89), calls=%async_computation.1 | async-start | bytes 8912896 | tf_op jit(solution)/shard_map/all_to_all | solution.py:485
  222.1 1.8 collective-permute-start.9
  224.0 16.8 %collective-permute-start.10 = (bf16[4,2,6,32,128]{4,3,2,0,1:T(8,128)(2,1)S(1)}, bf16[4,2,6,32,128]{4,3,2,0,1:T(8,128)(2,1)S(1)}, u32[]{:S(2)}, u32[]{:S(2)}) collective-permute-start(bf16[4,2,6,32,128]{4,3,2,0,1:T(8,128)(2,1)S(1)} %get-tuple-element.20), channel_id=1, source_target_pairs={{0,2},{1,3},{2,0},{3,1},{4,6},{5,7},{6,4},{7,5},{8,10},{9,11},{10,... | collective-permute-start | bytes 1179656 | tf_op jit(solution)/shard_map/ppermute | solution.py:491
  241.0 47.1 %collective-permute-start.11 = (bf16[2,4,6,32,128]{4,3,2,1,0:T(8,128)(2,1)S(1)}, bf16[2,4,6,32,128]{4,3,2,1,0:T(8,128)(2,1)S(1)}, u32[]{:S(2)}, u32[]{:S(2)}) collective-permute-start(bf16[2,4,6,32,128]{4,3,2,1,0:T(8,128)(2,1)S(1)} %slice_bitcast_fusion.3), channel_id=1, source_target_pairs={{0,4},{1,5},{2,6},{3,7},{4,0},{5,1},{6,2},{7,3},{8,12},{9,13},{10,... | collective-permute-start | bytes 1179656 | tf_op jit(solution)/shard_map/ppermute | solution.py:491
  288.3 32.4 %collective-permute-start.12 = (bf16[1,8,6,32,128]{4,3,2,1,0:T(8,128)(2,1)S(1)}, bf16[1,8,6,32,128]{4,3,2,1,0:T(8,128)(2,1)S(1)}, u32[]{:S(2)}, u32[]{:S(2)}) collective-permute-start(bf16[1,8,6,32,128]{4,3,2,1,0:T(8,128)(2,1)S(1)} %get-tuple-element.18), channel_id=1, source_target_pairs={{0,8},{1,9},{2,10},{3,11},{4,12},{5,13},{6,14},{7,15},{8,0},{9,1},... | collective-permute-start | bytes 1179656 | tf_op jit(solution)/shard_map/ppermute | solution.py:491
  312.6 86.7 %all-to-all-start.3 = ((bf16[16,896,128]{2,1,0:T(8,128)(2,1)}), bf16[16,896,128]{2,1,0:T(8,128)(2,1)}, u32[]{:S(2)}, u32[]{:S(2)}) async-start(bf16[16,896,128]{2,1,0:T(8,128)(2,1)} %bitcast.93), calls=%async_computation.3 | async-start | bytes 7340032 | tf_op jit(solution)/shard_map/all_to_all | solution.py:485
